TPU v7x, 32 devices: a whole 2x2x4 slice. The times are simulated.
32 devices in a mesh: gx: 4 (over z), gy: 8 (over y, x, core).
Axes of the slice: x: 2, y: 2, z: 4, core: 2. Of those that a mesh axis runs over, the one named last changes fastest.
Arguments:
- velocity: float32 [3, 4, 128, 1024], P(None, 'gx', 'gy'), may hold values from -6 to 6
- y_metric: float32 [128], P('gy'), may hold values from 0.5 to 4
- forward_rate: float32 [3, 128], P(None, 'gy'), may hold values from 0.96875 to 1
- backward_rate: float32 [3, 128], P(None, 'gy'), may hold values from 0.96875 to 1
- pivot_inv: float32 [3, 128], P(None, 'gy'), may hold values from 0 to 0.01171875
- particle_vel: float32 [3, 114688], P(None, ('gx', 'gy')), may hold values from -6 to 6
- particle_cell: int32 [114688], P(('gx', 'gy')), may hold values from 0 to 16383
- particle_offset: float32 [3, 114688], P(None, ('gx', 'gy')), may hold values from 0 to 1
- inverse_tau: float32 [114688], P(('gx', 'gy')), may hold values from 0.5 to 8
- outgoing_count: int32 [4, 8, 3], P('gx', 'gy'), may hold values from 0 to 512, as said below
Outputs:
- velocity_out: float32 [3, 4, 128, 1024], P(None, 'gx', 'gy')
- particle_out: float32 [3, 114688], P(None, ('gx', 'gy'))
Inputs may be any that keep to these rules, and one draw needn't show every extreme that they name: `outgoing_count`: entry d of a block counts the live leading slots of its outgoing block d; the -y block of the lowest and the +y block of the highest wall-normal blocks are empty; some +x block is full.
All inputs are finite; a program needn't handle non-finite values.
Results may differ from a plain program's by a relative error of at most 0.00029.
Values sent between devices are 32-bit elements; how exact they have to be, the bound alone decides.
No kernel may reach another device: no remote copies, remote signals or barrier semaphores. Data moves between devices by JAX's collectives and lax.ppermute only.
A program may use at most 192 MiB of HBM per device.

v0:
```python
import jax
import jax.numpy as jnp
from jax import lax
from jax.sharding import PartitionSpec as P

RESIDENT = 2048
CAP = 512
SECTIONS = 3


SECTION_WEIGHTS = (8.0 / 15.0, 5.0 / 12.0, 3.0 / 4.0)
TIME_STEP = 0.3
STREAM_SCALE = 2.0
SPAN_SCALE = 2.0
COUPLING = 0.5
CORNER_LIST = (
    (0, 0, 0),
    (0, 0, 1),
    (0, 1, 0),
    (0, 1, 1),
    (1, 0, 0),
    (1, 0, 1),
    (1, 1, 0),
    (1, 1, 1),
)


def extended_2(x, sides, width, wrap):
    for axis, dim in sides:
        size, length = (lax.axis_size(axis), x.shape[dim])
        up = [(i, (i + 1) % size) for i in range(size if wrap else size - 1)]
        down = [(j, i) for i, j in up]
        last = lax.slice_in_dim(x, length - width, length, axis=dim)
        first = lax.slice_in_dim(x, 0, width, axis=dim)
        before = lax.ppermute(last, axis, up)
        after = lax.ppermute(first, axis, down)
        x = jnp.concatenate([before, x, after], axis=dim)
    return x


def from_behind(block, axis, distance):
    devices = range(lax.axis_size(axis))
    route = [((i - distance) % len(devices), i) for i in devices]
    return lax.ppermute(block, axis, route)


def stencil(field, upper_x, lower_x, upper_y, lower_y, upper_z, lower_z, y_metric):
    slope_x = (upper_x - lower_x) * (0.5 * STREAM_SCALE)
    slope_y = (upper_y - lower_y) * (0.5 * y_metric)[None, None, :, None]
    slope_z = (upper_z - lower_z) * (0.5 * SPAN_SCALE)
    return -(field[0:1] * slope_x + field[1:2] * slope_y + field[2:3] * slope_z)


def corner_weight(offsets, corner):
    weight = None
    for dimension in range(3):
        factor = offsets[dimension] if corner[dimension] else 1.0 - offsets[dimension]
        weight = factor if weight is None else weight * factor
    return weight


def combine_all(factors, offsets, backward):
    count = factors.shape[0]
    own = lax.axis_index("gy")
    logs = jnp.log(factors.reshape(count))
    order = jnp.arange(count)
    totals = jnp.cumsum(logs)
    own_total = jnp.sum(jnp.where(order == own, totals, 0.0))
    own_log = jnp.sum(jnp.where(order == own, logs, 0.0))
    if backward:
        select = order > own
        spread = totals - logs - own_total
    else:
        select = order < own
        spread = own_total - own_log - totals
    weights = jnp.where(select, jnp.exp(jnp.where(select, spread, 0.0)), 0.0)
    return jnp.einsum("n,ncxz->cxz", weights, offsets, precision=lax.Precision.HIGHEST)


def carry_in(factor, offset, backward):
    if backward:
        factors, offsets = (
            lax.all_gather(factor[None], "gy", axis=0, tiled=True),
            lax.all_gather(offset[None], "gy", axis=0, tiled=True),
        )
        return combine_all(factors, offsets, True)
    factors, offsets = (
        lax.all_gather(factor[None], "gy", axis=0, tiled=True),
        lax.all_gather(offset[None], "gy", axis=0, tiled=True),
    )
    return combine_all(factors, offsets, False)


def local_solve(rhs, down_rate, up_rate, scale_rate):
    rows = rhs.shape[2]
    order = jnp.arange(rows)
    growth = jnp.cumprod(down_rate)
    lower_table = jnp.where(
        order[:, None] >= order[None, :], growth[:, None] / growth[None, :], 0.0
    )
    partial_down = jnp.einsum("ji,cxiz->cxjz", lower_table, rhs, precision=lax.Precision.HIGHEST)
    entering = carry_in(growth[-1:].reshape(1, 1), partial_down[:, :, -1, :], False)
    forward = partial_down + growth[None, None, :, None] * entering[:, :, None, :]
    shrink = jnp.cumprod(up_rate[::-1])[::-1]
    upper_table = jnp.where(
        order[:, None] <= order[None, :], shrink[:, None] / shrink[None, :], 0.0
    )
    scaled = scale_rate[None, None, :, None] * forward
    partial_up = jnp.einsum("ji,cxiz->cxjz", upper_table, scaled, precision=lax.Precision.HIGHEST)
    leaving = carry_in(shrink[:1].reshape(1, 1), partial_up[:, :, 0, :], True)
    return partial_up + shrink[None, None, :, None] * leaving[:, :, None, :]


def on_device(
    velocity,
    y_metric,
    forward_rate,
    backward_rate,
    pivot_inv,
    particle_vel,
    particle_cell,
    particle_offset,
    inverse_tau,
    outgoing_count,
):
    comps, cells_x, cells_y, cells_z = velocity.shape
    slot_total = particle_vel.shape[1]
    counts = outgoing_count.reshape(3)
    slot_num = jnp.arange(slot_total)
    remain = slot_num - RESIDENT
    heading = jnp.clip(remain // CAP, 0, 2)
    limit = jnp.where(heading == 0, counts[0], jnp.where(heading == 1, counts[1], counts[2]))
    live = jnp.where((slot_num < RESIDENT) | (remain % CAP < limit), 1.0, 0.0).astype(jnp.float32)
    cell_x = particle_cell // (cells_y * cells_z)
    cell_y = particle_cell // cells_z % cells_y
    cell_z = particle_cell % cells_z
    lanes = lax.axis_size("gy")
    position = lax.axis_index("gy")
    row_order = jnp.arange(cells_y + 2)
    wall_rows = (row_order == 0) & (position == 0) | (row_order == cells_y + 1) & (
        position == lanes - 1
    )
    keep_rows = jnp.where(wall_rows, 0.0, 1.0)[None, None, :, None]
    field = velocity
    moving = particle_vel
    for section_num in range(SECTIONS):
        step_size = TIME_STEP * SECTION_WEIGHTS[section_num]
        extended = extended_2(field, (("gx", 1), ("gy", 2)), 1, True) * keep_rows
        flat_ext = extended.reshape(comps, -1)
        fluid_at = jnp.zeros_like(moving)
        for corner in CORNER_LIST:
            lookup = (
                (cell_x + 1 + corner[0]) * (cells_y + 2) + cell_y + 1 + corner[1]
            ) * cells_z + (cell_z + corner[2]) % cells_z
            fluid_at = fluid_at + corner_weight(particle_offset, corner) * flat_ext[:, lookup]
        drag = inverse_tau * (fluid_at - moving)
        moving = moving + step_size * drag
        force = (
            jnp.zeros((comps, cells_x * cells_y * cells_z), jnp.float32)
            .at[:, particle_cell]
            .add(-COUPLING * drag * live)
        )
        convection = stencil(
            field,
            extended[:, 2:, 1:-1, :],
            extended[:, :-2, 1:-1, :],
            extended[:, 1:-1, 2:, :],
            extended[:, 1:-1, :-2, :],
            jnp.roll(field, -1, axis=3),
            jnp.roll(field, 1, axis=3),
            y_metric,
        )
        rhs = field + step_size * (convection + force.reshape(field.shape))
        field = local_solve(
            rhs, forward_rate[section_num], backward_rate[section_num], pivot_inv[section_num]
        )
    masked = moving * live[None, :]
    kept = masked[:, :RESIDENT]
    to_x = masked[:, RESIDENT : RESIDENT + CAP]
    to_lower = masked[:, RESIDENT + CAP : RESIDENT + 2 * CAP]
    to_upper = masked[:, RESIDENT + 2 * CAP :]
    from_x = from_behind(to_x, "gx", 1)
    paired = jnp.stack([to_lower, to_upper], axis=1)
    arrived = extended_2(paired, (("gy", 1),), 1, False)
    moved = jnp.concatenate([kept, from_x, arrived[:, 3], arrived[:, 0]], axis=1)
    return (field, moved)


def solution(mesh):
    return jax.shard_map(
        on_device,
        mesh=mesh,
        in_specs=(
            P(None, "gx", "gy", None),
            P("gy"),
            P(None, "gy"),
            P(None, "gy"),
            P(None, "gy"),
            P(None, ("gx", "gy")),
            P(("gx", "gy")),
            P(None, ("gx", "gy")),
            P(("gx", "gy")),
            P("gx", "gy", None),
        ),
        out_specs=(P(None, "gx", "gy", None), P(None, ("gx", "gy"))),
        check_vma=False,
    )
```

profile of v0, /device:TPU:0, one launch (start us, length us, event | category | flops | bytes accessed | tf_op | source)
XLA Modules:
  0.0 811.3 jit_solution(15511217554201586929)
XLA Ops:
  62.6 13.5 %copy.207 = f32[3,3,18,1024]{0,3,2,1:T(8,128)} copy(f32[3,3,18,1024]{3,2,0,1:T(8,128)S(1)} %get-tuple-element.39) | data formatting | bytes 1327104 | tf_op jit(solution)/shard_map/concatenate | solution.py:37
  76.1 25.9 %bitcast_multiply_fusion.2 = f32[3,55296]{0,1:T(8,128)} fusion(f32[3,3,18,1024]{0,3,2,1:T(8,128)} %copy.207, f32[55296]{0:T(1024)S(1)} %mul.778), kind=kLoop, calls=%fused_computation.29 | loop fusion | flops 165888 | bytes 1548288 | tf_op jit(solution)/shard_map/mul | solution.py:148
  102.0 15.7 %gather_fusion.7 = f32[3584,3]{1,0:T(8,128)S(1)} fusion(f32[3,55296]{0,1:T(8,128)} %bitcast_multiply_fusion.2, s32[4096]{0:T(1024)} %get-tuple-element.111), kind=kCustom, calls=%fused_computation.7 | custom fusion | bytes 100352 | tf_op jit(solution)/shard_map/gather | solution.py:155
  118.9 15.7 %gather_fusion.6 = f32[3584,3]{1,0:T(8,128)S(1)} fusion(f32[3,55296]{0,1:T(8,128)} %bitcast_multiply_fusion.2, s32[4096]{0:T(1024)} %get-tuple-element.112), kind=kCustom, calls=%fused_computation.6 | custom fusion | bytes 100352 | tf_op jit(solution)/shard_map/gather | solution.py:155
  135.8 15.7 %gather_fusion.5 = f32[3584,3]{1,0:T(8,128)S(1)} fusion(f32[3,55296]{0,1:T(8,128)} %bitcast_multiply_fusion.2, s32[4096]{0:T(1024)} %pad_clamp_fusion.2), kind=kCustom, calls=%fused_computation.5 | custom fusion | bytes 100352 | tf_op jit(solution)/shard_map/gather | solution.py:155
  152.6 15.7 %gather_fusion.4 = f32[3584,3]{1,0:T(8,128)S(1)} fusion(f32[3,55296]{0,1:T(8,128)} %bitcast_multiply_fusion.2, s32[4096]{0:T(1024)} %get-tuple-element.103), kind=kCustom, calls=%fused_computation.4 | custom fusion | bytes 100352 | tf_op jit(solution)/shard_map/gather | solution.py:155
  169.5 15.7 %gather_fusion.3 = f32[3584,3]{1,0:T(8,128)S(1)} fusion(f32[3,55296]{0,1:T(8,128)} %bitcast_multiply_fusion.2, s32[4096]{0:T(1024)} %get-tuple-element.104), kind=kCustom, calls=%fused_computation.3 | custom fusion | bytes 100352 | tf_op jit(solution)/shard_map/gather | solution.py:155
  186.4 15.7 %gather_fusion.2 = f32[3584,3]{1,0:T(8,128)S(1)} fusion(f32[3,55296]{0,1:T(8,128)} %bitcast_multiply_fusion.2, s32[4096]{0:T(1024)} %get-tuple-element.105), kind=kCustom, calls=%fused_computation.2 | custom fusion | bytes 100352 | tf_op jit(solution)/shard_map/gather | solution.py:155
  203.3 15.7 %gather_fusion.1 = f32[3584,3]{1,0:T(8,128)S(1)} fusion(f32[3,55296]{0,1:T(8,128)} %bitcast_multiply_fusion.2, s32[4096]{0:T(1024)} %get-tuple-element.106), kind=kCustom, calls=%fused_computation.1 | custom fusion | bytes 100352 | tf_op jit(solution)/shard_map/gather | solution.py:155
  220.1 14.7 %gather_fusion = f32[3584,3]{1,0:T(8,128)S(1)} fusion(f32[3,55296]{0,1:T(8,128)} %bitcast_multiply_fusion.2, s32[4096]{0:T(1024)S(1)} %pad_clamp_fusion.7), kind=kCustom, calls=%fused_computation | custom fusion | bytes 100352 | tf_op jit(solution)/shard_map/gather | solution.py:155
  239.4 23.5 %scatter_custom_fusion = f32[3,16384]{0,1:T(8,128)} fusion(s32[3584]{0:T(1024)} %get-tuple-element.84, f32[3584,3]{1,0:T(8,128)S(1)} %copy.155, f32[]{:T(128)} %constant.184.clone.1), kind=kCustom, calls=%fused_computation.34 | custom fusion | flops 10752 | bytes 197120 | tf_op jit(solution)/shard_map/scatter-add | solution.py:161
  307.8 13.5 %copy.209 = f32[3,3,18,1024]{0,3,2,1:T(8,128)} copy(f32[3,3,18,1024]{3,2,0,1:T(8,128)S(1)} %get-tuple-element.37) | data formatting | bytes 1327104 | tf_op jit(solution)/shard_map/concatenate | solution.py:37
  321.3 26.0 %bitcast_multiply_fusion.1 = f32[3,55296]{0,1:T(8,128)} fusion(f32[3,3,18,1024]{0,3,2,1:T(8,128)} %copy.209, f32[55296]{0:T(1024)S(1)} %mul.778), kind=kLoop, calls=%fused_computation.28 | loop fusion | flops 165888 | bytes 1548288 | tf_op jit(solution)/shard_map/mul | solution.py:148
  347.3 16.4 %gather_fusion.15 = f32[3584,3]{1,0:T(8,128)} fusion(f32[3,55296]{0,1:T(8,128)} %bitcast_multiply_fusion.1, s32[4096]{0:T(1024)S(1)} %copy-done.16), kind=kCustom, calls=%fused_computation.15 | custom fusion | bytes 100352 | tf_op jit(solution)/shard_map/gather | solution.py:155
  363.7 16.4 %gather_fusion.14 = f32[3584,3]{1,0:T(8,128)} fusion(f32[3,55296]{0,1:T(8,128)} %bitcast_multiply_fusion.1, s32[4096]{0:T(1024)S(1)} %copy-done.10), kind=kCustom, calls=%fused_computation.14 | custom fusion | bytes 100352 | tf_op jit(solution)/shard_map/gather | solution.py:155
  380.1 16.4 %gather_fusion.13 = f32[3584,3]{1,0:T(8,128)} fusion(f32[3,55296]{0,1:T(8,128)} %bitcast_multiply_fusion.1, s32[4096]{0:T(1024)S(1)} %copy-done.6), kind=kCustom, calls=%fused_computation.13 | custom fusion | bytes 100352 | tf_op jit(solution)/shard_map/gather | solution.py:155
  396.5 16.4 %gather_fusion.12 = f32[3584,3]{1,0:T(8,128)} fusion(f32[3,55296]{0,1:T(8,128)} %bitcast_multiply_fusion.1, s32[4096]{0:T(1024)S(1)} %copy-done.12), kind=kCustom, calls=%fused_computation.12 | custom fusion | bytes 100352 | tf_op jit(solution)/shard_map/gather | solution.py:155
  412.9 16.4 %gather_fusion.11 = f32[3584,3]{1,0:T(8,128)} fusion(f32[3,55296]{0,1:T(8,128)} %bitcast_multiply_fusion.1, s32[4096]{0:T(1024)S(1)} %copy-done.8), kind=kCustom, calls=%fused_computation.11 | custom fusion | bytes 100352 | tf_op jit(solution)/shard_map/gather | solution.py:155
  429.3 16.4 %gather_fusion.10 = f32[3584,3]{1,0:T(8,128)} fusion(f32[3,55296]{0,1:T(8,128)} %bitcast_multiply_fusion.1, s32[4096]{0:T(1024)S(1)} %copy-done.18), kind=kCustom, calls=%fused_computation.10 | custom fusion | bytes 100352 | tf_op jit(solution)/shard_map/gather | solution.py:155
  445.7 16.4 %gather_fusion.9 = f32[3584,3]{1,0:T(8,128)} fusion(f32[3,55296]{0,1:T(8,128)} %bitcast_multiply_fusion.1, s32[4096]{0:T(1024)S(1)} %copy-done.14), kind=kCustom, calls=%fused_computation.9 | custom fusion | bytes 100352 | tf_op jit(solution)/shard_map/gather | solution.py:155
  462.1 14.7 %gather_fusion.8 = f32[3584,3]{1,0:T(8,128)S(1)} fusion(f32[3,55296]{0,1:T(8,128)} %bitcast_multiply_fusion.1, s32[4096]{0:T(1024)S(1)} %pad_clamp_fusion.7), kind=kCustom, calls=%fused_computation.8 | custom fusion | bytes 100352 | tf_op jit(solution)/shard_map/gather | solution.py:155
  499.9 23.5 %scatter_custom_fusion.1 = f32[3,16384]{0,1:T(8,128)} fusion(s32[3584]{0:T(1024)} %get-tuple-element.84, f32[3584,3]{1,0:T(8,128)S(1)} %copy.172, f32[]{:T(128)} %constant.184.clone.1), kind=kCustom, calls=%fused_computation.32 | custom fusion | flops 10752 | bytes 197120 | tf_op jit(solution)/shard_map/scatter-add | solution.py:161
  579.5 26.0 %bitcast_multiply_fusion = f32[3,55296]{0,1:T(8,128)} fusion(f32[3,3,18,1024]{0,3,2,1:T(8,128)} %copy.211, f32[55296]{0:T(1024)S(1)} %mul.778), kind=kLoop, calls=%fused_computation.27 | loop fusion | flops 165888 | bytes 1548288 | tf_op jit(solution)/shard_map/mul | solution.py:148
  605.6 14.8 %gather_fusion.23 = f32[3584,3]{1,0:T(8,128)S(1)} fusion(f32[3,55296]{0,1:T(8,128)} %bitcast_multiply_fusion, s32[4096]{0:T(1024)S(1)} %copy-done.17), kind=kCustom, calls=%fused_computation.23 | custom fusion | bytes 100352 | tf_op jit(solution)/shard_map/gather | solution.py:155
  620.3 16.4 %gather_fusion.22 = f32[3584,3]{1,0:T(8,128)} fusion(f32[3,55296]{0,1:T(8,128)} %bitcast_multiply_fusion, s32[4096]{0:T(1024)S(1)} %copy-done.11), kind=kCustom, calls=%fused_computation.22 | custom fusion | bytes 100352 | tf_op jit(solution)/shard_map/gather | solution.py:155
  636.7 16.4 %gather_fusion.21 = f32[3584,3]{1,0:T(8,128)} fusion(f32[3,55296]{0,1:T(8,128)} %bitcast_multiply_fusion, s32[4096]{0:T(1024)S(1)} %copy-done.7), kind=kCustom, calls=%fused_computation.21 | custom fusion | bytes 100352 | tf_op jit(solution)/shard_map/gather | solution.py:155
  653.2 16.4 %gather_fusion.20 = f32[3584,3]{1,0:T(8,128)} fusion(f32[3,55296]{0,1:T(8,128)} %bitcast_multiply_fusion, s32[4096]{0:T(1024)S(1)} %copy-done.13), kind=kCustom, calls=%fused_computation.20 | custom fusion | bytes 100352 | tf_op jit(solution)/shard_map/gather | solution.py:155
  669.6 16.4 %gather_fusion.19 = f32[3584,3]{1,0:T(8,128)} fusion(f32[3,55296]{0,1:T(8,128)} %bitcast_multiply_fusion, s32[4096]{0:T(1024)S(1)} %copy-done.9), kind=kCustom, calls=%fused_computation.19 | custom fusion | bytes 100352 | tf_op jit(solution)/shard_map/gather | solution.py:155
  685.9 16.4 %gather_fusion.18 = f32[3584,3]{1,0:T(8,128)} fusion(f32[3,55296]{0,1:T(8,128)} %bitcast_multiply_fusion, s32[4096]{0:T(1024)S(1)} %copy-done.19), kind=kCustom, calls=%fused_computation.18 | custom fusion | bytes 100352 | tf_op jit(solution)/shard_map/gather | solution.py:155
  702.4 16.4 %gather_fusion.17 = f32[3584,3]{1,0:T(8,128)} fusion(f32[3,55296]{0,1:T(8,128)} %bitcast_multiply_fusion, s32[4096]{0:T(1024)S(1)} %copy-done.15), kind=kCustom, calls=%fused_computation.17 | custom fusion | bytes 100352 | tf_op jit(solution)/shard_map/gather | solution.py:155
  718.7 16.4 %gather_fusion.16 = f32[3584,3]{1,0:T(8,128)} fusion(f32[3,55296]{0,1:T(8,128)} %bitcast_multiply_fusion, s32[4096]{0:T(1024)S(1)} %pad_clamp_fusion.7), kind=kCustom, calls=%fused_computation.16 | custom fusion | bytes 100352 | tf_op jit(solution)/shard_map/gather | solution.py:155
  752.1 23.5 %scatter_custom_fusion.2 = f32[3,16384]{0,1:T(8,128)} fusion(s32[3584]{0:T(1024)} %get-tuple-element.84, f32[3584,3]{1,0:T(8,128)S(1)} %copy.188, f32[]{:T(128)} %constant.184.clone.1), kind=kCustom, calls=%fused_computation.30 | custom fusion | flops 10752 | bytes 197120 | tf_op jit(solution)/shard_map/scatter-add | solution.py:161
  (385 shorter events, 246.2 us)
Async XLA Ops:
  0.6 53.9 %copy-start = (f32[3,1,16,1024]{3,2,1,0:T(8,128)S(1)}, f32[3,1,16,1024]{3,2,1,0:T(8,128)}, u32[]{:S(2)}) copy-start(f32[3,1,16,1024]{3,2,1,0:T(8,128)} %param.10) | copy-start | bytes 589828
  0.7 43.7 %copy-start.68 = (f32[3,16]{1,0:T(4,128)S(1)}, f32[3,16]{1,0:T(4,128)}, u32[]{:S(2)}) copy-start(f32[3,16]{1,0:T(4,128)} %param.14) | copy-start | bytes 580
  0.7 53.3 %copy-start.87 = (f32[16]{0:T(128)S(1)}, f32[16]{0:T(128)}, u32[]{:S(2)}) copy-start(f32[16]{0:T(128)} %param.11) | copy-start | bytes 196
  0.7 53.8 %collective-permute-start.1 = (f32[3,1,16,1024]{3,2,0,1:T(8,128)}, f32[3,1,16,1024]{3,2,0,1:T(8,128)S(1)}, u32[]{:S(2)}, u32[]{:S(2)}) collective-permute-start(f32[3,1,16,1024]{3,2,0,1:T(8,128)} %bitcast.339), channel_id=1, source_target_pairs={{8,0},{16,8},{24,16},{0,24},{9,1},{17,9},{25,17},{1,25},{10,2},{18... | collective-permute-start | bytes 589832 | tf_op jit(solution)/shard_map/ppermute | solution.py:36
  5.8 48.7 %collective-permute-start = (f32[3,1,16,1024]{3,2,0,1:T(8,128)}, f32[3,1,16,1024]{3,2,0,1:T(8,128)S(1)}, u32[]{:S(2)}, u32[]{:S(2)}) collective-permute-start(f32[3,1,16,1024]{3,2,0,1:T(8,128)} %bitcast.340), channel_id=1, source_target_pairs={{0,8},{8,16},{16,24},{24,0},{1,9},{9,17},{17,25},{25,1},{2,10},{10... | collective-permute-start | bytes 589832 | tf_op jit(solution)/shard_map/ppermute | solution.py:35
  54.6 7.7 collective-permute-start.3
  54.6 7.7 collective-permute-start.2
  278.3 29.2 %copy-start.56 = (f32[18]{0:T(128)S(1)}, f32[18]{0:T(128)}, u32[]{:S(2)}) copy-start(f32[18]{0:T(128)} %copy-done.55) | copy-start | bytes 220
  289.0 8.8 %collective-permute-start.5 = (f32[3,1,16,1024]{3,2,0,1:T(8,128)S(1)}, f32[3,1,16,1024]{3,2,0,1:T(8,128)S(1)}, u32[]{:S(2)}, u32[]{:S(2)}) collective-permute-start(f32[3,1,16,1024]{3,2,0,1:T(8,128)S(1)} %multiply_add_fusion.1), channel_id=1, source_target_pairs={{8,0},{16,8},{24,16},{0,24},{9,1},{17,9},{25,17},{1,25},{10,2},{18... | collective-permute-start | bytes 589832 | tf_op jit(solution)/shard_map/ppermute | solution.py:36
  292.6 9.6 %collective-permute-start.4 = (f32[3,1,16,1024]{3,2,0,1:T(8,128)S(1)}, f32[3,1,16,1024]{3,2,0,1:T(8,128)S(1)}, u32[]{:S(2)}, u32[]{:S(2)}) collective-permute-start(f32[3,1,16,1024]{3,2,0,1:T(8,128)S(1)} %multiply_add_fusion.1), channel_id=1, source_target_pairs={{0,8},{8,16},{16,24},{24,0},{1,9},{9,17},{17,25},{25,1},{2,10},{10... | collective-permute-start | bytes 589832 | tf_op jit(solution)/shard_map/ppermute | solution.py:35
  302.3 2.8 collective-permute-start.7
  303.2 4.3 collective-permute-start.6
  321.3 42.4 %copy-start.10 = (s32[4096]{0:T(1024)S(1)}, s32[4096]{0:T(1024)}, u32[]{:S(2)}) copy-start(s32[4096]{0:T(1024)} %get-tuple-element.112) | copy-start | bytes 49156
  321.3 58.8 %copy-start.6 = (s32[4096]{0:T(1024)S(1)}, s32[4096]{0:T(1024)}, u32[]{:S(2)}) copy-start(s32[4096]{0:T(1024)} %pad_clamp_fusion.2) | copy-start | bytes 49156
  321.3 75.2 %copy-start.12 = (s32[4096]{0:T(1024)S(1)}, s32[4096]{0:T(1024)}, u32[]{:S(2)}) copy-start(s32[4096]{0:T(1024)} %get-tuple-element.103) | copy-start | bytes 49156
  347.3 65.6 %copy-start.8 = (s32[4096]{0:T(1024)S(1)}, s32[4096]{0:T(1024)}, u32[]{:S(2)}) copy-start(s32[4096]{0:T(1024)} %get-tuple-element.104) | copy-start | bytes 49156
  347.3 82.0 %copy-start.18 = (s32[4096]{0:T(1024)S(1)}, s32[4096]{0:T(1024)}, u32[]{:S(2)}) copy-start(s32[4096]{0:T(1024)} %get-tuple-element.105) | copy-start | bytes 49156
  347.3 98.4 %copy-start.14 = (s32[4096]{0:T(1024)S(1)}, s32[4096]{0:T(1024)}, u32[]{:S(2)}) copy-start(s32[4096]{0:T(1024)} %get-tuple-element.106) | copy-start | bytes 49156
  538.6 27.2 %copy-start.57 = (f32[18]{0:T(128)S(1)}, f32[18]{0:T(128)}, u32[]{:S(2)}) copy-start(f32[18]{0:T(128)} %copy-done.55) | copy-start | bytes 220
  549.3 11.4 %collective-permute-start.9 = (f32[3,1,16,1024]{3,2,0,1:T(8,128)S(1)}, f32[3,1,16,1024]{3,2,0,1:T(8,128)S(1)}, u32[]{:S(2)}, u32[]{:S(2)}) collective-permute-start(f32[3,1,16,1024]{3,2,0,1:T(8,128)S(1)} %multiply_add_fusion), channel_id=1, source_target_pairs={{8,0},{16,8},{24,16},{0,24},{9,1},{17,9},{25,17},{1,25},{10,2},{18... | collective-permute-start | bytes 589832 | tf_op jit(solution)/shard_map/ppermute | solution.py:36
  550.8 9.9 %collective-permute-start.8 = (f32[3,1,16,1024]{3,2,0,1:T(8,128)S(1)}, f32[3,1,16,1024]{3,2,0,1:T(8,128)S(1)}, u32[]{:S(2)}, u32[]{:S(2)}) collective-permute-start(f32[3,1,16,1024]{3,2,0,1:T(8,128)S(1)} %multiply_add_fusion), channel_id=1, source_target_pairs={{0,8},{8,16},{16,24},{24,0},{1,9},{9,17},{17,25},{25,1},{2,10},{10... | collective-permute-start | bytes 589832 | tf_op jit(solution)/shard_map/ppermute | solution.py:35
  560.8 2.6 collective-permute-start.11
  561.5 4.3 collective-permute-start.10
  579.5 40.8 %copy-start.11 = (s32[4096]{0:T(1024)S(1)}, s32[4096]{0:T(1024)}, u32[]{:S(2)}) copy-start(s32[4096]{0:T(1024)} %get-tuple-element.112) | copy-start | bytes 49156
  579.5 57.2 %copy-start.7 = (s32[4096]{0:T(1024)S(1)}, s32[4096]{0:T(1024)}, u32[]{:S(2)}) copy-start(s32[4096]{0:T(1024)} %pad_clamp_fusion.2) | copy-start | bytes 49156
  579.5 73.6 %copy-start.13 = (s32[4096]{0:T(1024)S(1)}, s32[4096]{0:T(1024)}, u32[]{:S(2)}) copy-start(s32[4096]{0:T(1024)} %get-tuple-element.103) | copy-start | bytes 49156
  605.5 64.0 %copy-start.9 = (s32[4096]{0:T(1024)S(1)}, s32[4096]{0:T(1024)}, u32[]{:S(2)}) copy-start(s32[4096]{0:T(1024)} %get-tuple-element.104) | copy-start | bytes 49156
  605.5 80.4 %copy-start.19 = (s32[4096]{0:T(1024)S(1)}, s32[4096]{0:T(1024)}, u32[]{:S(2)}) copy-start(s32[4096]{0:T(1024)} %get-tuple-element.105) | copy-start | bytes 49156
  605.6 96.8 %copy-start.15 = (s32[4096]{0:T(1024)S(1)}, s32[4096]{0:T(1024)}, u32[]{:S(2)}) copy-start(s32[4096]{0:T(1024)} %get-tuple-element.106) | copy-start | bytes 49156
  801.4 5.8 collective-permute-start.14
  803.6 3.6 collective-permute-start.13
  804.9 5.5 collective-permute-start.12
  (72 other events, 570.7 us)
where the time goes:
time: 819 us; the launch traced here: 811 us
  local copies, waits for them, and re-layouts  512 us (63%)
  other arithmetic  175 us (21%)
  blocking collectives  66.6 us (8%)
  waiting for transfers between devices  27.9 us (3%)
  starting transfers between devices  18.2 us (2%)
    gather x48, local copies, waits for them, and re-layouts, on_device(): flat_ext[:, lookup]  428 us
    mul x6, other arithmetic, on_device(): extended = extended_2(field, (('gx', 1), ('gy', 2)), 1, True) * keep_rows  78.6 us
    scatter-add x3, other arithmetic, on_device(): force = jnp.zeros((comps, cells_x * cells_y * cells_z), jnp.float32).at[:...  70.4 us
    all_gather x6, blocking collectives, carry_in(): lax.all_gather(offset[None], 'gy', axis=0, tiled=True)  53.2 us
    concatenate x3, local copies, waits for them, and re-layouts, extended_2(): x = jnp.concatenate([before, x, after], axis=dim)  40.6 us
  transfers between devices with their start and end apart: 15, of which 8 were waited for; matrix products, arithmetic and copies ran while one was open for 5% of the time, Pallas kernels for 0%

commit v1 on v0

v1 whole, which is shorter than its diff:
```python
import functools

import jax
import jax.numpy as jnp
from jax import lax
from jax.experimental import pallas as pl
from jax.experimental.pallas import tpu as pltpu
from jax.sharding import PartitionSpec as P

RESIDENT = 2048
CAP = 512
SECTIONS = 3

SECTION_WEIGHTS = (8.0 / 15.0, 5.0 / 12.0, 3.0 / 4.0)
TIME_STEP = 0.3
STREAM_SCALE = 2.0
SPAN_SCALE = 2.0
COUPLING = 0.5
COMPS = 3
TILE = 512
DEPTH = 256
VMEM_LIMIT = 24 * 1024 * 1024

F32 = jnp.float32
BF16 = jnp.bfloat16


def params():
    return pltpu.CompilerParams(vmem_limit_bytes=VMEM_LIMIT)


def whole_in_vmem(count):
    return [pl.BlockSpec(memory_space=pltpu.VMEM)] * count


def selector(column, depth_total):
    width = column.shape[1]
    shape = (DEPTH // 16, 16, width)
    order = lax.broadcasted_iota(jnp.int32, shape, 0) * 16 + lax.broadcasted_iota(jnp.int32, shape, 1)
    order = order.astype(F32).astype(BF16)
    one, none = jnp.ones((), BF16), jnp.zeros((), BF16)
    tiles = []
    for k in range(depth_total // DEPTH):
        wanted = jnp.broadcast_to(column - float(DEPTH * k), (16, width)).astype(BF16)
        tiles.append(jnp.where(order == wanted[None], one, none).reshape(DEPTH, width))
    return tiles


def split_rows(rows):
    length = rows.shape[1]
    high = rows.astype(BF16).astype(F32)
    low = rows - high
    ahead = [pltpu.roll(part, length - 1, 1) for part in (high, low)]
    return jnp.concatenate([high, low] + ahead, axis=0).astype(BF16)


def looked_up(table_ref, tiles):
    total = None
    for k, tile in enumerate(tiles):
        part = jnp.dot(
            table_ref[:, DEPTH * k : DEPTH * (k + 1)], tile, preferred_element_type=F32
        )
        total = part if total is None else total + part
    return total


def blend_z(values, fz):
    rows = values.shape[0] // 4
    near = values[:rows] + values[rows : 2 * rows]
    far = values[2 * rows : 3 * rows] + values[3 * rows :]
    return near * (1.0 - fz) + far * fz


def own_plane_kernel(cells_z, u_ref, cell_ref, off_ref, out_ref, table_ref):
    rows = u_ref.shape[0] // COMPS
    table_ref[...] = split_rows(u_ref[...])

    @pl.loop(0, cell_ref.shape[1] // TILE)
    def _(t):
        here = pl.ds(pl.multiple_of(t * TILE, TILE), TILE)
        cell = cell_ref[:, here]
        row, column = cell // cells_z, (cell % cells_z).astype(F32)
        fx, fy, fz = (off_ref[d : d + 1, here] for d in range(3))
        blended = blend_z(looked_up(table_ref, selector(column, cells_z)), fz)
        order = lax.broadcasted_iota(jnp.int32, (rows, TILE), 0)
        weight = jnp.where(order == row, 1.0 - fy, jnp.where(order == row + 1, fy, 0.0))
        weight = weight * (1.0 - fx)
        for c in range(COMPS):
            part = blended[rows * c : rows * (c + 1)] * weight
            out_ref[c : c + 1, here] = jnp.sum(part, axis=0, keepdims=True)


def section_kernel(
    cells_z,
    step,
    last,
    info_ref,
    u_ref,
    xp_ref,
    xm_ref,
    yp_ref,
    ym_ref,
    corner_ref,
    cell_ref,
    off_ref,
    tau_ref,
    v_ref,
    near_ref,
    metric_ref,
    mat_ref,
    scal_ref,
    w_ref,
    pq_ref,
    v_out_ref,
    table_ref,
    force_ref,
):
    rows = u_ref.shape[0] // COMPS
    top = jnp.where(info_ref[4] == 0, 0.0, 1.0).astype(F32)
    bottom = jnp.where(info_ref[3] == 0, 0.0, 1.0).astype(F32)
    y_plus = yp_ref[...] * top
    y_minus = ym_ref[...] * bottom
    corner = corner_ref[...] * top
    pad = jnp.zeros((2, cells_z), F32)
    table_ref[...] = split_rows(jnp.concatenate([xp_ref[...], y_plus, corner, pad], axis=0))
    force_ref[...] = jnp.zeros_like(force_ref)

    @pl.loop(0, cell_ref.shape[1] // TILE)
    def _(t):
        here = pl.ds(pl.multiple_of(t * TILE, TILE), TILE)
        cell = cell_ref[:, here]
        row, column = cell // cells_z, (cell % cells_z).astype(F32)
        fx, fy, fz = (off_ref[d : d + 1, here] for d in range(3))
        tiles = selector(column, cells_z)
        blended = blend_z(looked_up(table_ref, tiles), fz)
        order = lax.broadcasted_iota(jnp.int32, (rows, TILE), 0)
        at_row = order == row
        weight = jnp.where(at_row, 1.0 - fy, jnp.where(order == row + 1, fy, 0.0)) * fx
        edge = jnp.where(row == rows - 1, fy, 0.0)
        slot = t * TILE + lax.broadcasted_iota(jnp.int32, (1, TILE), 1)
        remain = slot - RESIDENT
        heading = remain // CAP
        limit = jnp.where(
            heading <= 0, info_ref[0], jnp.where(heading == 1, info_ref[1], info_ref[2])
        )
        live = jnp.where((remain < 0) | (remain % CAP < limit), 1.0, 0.0)
        base = COMPS * rows
        tau = tau_ref[:, here]
        spread = []
        for c in range(COMPS):
            part = jnp.sum(blended[rows * c : rows * (c + 1)] * weight, axis=0, keepdims=True)
            side = blended[base + c : base + c + 1] * (1.0 - fx)
            side = side + blended[base + COMPS + c : base + COMPS + c + 1] * fx
            fluid = near_ref[c : c + 1, here] + part + side * edge
            v = v_ref[c : c + 1, here]
            drag = tau * (fluid - v)
            v = v + step * drag
            v_out_ref[c : c + 1, here] = v * live if last else v
            spread.append(jnp.where(at_row, drag * live * (-COUPLING), 0.0))
        spread = jnp.concatenate(spread, axis=0)
        high = spread.astype(BF16).astype(F32)
        spread = jnp.concatenate([high, spread - high], axis=0).astype(BF16)
        for k, tile in enumerate(tiles):
            force_ref[:, DEPTH * k : DEPTH * (k + 1)] += lax.dot_general(
                spread, tile, (((1,), (1,)), ((), ())), preferred_element_type=F32
            )

    u = u_ref[...]
    slope_x = (xp_ref[...] - xm_ref[...]) * (0.5 * STREAM_SCALE)
    slope_z = (pltpu.roll(u, cells_z - 1, 1) - pltpu.roll(u, 1, 1)) * (0.5 * SPAN_SCALE)
    metric = 0.5 * metric_ref[...]
    count = COMPS * rows
    rhs = []
    for c in range(COMPS):
        own = slice(rows * c, rows * (c + 1))
        field = u[own]
        upper = jnp.concatenate([field[1:], y_plus[c : c + 1]], axis=0)
        lower = jnp.concatenate([y_minus[c : c + 1], field[:-1]], axis=0)
        slope_y = (upper - lower) * metric
        convection = -(
            u[:rows] * slope_x[own] + u[rows : 2 * rows] * slope_y + u[2 * rows :] * slope_z[own]
        )
        force = force_ref[own, :] + force_ref[count + rows * c : count + rows * (c + 1), :]
        rhs.append(field + step * (convection + force))
    solved = jnp.dot(
        mat_ref[...],
        jnp.concatenate(rhs, axis=0),
        precision=lax.Precision.HIGHEST,
        preferred_element_type=F32,
    )
    w_ref[...] = solved[:count]
    pq_ref[0:COMPS, :] = solved[count : count + COMPS]
    for c in range(COMPS):
        pq_ref[COMPS + c : COMPS + c + 1, :] = solved[rows * c : rows * c + 1]
    pq_ref[6:7, :] = scal_ref[...]
    pq_ref[7:8, :] = jnp.zeros_like(scal_ref)


def join_kernel(last, info_ref, all_ref, w_ref, enter_ref, leave_ref, u_ref, *more):
    blocks = all_ref.shape[0]
    rows = w_ref.shape[0] // COMPS
    here = info_ref[3]
    scal = [[all_ref[k, 6:7, i : i + 1] for i in range(5)] for k in range(blocks)]
    entering = jnp.zeros(all_ref.shape[1:], F32)[:COMPS]
    zero = entering
    at = []
    own_in = zero
    below = [jnp.zeros((1, 1), F32)] * 2
    for k in range(blocks):
        at.append(entering)
        own_in = jnp.where(here == k, entering, own_in)
        below = [jnp.where(here == k + 1, scal[k][3 + i], below[i]) for i in range(2)]
        entering = all_ref[k, 0:COMPS, :] + scal[k][0] * entering
    leaving = zero
    own_out = zero
    for k in reversed(range(blocks)):
        own_out = jnp.where(here == k, leaving, own_out)
        leaving = all_ref[k, COMPS : 2 * COMPS, :] + scal[k][2] * at[k] + scal[k][1] * leaving
    for c in range(COMPS):
        own = slice(rows * c, rows * (c + 1))
        u_ref[own, :] = (
            w_ref[own, :]
            + enter_ref[...] * own_in[c : c + 1]
            + leave_ref[...] * own_out[c : c + 1]
        )
    if not last:
        yp_ref, ym_ref = more
        yp_ref[...] = own_out
        for c in range(COMPS):
            ym_ref[c : c + 1, :] = (
                below[0] * own_in[c : c + 1] + below[1] * u_ref[rows * c : rows * c + 1, :]
            )


def block_tables(forward_rate, backward_rate, pivot_inv):
    rows = forward_rate.shape[1]
    i = jnp.arange(rows)[:, None, None]
    j = jnp.arange(rows + 1)[None, :, None]
    m = jnp.arange(rows)[None, None, :]
    lower = jnp.prod(
        jnp.where((m >= j) & (m <= i), forward_rate[:, None, None, :], 1.0), axis=-1
    ) * jnp.where(i >= j - 1, 1.0, 0.0)[..., 0]
    upper = jnp.prod(
        jnp.where((m >= i) & (m < j), backward_rate[:, None, None, :], 1.0), axis=-1
    ) * jnp.where(j >= i, 1.0, 0.0)[..., 0]
    both = jnp.sum(
        upper[:, :, :rows, None] * (pivot_inv[:, :, None] * lower)[:, None, :, :], axis=2
    )
    eye = jnp.eye(COMPS, dtype=F32)
    body = (eye[None, :, None, :, None] * both[:, None, :, None, 1:]).reshape(
        SECTIONS, COMPS * rows, COMPS * rows
    )
    tail = (eye[None, :, :, None] * lower[:, None, None, -1, 1:]).reshape(
        SECTIONS, COMPS, COMPS * rows
    )
    matrix = jnp.concatenate(
        [body, tail, jnp.zeros((SECTIONS, 8 - COMPS, COMPS * rows), F32)], axis=1
    )
    enter, leave = both[:, :, 0], upper[:, :, -1]
    scal = jnp.stack(
        [lower[:, -1, 0], leave[:, 0], enter[:, 0], pivot_inv[:, -1], backward_rate[:, -1]], axis=1
    )
    return matrix, enter[:, :, None], leave[:, :, None], scal


def on_device(
    velocity,
    y_metric,
    forward_rate,
    backward_rate,
    pivot_inv,
    particle_vel,
    particle_cell,
    particle_offset,
    inverse_tau,
    outgoing_count,
):
    comps, cells_x, cells_y, cells_z = velocity.shape
    assert (comps, cells_x) == (COMPS, 1)
    slots = particle_vel.shape[1]
    size_x, size_y = lax.axis_size("gx"), lax.axis_size("gy")
    ring_x = [(i, (i + 1) % size_x) for i in range(size_x)]
    back_x = [(b, a) for a, b in ring_x]
    ring_y = [(i, (i + 1) % size_y) for i in range(size_y)]
    back_y = [(b, a) for a, b in ring_y]
    diagonal = [
        (((x + 1) % size_x) * size_y + (y + 1) % size_y, x * size_y + y)
        for x in range(size_x)
        for y in range(size_y)
    ]
    position = lax.axis_index("gy")
    info = jnp.concatenate(
        [
            outgoing_count.reshape(3),
            jnp.stack([position, size_y - 1 - position]).astype(jnp.int32),
        ]
    )
    u = velocity.reshape(COMPS * cells_y, cells_z)
    first = velocity[:, 0, 0, :]
    final = velocity[:, 0, cells_y - 1, :]
    xp = lax.ppermute(u, "gx", back_x)
    xm = lax.ppermute(u, "gx", ring_x)
    yp = lax.ppermute(first, "gy", back_y)
    ym = lax.ppermute(final, "gy", ring_y)
    corner = lax.ppermute(first, ("gx", "gy"), diagonal)

    cell = particle_cell.reshape(1, slots)
    tau = inverse_tau.reshape(1, slots)
    metric = y_metric.reshape(cells_y, 1)
    matrix, enter, leave, scal = block_tables(forward_rate, backward_rate, pivot_inv)
    scal = jnp.pad(scal, ((0, 0), (0, cells_z - scal.shape[1])))
    v = particle_vel
    field_like = jax.ShapeDtypeStruct(u.shape, F32)
    edge_like = jax.ShapeDtypeStruct((COMPS, cells_z), F32)
    slots_like = jax.ShapeDtypeStruct((COMPS, slots), F32)
    smem = pl.BlockSpec(memory_space=pltpu.SMEM)
    for k in range(SECTIONS):
        last = k == SECTIONS - 1
        near = pl.pallas_call(
            functools.partial(own_plane_kernel, cells_z),
            out_shape=slots_like,
            in_specs=whole_in_vmem(3),
            out_specs=whole_in_vmem(1)[0],
            scratch_shapes=[pltpu.VMEM((4 * u.shape[0], cells_z), BF16)],
            compiler_params=params(),
            cost_estimate=pl.CostEstimate(
                flops=8 * u.shape[0] * cells_z * slots, bytes_accessed=1 << 18, transcendentals=0
            ),
            name="own_plane",
        )(u, cell, particle_offset)
        w, pq, v = pl.pallas_call(
            functools.partial(
                section_kernel, cells_z, TIME_STEP * SECTION_WEIGHTS[k], last
            ),
            out_shape=(field_like, jax.ShapeDtypeStruct((8, cells_z), F32), slots_like),
            in_specs=[smem] + whole_in_vmem(14),
            out_specs=tuple(whole_in_vmem(3)),
            scratch_shapes=[
                pltpu.VMEM((4 * (u.shape[0] + 8), cells_z), BF16),
                pltpu.VMEM((2 * u.shape[0], cells_z), F32),
            ],
            compiler_params=params(),
            name="section",
        )(
            info, u, xp, xm, yp, ym, corner, cell, particle_offset, tau, v, near, metric,
            matrix[k], scal[k : k + 1],
        )
        if last:
            from_x = lax.ppermute(v[:, RESIDENT : RESIDENT + CAP], "gx", ring_x)
            from_above = lax.ppermute(v[:, RESIDENT + CAP : RESIDENT + 2 * CAP], "gy", back_y)
            from_below = lax.ppermute(v[:, RESIDENT + 2 * CAP :], "gy", ring_y)
        gathered = lax.all_gather(pq, "gy", axis=0)
        joined = pl.pallas_call(
            functools.partial(join_kernel, last),
            out_shape=(field_like,) + (() if last else (edge_like, edge_like)),
            in_specs=[smem] + whole_in_vmem(4),
            out_specs=tuple(whole_in_vmem(1 if last else 3)),
            compiler_params=params(),
            name="join",
        )(info, gathered, w, enter[k], leave[k])
        u = joined[0]
        if not last:
            yp, ym = joined[1:]
            xp = lax.ppermute(u, "gx", back_x)
            xm = lax.ppermute(u, "gx", ring_x)
            corner = lax.ppermute(yp, "gx", back_x)
    moved = jnp.concatenate([v[:, :RESIDENT], from_x, from_above, from_below], axis=1)
    return (u.reshape(velocity.shape), moved)


def solution(mesh):
    return jax.shard_map(
        on_device,
        mesh=mesh,
        in_specs=(
            P(None, "gx", "gy", None),
            P("gy"),
            P(None, "gy"),
            P(None, "gy"),
            P(None, "gy"),
            P(None, ("gx", "gy")),
            P(("gx", "gy")),
            P(None, ("gx", "gy")),
            P(("gx", "gy")),
            P("gx", "gy", None),
        ),
        out_specs=(P(None, "gx", "gy", None), P(None, ("gx", "gy"))),
        check_vma=False,
    )
```

time: 819 us -> 103 us (0.13)
  local copies, waits for them, and re-layouts: 512 us -> 6.3 us
  other arithmetic: 175 us -> 1.63 us
  blocking collectives: 66.6 us -> 26.9 us
  Pallas kernels: 0 us -> 33.3 us
  waiting for transfers between devices: 27.9 us -> 10.4 us
    gather x48 -> x0, local copies, waits for them, and re-layouts: 428 us -> none  [on_device(): flat_ext[:, lookup]]
    mul x12 -> x4, other arithmetic: 85.6 us -> 0.09 us  [the longest x1 0.08 us: block_tables(): pivot_inv[:, :, None] * lower]
    scatter-add x3 -> x0, other arithmetic: 70.4 us -> none  [on_device(): force = jnp.zeros((comps, cells_x * cells_y * cells_z), jnp.float32).at[:...]
    concatenate x3 -> x1, local copies, waits for them, and re-layouts: 40.6 us -> 0.07 us  [block_tables(): jnp.concatenate([body, tail, jnp.zeros((SECTIONS, 8 - COMPS, COMPS * rows...]
    pallas_call x0 -> x9, Pallas kernels: none -> 33.3 us  [the longest x3 21.2 us: on_device(): pl.pallas_call(functools.partial(section_kernel, cells_z, TIME_STEP * SEC...]
    all_gather x6 -> x3, blocking collectives: 53.2 us -> 26.9 us  [on_device(): gathered = lax.all_gather(pq, 'gy', axis=0)]
    ppermute x15 -> x14, waiting for transfers between devices: 27.9 us -> 10.4 us  [the longest x2 10.3 us: on_device(): corner = lax.ppermute(yp, 'gx', back_x)]
    reshape x4 -> x3, local copies, waits for them, and re-layouts: 16 us -> 0.1 us  [the longest x1 0.08 us: on_device(): metric = y_metric.reshape(cells_y, 1)]
  transfers between devices with their start and end apart: 15 -> 14, of which waited for: 8 -> 2; matrix products, arithmetic and copies ran while one was open for 5% -> 2% of each run, Pallas kernels for 0% -> 10%
where the time goes in v1:
time: 103 us
  Pallas kernels  33.3 us (32%)
  blocking collectives  26.9 us (26%)
  starting transfers between devices  23.3 us (23%)
  waiting for transfers between devices  10.4 us (10%)
  local copies, waits for them, and re-layouts  6.3 us (6%)
  other arithmetic  1.63 us (2%)
    all_gather x3, blocking collectives, on_device(): gathered = lax.all_gather(pq, 'gy', axis=0)  26.9 us
    pallas_call x3, Pallas kernels, on_device(): pl.pallas_call(functools.partial(section_kernel, cells_z, TIME_STEP * SEC...  21.2 us
    ppermute x3, starting transfers between devices, on_device(): xp = lax.ppermute(u, 'gx', back_x)  11.4 us
    ppermute x2, waiting for transfers between devices, on_device(): corner = lax.ppermute(yp, 'gx', back_x)  10.3 us
    pallas_call x3, Pallas kernels, on_device(): pl.pallas_call(functools.partial(own_plane_kernel, cells_z), out_shape=sl...  9.23 us
    ppermute x1, starting transfers between devices, on_device(): corner = lax.ppermute(first, ('gx', 'gy'), diagonal)  6.42 us
    unnamed x24, local copies, waits for them, and re-layouts  3.8 us
    pallas_call x3, Pallas kernels, on_device(): pl.pallas_call(functools.partial(join_kernel, last), out_shape=(field_lik...  2.87 us
  transfers between devices with their start and end apart: 14, of which 2 were waited for; matrix products, arithmetic and copies ran while one was open for 2% of the time, Pallas kernels for 10%

profile of v1, /device:TPU:0, one launch (start us, length us, event | category | flops | bytes accessed | tf_op | source)
XLA Modules:
  0.0 102.8 jit_solution(15248957543609056086)
XLA Ops:
  0.6 1.0 fusion.3
  1.6 6.4 %collective-permute-start.4 = (f32[3,1024]{1,0:T(4,128)S(1)}, f32[3,1024]{1,0:T(4,128)S(1)}, u32[]{:S(2)}, u32[]{:S(2)}) collective-permute-start(f32[3,1024]{1,0:T(4,128)S(1)} %bitcast.53), channel_id=1, source_target_pairs={{9,0},{10,1},{11,2},{12,3},{13,4},{14,5},{15,6},{8,7},{17,8},{18,9... | collective-permute-start | bytes 36872 | tf_op jit(solution)/shard_map/ppermute | solution.py:305
  8.0 0.8 collective-permute-start.2
  8.9 3.8 %collective-permute-start = (f32[48,1024]{1,0:T(8,128)}, f32[48,1024]{1,0:T(8,128)S(1)}, u32[]{:S(2)}, u32[]{:S(2)}) collective-permute-start(f32[48,1024]{1,0:T(8,128)} %bitcast.48), channel_id=1, source_target_pairs={{8,0},{16,8},{24,16},{0,24},{9,1},{17,9},{25,17},{1,25},{10,2},{18... | collective-permute-start | bytes 589832 | tf_op jit(solution)/shard_map/ppermute | solution.py:301
  12.8 0.7 copy-done.5
  13.7 0.6 copy-done.7
  14.6 0.7 copy-done.6
  15.7 0.2 multiply_reduce_fusion
  16.3 0.6 copy-done.3
  17.3 0.2 mul.102
  17.6 0.8 copy-done.1
  18.5 3.1 %own_plane.3.near_ref = f32[3,3584]{1,0:T(4,128)S(1)} custom-call(f32[48,1024]{1,0:T(8,128)S(1)} %bitcast.49, s32[1,3584]{1,0:T(1,128)S(1)} %reshape.165.cell_ref, f32[3,3584]{1,0:T(4,128)S(1)} %copy-done), custom_call_target="tpu_custom_call" | custom-call | flops 1409286144 | bytes 262144 | tf_op jit(solution)/shard_map/own_plane/pallas_call | solution.py:319
  21.9 0.5 copy-done.2
  22.4 7.1 %section.3 = (f32[48,1024]{1,0:T(8,128)S(1)}, f32[8,1024]{1,0:T(8,128)S(1)}, f32[3,3584]{1,0:T(4,128)S(1)}) custom-call(s32[5]{0:T(128)S(1)} %pad_add_fusion.info_ref, f32[48,1024]{1,0:T(8,128)S(1)} %bitcast.50, f32[48,1024]{1,0:T(8,128)S(1)} %collective-permute-done.xp_ref, f32[48,1024]{1,0:T(8,128)S(1)} %collective-permute-done.1.xm_ref, ...), custom_call_target="tpu_custom_call" | custom-call | tf_op jit(solution)/shard_map/section/pallas_call | solution.py:331
  29.5 9.3 %all-gather = f32[64,1024]{1,0:T(8,128)S(1)} all-gather(f32[8,1024]{1,0:T(8,128)S(1)} %get-tuple-element.17), channel_id=2, replica_groups=mesh['gx'=4,'gy'=8] {'gy'}, dimensions={0}, use_global_device_ids=true | all-gather | bytes 294912 | tf_op jit(solution)/shard_map/all_gather | solution.py:352
  38.8 0.7 join.3
  39.6 3.8 %collective-permute-start.5 = (f32[48,1024]{1,0:T(8,128)S(1)}, f32[48,1024]{1,0:T(8,128)S(1)}, u32[]{:S(2)}, u32[]{:S(2)}) collective-permute-start(f32[48,1024]{1,0:T(8,128)S(1)} %get-tuple-element.19.u_ref), channel_id=1, source_target_pairs={{8,0},{16,8},{24,16},{0,24},{9,1},{17,9},{25,17},{1,25},{10,2},{18... | collective-permute-start | bytes 589832 | tf_op jit(solution)/shard_map/ppermute | solution.py:364
  43.4 3.1 %own_plane.4.near_ref = f32[3,3584]{1,0:T(4,128)S(1)} custom-call(f32[48,1024]{1,0:T(8,128)S(1)} %get-tuple-element.19.u_ref, s32[1,3584]{1,0:T(1,128)S(1)} %reshape.165.cell_ref, f32[3,3584]{1,0:T(4,128)S(1)} %copy-done), custom_call_target="tpu_custom_call" | custom-call | flops 1409286144 | bytes 262144 | tf_op jit(solution)/shard_map/own_plane/pallas_call | solution.py:319
  46.5 4.8 %collective-permute-done.7.corner_ref = f32[3,1024]{1,0:T(4,128)S(1)} collective-permute-done((f32[3,1024]{1,0:T(4,128)S(1)}, f32[3,1024]{1,0:T(4,128)S(1)}, u32[]{:S(2)}, u32[]{:S(2)}) %collective-permute-start.7) | collective-permute-done | bytes 12320 | tf_op jit(solution)/shard_map/ppermute | solution.py:366
  51.4 7.1 %section.4 = (f32[48,1024]{1,0:T(8,128)S(1)}, f32[8,1024]{1,0:T(8,128)S(1)}, f32[3,3584]{1,0:T(4,128)S(1)}) custom-call(s32[5]{0:T(128)S(1)} %pad_add_fusion.info_ref, f32[48,1024]{1,0:T(8,128)S(1)} %get-tuple-element.19.u_ref, f32[48,1024]{1,0:T(8,128)S(1)} %collective-permute-done.5.xp_ref, f32[48,1024]{1,0:T(8,128)S(1)} %collective-permute-done.6.xm_ref, ...), custom_call_target="tpu_custom_call" | custom-call | tf_op jit(solution)/shard_map/section/pallas_call | solution.py:331
  58.5 8.4 %all-gather.1 = f32[64,1024]{1,0:T(8,128)S(1)} all-gather(f32[8,1024]{1,0:T(8,128)S(1)} %get-tuple-element.23), channel_id=3, replica_groups=mesh['gx'=4,'gy'=8] {'gy'}, dimensions={0}, use_global_device_ids=true | all-gather | bytes 294912 | tf_op jit(solution)/shard_map/all_gather | solution.py:352
  66.8 0.7 join.4
  67.6 3.8 %collective-permute-start.8 = (f32[48,1024]{1,0:T(8,128)S(1)}, f32[48,1024]{1,0:T(8,128)S(1)}, u32[]{:S(2)}, u32[]{:S(2)}) collective-permute-start(f32[48,1024]{1,0:T(8,128)S(1)} %get-tuple-element.25.u_ref), channel_id=1, source_target_pairs={{8,0},{16,8},{24,16},{0,24},{9,1},{17,9},{25,17},{1,25},{10,2},{18... | collective-permute-start | bytes 589832 | tf_op jit(solution)/shard_map/ppermute | solution.py:364
  71.5 0.2 collective-permute-start.10
  71.7 3.1 %own_plane.5.near_ref = f32[3,3584]{1,0:T(4,128)S(1)} custom-call(f32[48,1024]{1,0:T(8,128)S(1)} %get-tuple-element.25.u_ref, s32[1,3584]{1,0:T(1,128)S(1)} %reshape.165.cell_ref, f32[3,3584]{1,0:T(4,128)S(1)} %copy-done), custom_call_target="tpu_custom_call" | custom-call | flops 1409286144 | bytes 262144 | tf_op jit(solution)/shard_map/own_plane/pallas_call | solution.py:319
  74.8 5.5 %collective-permute-done.10.corner_ref = f32[3,1024]{1,0:T(4,128)S(1)} collective-permute-done((f32[3,1024]{1,0:T(4,128)S(1)}, f32[3,1024]{1,0:T(4,128)S(1)}, u32[]{:S(2)}, u32[]{:S(2)}) %collective-permute-start.10) | collective-permute-done | bytes 12320 | tf_op jit(solution)/shard_map/ppermute | solution.py:366
  80.2 7.1 %section.5 = (f32[48,1024]{1,0:T(8,128)S(1)}, f32[8,1024]{1,0:T(8,128)S(1)}, f32[3,3584]{1,0:T(4,128)S(1)}) custom-call(s32[5]{0:T(128)S(1)} %pad_add_fusion.info_ref, f32[48,1024]{1,0:T(8,128)S(1)} %get-tuple-element.25.u_ref, f32[48,1024]{1,0:T(8,128)S(1)} %collective-permute-done.8.xp_ref, f32[48,1024]{1,0:T(8,128)S(1)} %collective-permute-done.9.xm_ref, ...), custom_call_target="tpu_custom_call" | custom-call | tf_op jit(solution)/shard_map/section/pallas_call | solution.py:331
  87.3 1.6 %collective-permute-start.11 = (f32[3,512]{1,0:T(4,128)S(1)}, f32[3,512]{1,0:T(4,128)S(1)}, u32[]{:S(2)}, u32[]{:S(2)}) collective-permute-start(f32[3,512]{1,0:T(4,128)S(1)} %get-tuple-element.47), channel_id=1, source_target_pairs={{0,8},{8,16},{16,24},{24,0},{1,9},{9,17},{17,25},{25,1},{2,10},{10... | collective-permute-start | bytes 18440 | tf_op jit(solution)/shard_map/ppermute | solution.py:349
  88.9 2.6 %collective-permute-start.12 = (f32[3,512]{1,0:T(4,128)S(1)}, f32[3,512]{1,0:T(4,128)S(1)}, u32[]{:S(2)}, u32[]{:S(2)}) collective-permute-start(f32[3,512]{1,0:T(4,128)S(1)} %get-tuple-element.49), channel_id=1, source_target_pairs={{1,0},{2,1},{3,2},{4,3},{5,4},{6,5},{7,6},{0,7},{9,8},{10,9},{11,1... | collective-permute-start | bytes 18440 | tf_op jit(solution)/shard_map/ppermute | solution.py:350
  91.5 9.2 %all-gather.2 = f32[64,1024]{1,0:T(8,128)S(1)} all-gather(f32[8,1024]{1,0:T(8,128)S(1)} %get-tuple-element.29), channel_id=4, replica_groups=mesh['gx'=4,'gy'=8] {'gy'}, dimensions={0}, use_global_device_ids=true | all-gather | bytes 294912 | tf_op jit(solution)/shard_map/all_gather | solution.py:352
  100.8 1.4 %join.5 = f32[48,1024]{1,0:T(8,128)} custom-call(s32[5]{0:T(128)S(1)} %pad_add_fusion.info_ref, f32[8,8,1024]{2,1,0:T(8,128)S(1)} %bitcast.44, f32[48,1024]{1,0:T(8,128)S(1)} %get-tuple-element.30.w_ref, f32[16,1]{1,0:T(8,128)S(1)} %get-tuple-element.61.enter_ref, f32[16,1]{1,0:T(8,128)S(1)} %get-tuple-element.50.leave_ref), custom_call_target="tpu_custom_call" | custom-call | tf_op jit(solution)/shard_map/join/pallas_call | solution.py:353
  102.2 0.6 pad_maximum_fusion
  (79 shorter events, 2.4 us)
Async XLA Ops:
  1.6 20.3 %collective-permute-start.4 = (f32[3,1024]{1,0:T(4,128)S(1)}, f32[3,1024]{1,0:T(4,128)S(1)}, u32[]{:S(2)}, u32[]{:S(2)}) collective-permute-start(f32[3,1024]{1,0:T(4,128)S(1)} %bitcast.53), channel_id=1, source_target_pairs={{9,0},{10,1},{11,2},{12,3},{13,4},{14,5},{15,6},{8,7},{17,8},{18,9... | collective-permute-start | bytes 36872 | tf_op jit(solution)/shard_map/ppermute | solution.py:305
  8.0 13.8 %collective-permute-start.2 = (f32[3,1024]{1,0:T(4,128)S(1)}, f32[3,1024]{1,0:T(4,128)S(1)}, u32[]{:S(2)}, u32[]{:S(2)}) collective-permute-start(f32[3,1024]{1,0:T(4,128)S(1)} %bitcast.54), channel_id=1, source_target_pairs={{1,0},{2,1},{3,2},{4,3},{5,4},{6,5},{7,6},{0,7},{9,8},{10,9},{11,1... | collective-permute-start | bytes 36872 | tf_op jit(solution)/shard_map/ppermute | solution.py:303
  8.9 13.0 %collective-permute-start.1 = (f32[48,1024]{1,0:T(8,128)}, f32[48,1024]{1,0:T(8,128)S(1)}, u32[]{:S(2)}, u32[]{:S(2)}) collective-permute-start(f32[48,1024]{1,0:T(8,128)} %bitcast.47), channel_id=1, source_target_pairs={{0,8},{8,16},{16,24},{24,0},{1,9},{9,17},{17,25},{25,1},{2,10},{10... | collective-permute-start | bytes 589832 | tf_op jit(solution)/shard_map/ppermute | solution.py:302
  8.9 13.0 %collective-permute-start = (f32[48,1024]{1,0:T(8,128)}, f32[48,1024]{1,0:T(8,128)S(1)}, u32[]{:S(2)}, u32[]{:S(2)}) collective-permute-start(f32[48,1024]{1,0:T(8,128)} %bitcast.48), channel_id=1, source_target_pairs={{8,0},{16,8},{24,16},{0,24},{9,1},{17,9},{25,17},{1,25},{10,2},{18... | collective-permute-start | bytes 589832 | tf_op jit(solution)/shard_map/ppermute | solution.py:301
  12.7 9.2 %collective-permute-start.3 = (f32[3,1024]{1,0:T(4,128)S(1)}, f32[3,1024]{1,0:T(4,128)S(1)}, u32[]{:S(2)}, u32[]{:S(2)}) collective-permute-start(f32[3,1024]{1,0:T(4,128)S(1)} %bitcast.55), channel_id=1, source_target_pairs={{0,1},{1,2},{2,3},{3,4},{4,5},{5,6},{6,7},{7,0},{8,9},{9,10},{10,1... | collective-permute-start | bytes 36872 | tf_op jit(solution)/shard_map/ppermute | solution.py:304
  12.8 0.7 copy-start.5
  13.6 0.7 copy-start.7
  14.5 0.7 copy-start.6
  16.2 0.7 copy-start.3
  17.5 0.9 copy-start.1
  17.6 0.8 copy-start
  18.5 3.2 %copy-start.9 = (s32[1,1,3]{2,1,0:T(1,128)S(1)}, s32[1,1,3]{2,1,0:T(1,128)}, u32[]{:S(2)}) copy-start(s32[1,1,3]{2,1,0:T(1,128)} %param.19) | copy-start | bytes 40
  18.5 3.3 %copy-start.8 = (f32[16]{0:T(128)S(1)}, f32[16]{0:T(128)}, u32[]{:S(2)}) copy-start(f32[16]{0:T(128)} %param.11) | copy-start | bytes 196
  18.5 3.4 %copy-start.4 = (f32[3584]{0:T(1024)S(1)}, f32[3584]{0:T(1024)}, u32[]{:S(2)}) copy-start(f32[3584]{0:T(1024)} %param.18) | copy-start | bytes 43012
  21.5 0.8 copy-start.2
  39.5 11.8 %collective-permute-start.6 = (f32[48,1024]{1,0:T(8,128)S(1)}, f32[48,1024]{1,0:T(8,128)S(1)}, u32[]{:S(2)}, u32[]{:S(2)}) collective-permute-start(f32[48,1024]{1,0:T(8,128)S(1)} %get-tuple-element.19.u_ref), channel_id=1, source_target_pairs={{0,8},{8,16},{16,24},{24,0},{1,9},{9,17},{17,25},{25,1},{2,10},{10... | collective-permute-start | bytes 589832 | tf_op jit(solution)/shard_map/ppermute | solution.py:365
  39.6 11.8 %collective-permute-start.5 = (f32[48,1024]{1,0:T(8,128)S(1)}, f32[48,1024]{1,0:T(8,128)S(1)}, u32[]{:S(2)}, u32[]{:S(2)}) collective-permute-start(f32[48,1024]{1,0:T(8,128)S(1)} %get-tuple-element.19.u_ref), channel_id=1, source_target_pairs={{8,0},{16,8},{24,16},{0,24},{9,1},{17,9},{25,17},{1,25},{10,2},{18... | collective-permute-start | bytes 589832 | tf_op jit(solution)/shard_map/ppermute | solution.py:364
  43.4 8.0 %collective-permute-start.7 = (f32[3,1024]{1,0:T(4,128)S(1)}, f32[3,1024]{1,0:T(4,128)S(1)}, u32[]{:S(2)}, u32[]{:S(2)}) collective-permute-start(f32[3,1024]{1,0:T(4,128)S(1)} %get-tuple-element.20.yp_ref), channel_id=1, source_target_pairs={{8,0},{16,8},{24,16},{0,24},{9,1},{17,9},{25,17},{1,25},{10,2},{18... | collective-permute-start | bytes 36872 | tf_op jit(solution)/shard_map/ppermute | solution.py:366
  67.6 12.7 %collective-permute-start.9 = (f32[48,1024]{1,0:T(8,128)S(1)}, f32[48,1024]{1,0:T(8,128)S(1)}, u32[]{:S(2)}, u32[]{:S(2)}) collective-permute-start(f32[48,1024]{1,0:T(8,128)S(1)} %get-tuple-element.25.u_ref), channel_id=1, source_target_pairs={{0,8},{8,16},{16,24},{24,0},{1,9},{9,17},{17,25},{25,1},{2,10},{10... | collective-permute-start | bytes 589832 | tf_op jit(solution)/shard_map/ppermute | solution.py:365
  67.6 12.6 %collective-permute-start.8 = (f32[48,1024]{1,0:T(8,128)S(1)}, f32[48,1024]{1,0:T(8,128)S(1)}, u32[]{:S(2)}, u32[]{:S(2)}) collective-permute-start(f32[48,1024]{1,0:T(8,128)S(1)} %get-tuple-element.25.u_ref), channel_id=1, source_target_pairs={{8,0},{16,8},{24,16},{0,24},{9,1},{17,9},{25,17},{1,25},{10,2},{18... | collective-permute-start | bytes 589832 | tf_op jit(solution)/shard_map/ppermute | solution.py:364
  71.5 8.8 %collective-permute-start.10 = (f32[3,1024]{1,0:T(4,128)S(1)}, f32[3,1024]{1,0:T(4,128)S(1)}, u32[]{:S(2)}, u32[]{:S(2)}) collective-permute-start(f32[3,1024]{1,0:T(4,128)S(1)} %get-tuple-element.26.yp_ref), channel_id=1, source_target_pairs={{8,0},{16,8},{24,16},{0,24},{9,1},{17,9},{25,17},{1,25},{10,2},{18... | collective-permute-start | bytes 36872 | tf_op jit(solution)/shard_map/ppermute | solution.py:366
  87.3 14.8 %collective-permute-start.11 = (f32[3,512]{1,0:T(4,128)S(1)}, f32[3,512]{1,0:T(4,128)S(1)}, u32[]{:S(2)}, u32[]{:S(2)}) collective-permute-start(f32[3,512]{1,0:T(4,128)S(1)} %get-tuple-element.47), channel_id=1, source_target_pairs={{0,8},{8,16},{16,24},{24,0},{1,9},{9,17},{17,25},{25,1},{2,10},{10... | collective-permute-start | bytes 18440 | tf_op jit(solution)/shard_map/ppermute | solution.py:349
  88.9 13.3 %collective-permute-start.13 = (f32[3,512]{1,0:T(4,128)S(1)}, f32[3,512]{1,0:T(4,128)S(1)}, u32[]{:S(2)}, u32[]{:S(2)}) collective-permute-start(f32[3,512]{1,0:T(4,128)S(1)} %get-tuple-element.48), channel_id=1, source_target_pairs={{0,1},{1,2},{2,3},{3,4},{4,5},{5,6},{6,7},{7,0},{8,9},{9,10},{10,1... | collective-permute-start | bytes 18440 | tf_op jit(solution)/shard_map/ppermute | solution.py:351
  88.9 13.3 %collective-permute-start.12 = (f32[3,512]{1,0:T(4,128)S(1)}, f32[3,512]{1,0:T(4,128)S(1)}, u32[]{:S(2)}, u32[]{:S(2)}) collective-permute-start(f32[3,512]{1,0:T(4,128)S(1)} %get-tuple-element.49), channel_id=1, source_target_pairs={{1,0},{2,1},{3,2},{4,3},{5,4},{6,5},{7,6},{0,7},{9,8},{10,9},{11,1... | collective-permute-start | bytes 18440 | tf_op jit(solution)/shard_map/ppermute | solution.py:350

commit v2 on v1

v2 whole, which is shorter than its diff:
```python
import functools

import jax
import jax.numpy as jnp
from jax import lax
from jax.experimental import pallas as pl
from jax.experimental.pallas import tpu as pltpu
from jax.sharding import PartitionSpec as P

RESIDENT = 2048
CAP = 512
SECTIONS = 3

SECTION_WEIGHTS = (8.0 / 15.0, 5.0 / 12.0, 3.0 / 4.0)
TIME_STEP = 0.3
STREAM_SCALE = 2.0
SPAN_SCALE = 2.0
COUPLING = 0.5
COMPS = 3
TILE = 512
DEPTH = 256
VMEM_LIMIT = 32 * 1024 * 1024
ENTER, LEAVE, PIVOT, UPWARD, METRIC = range(16, 21)

F32 = jnp.float32
BF16 = jnp.bfloat16


def call(kernel, out_shape, in_specs, name, scratch_shapes=()):
    several = isinstance(out_shape, tuple)
    out_specs = whole_in_vmem(len(out_shape)) if several else whole_in_vmem(1)[0]
    return pl.pallas_call(
        kernel,
        out_shape=out_shape,
        in_specs=in_specs,
        out_specs=tuple(out_specs) if several else out_specs,
        scratch_shapes=scratch_shapes,
        compiler_params=pltpu.CompilerParams(vmem_limit_bytes=VMEM_LIMIT),
        name=name,
    )


def whole_in_vmem(count):
    return [pl.BlockSpec(memory_space=pltpu.VMEM)] * count


def scalars(count):
    return [pl.BlockSpec(memory_space=pltpu.SMEM)] * count


def across(row, depth):
    width = row.shape[1]
    shape = (DEPTH // 16, 16, width)
    order = lax.broadcasted_iota(jnp.int32, shape, 0) * 16 + lax.broadcasted_iota(jnp.int32, shape, 1)
    order = order.astype(F32).astype(BF16)
    one, none = jnp.ones((), BF16), jnp.zeros((), BF16)
    parts = []
    for k in range(depth // DEPTH):
        wanted = jnp.broadcast_to(row - float(DEPTH * k), (16, width)).astype(BF16)
        parts.append(jnp.where(order == wanted[None], one, none).reshape(DEPTH, width))
    return jnp.concatenate(parts, axis=0)


def down(row, depth):
    width = row.shape[1]
    order = lax.broadcasted_iota(jnp.int32, (width, DEPTH), 1).astype(F32).astype(BF16)
    one, none = jnp.ones((), BF16), jnp.zeros((), BF16)
    column = jnp.broadcast_to(row, (8, width)).T[:, 0:1]
    parts = []
    for k in range(depth // DEPTH):
        wanted = jnp.broadcast_to(column - float(DEPTH * k), (width, DEPTH)).astype(BF16)
        parts.append(jnp.where(order == wanted, one, none))
    return jnp.concatenate(parts, axis=1)


def split_rows(rows):
    length = rows.shape[1]
    high = rows.astype(BF16).astype(F32)
    low = rows - high
    ahead = [pltpu.roll(part, length - 1, 1) for part in (high, low)]
    return jnp.concatenate([high, low] + ahead, axis=0).astype(BF16)


def blend_z(values, fz):
    rows = values.shape[0] // 4
    near = values[:rows] + values[rows : 2 * rows]
    far = values[2 * rows : 3 * rows] + values[3 * rows :]
    return near * (1.0 - fz) + far * fz


def tables_kernel(down_ref, up_ref, scale_ref, metric_ref, matrix_ref, answer_ref, scal_ref):
    sections, rows = down_ref.shape
    lane = lax.broadcasted_iota(jnp.int32, (1, 128), 1)
    at = lambda place: jnp.where(lane == place, 1.0, 0.0)
    matrix_ref[...] = jnp.zeros_like(matrix_ref)
    scal_ref[...] = jnp.zeros_like(scal_ref)
    for k in range(sections):
        lower = []
        row = at(ENTER)
        for i in range(rows):
            row = down_ref[k, i] * row + at(i)
            lower.append(row)
        last = jnp.where(lane < rows, row, 0.0)
        for c in range(COMPS):
            place = COMPS * rows + c
            matrix_ref[k, place : place + 1, :] = pltpu.roll(last, rows * c, 1)
        scal_ref[k, 0:1, :] = row
        row = at(LEAVE)
        for i in reversed(range(rows)):
            row = scale_ref[k, i] * lower[i] + up_ref[k, i] * row
            inner = jnp.where(lane < rows, row, 0.0)
            for c in range(COMPS):
                place = rows * c + i
                matrix_ref[k, place : place + 1, :] = inner if c == 0 else pltpu.roll(inner, rows * c, 1)
            answer_ref[k, i : i + 1, :] = row + metric_ref[i] * at(METRIC)
        scal_ref[k, 1:2, :] = (
            row + scale_ref[k, rows - 1] * at(PIVOT) + up_ref[k, rows - 1] * at(UPWARD)
        )


def own_plane_kernel(u_ref, cell_ref, off_ref, out_ref, table_ref):
    cells_z = u_ref.shape[1]
    rows = u_ref.shape[0] // COMPS
    table_ref[...] = split_rows(u_ref[...])
    order = lax.broadcasted_iota(jnp.int32, (rows, TILE), 0)
    for t in range(cell_ref.shape[1] // TILE):
        here = slice(t * TILE, (t + 1) * TILE)
        cell = cell_ref[:, here]
        row = cell // cells_z
        fx, fy, fz = (off_ref[d : d + 1, here] for d in range(3))
        chosen = across((cell % cells_z).astype(F32), cells_z)
        blended = blend_z(jnp.dot(table_ref[...], chosen, preferred_element_type=F32), fz)
        weight = jnp.where(order == row, 1.0 - fy, jnp.where(order == row + 1, fy, 0.0))
        weight = weight * (1.0 - fx)
        for c in range(COMPS):
            part = blended[rows * c : rows * (c + 1)] * weight
            out_ref[c : c + 1, here] = jnp.sum(part, axis=0, keepdims=True)


def section_kernel(number, step, last, *refs):
    first = number == 0
    refs = list(refs)
    take = lambda count: [refs.pop(0) for _ in range(count)]
    count_ref, u_ref, ym_ref, xp_ref, xm_ref, yp_ref, ahead_ref = take(7)
    behind_ref = None if first else refs.pop(0)
    cell_ref, off_ref, tau_ref, v_ref, near_ref, matrix_ref, answer_ref, scal_ref = take(8)
    w_ref, pq_ref, v_out_ref = take(3)
    leaving_ref = refs.pop(0) if last else None
    table_ref, spread_ref, chosen_ref = refs

    cells_z = u_ref.shape[1]
    rows = u_ref.shape[0] // COMPS
    count = COMPS * rows
    position = lax.axis_index("gy")
    top = jnp.where(position == lax.axis_size("gy") - 1, 0.0, 1.0).astype(F32)
    bottom = jnp.where(position == 0, 0.0, 1.0).astype(F32)
    y_minus = ym_ref[...] * bottom
    x_plus, x_minus = xp_ref[...], xm_ref[...]
    if first:
        y_plus = yp_ref[...] * top
        corner = ahead_ref[...] * top
    else:
        y_plus = yp_ref[COMPS : 2 * COMPS, :]
        corner = ahead_ref[COMPS : 2 * COMPS, :]
        enter = answer_ref[number - 1, :, ENTER : ENTER + 1]
        leave = answer_ref[number - 1, :, LEAVE : LEAVE + 1]

        def joined(plane, ref):
            return jnp.concatenate(
                [
                    plane[rows * c : rows * (c + 1)]
                    + enter * ref[c : c + 1, :]
                    + leave * ref[COMPS + c : COMPS + c + 1, :]
                    for c in range(COMPS)
                ],
                axis=0,
            )

        x_plus, x_minus = joined(x_plus, ahead_ref), joined(x_minus, behind_ref)
    pad = jnp.zeros((2, cells_z), F32)
    table_ref[...] = split_rows(jnp.concatenate([x_plus, y_plus, corner, pad], axis=0))
    order = lax.broadcasted_iota(jnp.int32, (rows, TILE), 0)
    for t in range(cell_ref.shape[1] // TILE):
        here = slice(t * TILE, (t + 1) * TILE)
        cell = cell_ref[:, here]
        row, column = cell // cells_z, (cell % cells_z).astype(F32)
        fx, fy, fz = (off_ref[d : d + 1, here] for d in range(3))
        found = jnp.dot(table_ref[...], across(column, cells_z), preferred_element_type=F32)
        chosen_ref[here, :] = down(column, cells_z)
        blended = blend_z(found, fz)
        at_row = order == row
        weight = jnp.where(at_row, 1.0 - fy, jnp.where(order == row + 1, fy, 0.0)) * fx
        edge = jnp.where(row == rows - 1, fy, 0.0)
        slot = t * TILE + lax.broadcasted_iota(jnp.int32, (1, TILE), 1)
        remain = slot - RESIDENT
        heading = remain // CAP
        limit = jnp.where(
            heading <= 0,
            count_ref[0, 0, 0],
            jnp.where(heading == 1, count_ref[0, 0, 1], count_ref[0, 0, 2]),
        )
        live = jnp.where((remain < 0) | (remain % CAP < limit), 1.0, 0.0)
        tau = tau_ref[:, here]
        spread = []
        for c in range(COMPS):
            part = jnp.sum(blended[rows * c : rows * (c + 1)] * weight, axis=0, keepdims=True)
            side = blended[count + c : count + c + 1] * (1.0 - fx)
            side = side + blended[count + COMPS + c : count + COMPS + c + 1] * fx
            fluid = near_ref[c : c + 1, here] + part + side * edge
            v = v_ref[c : c + 1, here]
            drag = tau * (fluid - v)
            v = v + step * drag
            v_out_ref[c : c + 1, here] = v * live if last else v
            spread.append(jnp.where(at_row, drag * live * (-COUPLING), 0.0))
        spread = jnp.concatenate(spread, axis=0)
        high = spread.astype(BF16).astype(F32)
        spread_ref[:, here] = jnp.concatenate([high, spread - high], axis=0).astype(BF16)
    pushed = jnp.dot(spread_ref[...], chosen_ref[...], preferred_element_type=F32)

    u = u_ref[...]
    slope_x = (x_plus - x_minus) * (0.5 * STREAM_SCALE)
    slope_z = (pltpu.roll(u, cells_z - 1, 1) - pltpu.roll(u, 1, 1)) * (0.5 * SPAN_SCALE)
    metric = 0.5 * answer_ref[number, :, METRIC : METRIC + 1]
    rhs = []
    for c in range(COMPS):
        own = slice(rows * c, rows * (c + 1))
        field = u[own]
        upper = jnp.concatenate([field[1:], y_plus[c : c + 1]], axis=0)
        lower = jnp.concatenate([y_minus[c : c + 1], field[:-1]], axis=0)
        slope_y = (upper - lower) * metric
        convection = -(
            u[:rows] * slope_x[own] + u[rows : 2 * rows] * slope_y + u[2 * rows :] * slope_z[own]
        )
        force = pushed[own] + pushed[count + rows * c : count + rows * (c + 1)]
        rhs.append(field + step * (convection + force))
    solved = jnp.dot(
        matrix_ref[number, :, 0:count],
        jnp.concatenate(rhs, axis=0),
        precision=lax.Precision.HIGHEST,
        preferred_element_type=F32,
    )
    w_ref[...] = solved[:count]
    pq_ref[0:COMPS, :] = solved[count : count + COMPS]
    for c in range(COMPS):
        pq_ref[COMPS + c : COMPS + c + 1, :] = solved[rows * c : rows * c + 1]
    pq_ref[6:8, :] = jnp.zeros((2, cells_z), F32)
    pq_ref[6:8, 0:128] = scal_ref[number]
    if last:
        leaving_ref[...] = v_out_ref[:, RESIDENT : RESIDENT + CAP]
        pq_ref[8 : 8 + COMPS, :] = v_out_ref[:, RESIDENT + CAP : RESIDENT + 3 * CAP]
        pq_ref[8 + COMPS :, :] = jnp.zeros((8 - COMPS, cells_z), F32)


def join_kernel(number, last, blocks, direct, *refs):
    refs = list(refs)
    take = lambda count: [refs.pop(0) for _ in range(count)]
    here = lax.axis_index("gy")
    if direct:
        sources = take(5)
    else:
        (all_ref,) = take(1)
    w_ref, answer_ref = take(2)
    if last:
        v_ref, from_x_ref, u_ref, moved_ref = take(4)
    else:
        u_ref, ef_ref, ym_ref = take(3)
    if direct:
        (all_ref,) = refs
        own_ref, partner_ref, side_ref, other_ref, far_ref = sources
        odd = here % 2 == 1
        all_ref[here] = own_ref[...]
        all_ref[here ^ 1] = partner_ref[...]
        near = here ^ jnp.where(odd, 4, 2)
        all_ref[near] = side_ref[0]
        all_ref[near ^ 1] = side_ref[1]
        near = here ^ jnp.where(odd, 2, 4)
        all_ref[near ^ 1] = other_ref[0]
        all_ref[near] = other_ref[1]
        all_ref[here ^ 6] = far_ref[0]
        all_ref[here ^ 7] = far_ref[1]
    rows = w_ref.shape[0] // COMPS

    def scal(k, which, row=7):
        return all_ref[k, row : row + 1, which : which + 1]

    zero = jnp.zeros((COMPS, w_ref.shape[1]), F32)
    entering, own_in, at = zero, zero, []
    for k in range(blocks):
        at.append(entering)
        own_in = jnp.where(here == k, entering, own_in)
        entering = all_ref[k, 0:COMPS, :] + scal(k, ENTER, 6) * entering
    leaving, own_out = zero, zero
    for k in reversed(range(blocks)):
        own_out = jnp.where(here == k, leaving, own_out)
        leaving = (
            all_ref[k, COMPS : 2 * COMPS, :] + scal(k, ENTER) * at[k] + scal(k, LEAVE) * leaving
        )
    enter = answer_ref[number, :, ENTER : ENTER + 1]
    leave = answer_ref[number, :, LEAVE : LEAVE + 1]
    for c in range(COMPS):
        own = slice(rows * c, rows * (c + 1))
        u_ref[own, :] = w_ref[own, :] + enter * own_in[c : c + 1] + leave * own_out[c : c + 1]
    below = jnp.maximum(here - 1, 0)
    if last:
        above = jnp.minimum(here + 1, blocks - 1)
        keep_above = jnp.where(here == blocks - 1, 0.0, 1.0).astype(F32)
        keep_below = jnp.where(here == 0, 0.0, 1.0).astype(F32)
        moved_ref[:, :RESIDENT] = v_ref[:, :RESIDENT]
        moved_ref[:, RESIDENT : RESIDENT + CAP] = from_x_ref[...]
        moved_ref[:, RESIDENT + CAP : RESIDENT + 2 * CAP] = (
            all_ref[above, 8 : 8 + COMPS, 0:CAP] * keep_above
        )
        moved_ref[:, RESIDENT + 2 * CAP :] = (
            all_ref[below, 8 : 8 + COMPS, CAP : 2 * CAP] * keep_below
        )
    else:
        ef_ref[0:COMPS, :] = own_in
        ef_ref[COMPS : 2 * COMPS, :] = own_out
        ef_ref[2 * COMPS :, :] = jnp.zeros((2, w_ref.shape[1]), F32)
        for c in range(COMPS):
            ym_ref[c : c + 1, :] = (
                scal(below, PIVOT) * own_in[c : c + 1]
                + scal(below, UPWARD) * u_ref[rows * c : rows * c + 1, :]
            )


def on_device(
    velocity,
    y_metric,
    forward_rate,
    backward_rate,
    pivot_inv,
    particle_vel,
    particle_cell,
    particle_offset,
    inverse_tau,
    outgoing_count,
):
    comps, cells_x, cells_y, cells_z = velocity.shape
    assert (comps, cells_x, cells_y) == (COMPS, 1, 16)
    slots = particle_vel.shape[1]
    size_x, size_y = lax.axis_size("gx"), lax.axis_size("gy")
    ring_x = [(i, (i + 1) % size_x) for i in range(size_x)]
    back_x = [(b, a) for a, b in ring_x]
    ring_y = [(i, (i + 1) % size_y) for i in range(size_y)]
    back_y = [(b, a) for a, b in ring_y]
    flip = lambda bits: [(i, i ^ bits) for i in range(size_y)]
    mixed = [(i, i ^ (4 if i % 2 else 2)) for i in range(size_y)]
    direct = size_y == 8

    u = velocity.reshape(COMPS * cells_y, cells_z)
    first = velocity[:, 0, 0, :]
    final = velocity[:, 0, cells_y - 1, :]
    xp = lax.ppermute(u, "gx", back_x)
    xm = lax.ppermute(u, "gx", ring_x)
    yp = lax.ppermute(first, "gy", back_y)
    ym = lax.ppermute(final, "gy", ring_y)
    ahead = lax.ppermute(yp, "gx", back_x)

    cell = particle_cell.reshape(1, slots)
    tau = inverse_tau.reshape(1, slots)
    like = lambda *shape: jax.ShapeDtypeStruct(shape, F32)
    matrix, answer, scal = call(
        tables_kernel,
        (like(SECTIONS, 56, 128), like(SECTIONS, cells_y, 128), like(SECTIONS, 2, 128)),
        scalars(4),
        "tables",
    )(forward_rate, backward_rate, pivot_inv, y_metric)
    v = particle_vel
    rows = COMPS * cells_y
    field_like, slots_like = like(rows, cells_z), like(COMPS, slots)
    for k in range(SECTIONS):
        last = k == SECTIONS - 1
        near = call(
            own_plane_kernel,
            slots_like,
            whole_in_vmem(3),
            "own_plane",
            [pltpu.VMEM((4 * rows, cells_z), BF16)],
        )(u, cell, particle_offset)
        sides = (u, ym, xp, xm, yp, ahead) + (() if k == 0 else (behind,))
        out = call(
            functools.partial(section_kernel, k, TIME_STEP * SECTION_WEIGHTS[k], last),
            (field_like, like(16 if last else 8, cells_z), slots_like)
            + ((like(COMPS, CAP),) if last else ()),
            scalars(1) + whole_in_vmem(len(sides) + 8),
            "section",
            [
                pltpu.VMEM((4 * (rows + 8), cells_z), BF16),
                pltpu.VMEM((2 * rows, slots), BF16),
                pltpu.VMEM((slots, cells_z), BF16),
            ],
        )(outgoing_count, *sides, cell, particle_offset, tau, v, near, matrix, answer, scal)
        w, pq, v = out[:3]
        if direct:
            partner = lax.ppermute(pq, "gy", flip(1))
            pair = jnp.stack([pq, partner])
            side = lax.ppermute(pair, "gy", mixed)
            far = lax.ppermute(pair, "gy", flip(6))
            other = lax.ppermute(side, "gy", flip(1))
            gathered = (pq, partner, side, other, far)
            scratch = [pltpu.VMEM((size_y,) + pq.shape, F32)]
        else:
            gathered = (lax.all_gather(pq, "gy", axis=0),)
            scratch = []
        if last:
            from_x = lax.ppermute(out[3], "gx", ring_x)
            more, shapes = (v, from_x), (field_like, slots_like)
        else:
            xp = lax.ppermute(w, "gx", back_x)
            xm = lax.ppermute(w, "gx", ring_x)
            more, shapes = (), (field_like, like(8, cells_z), like(COMPS, cells_z))
        joined = call(
            functools.partial(join_kernel, k, last, size_y, direct),
            shapes,
            whole_in_vmem(len(gathered) + 2 + len(more)),
            "join",
            scratch,
        )(*gathered, w, answer, *more)
        if not last:
            u, yp, ym = joined
            ahead = lax.ppermute(yp, "gx", back_x)
            behind = lax.ppermute(yp, "gx", ring_x)
    u, moved = joined
    return (u.reshape(velocity.shape), moved)


def solution(mesh):
    return jax.shard_map(
        on_device,
        mesh=mesh,
        in_specs=(
            P(None, "gx", "gy", None),
            P("gy"),
            P(None, "gy"),
            P(None, "gy"),
            P(None, "gy"),
            P(None, ("gx", "gy")),
            P(("gx", "gy")),
            P(None, ("gx", "gy")),
            P(("gx", "gy")),
            P("gx", "gy", None),
        ),
        out_specs=(P(None, "gx", "gy", None), P(None, ("gx", "gy"))),
        check_vma=False,
    )
```

time: 103 us -> 76.9 us (0.75)
  blocking collectives: 26.9 us -> 0 us
  Pallas kernels: 33.3 us -> 20.4 us
  starting transfers between devices: 23.3 us -> 33.3 us
  waiting for transfers between devices: 10.4 us -> 19.5 us
  local copies, waits for them, and re-layouts: 6.3 us -> 2.61 us
  other arithmetic: 1.63 us -> 0.02 us
    all_gather x3 -> x0, blocking collectives: 26.9 us -> none  [on_device(): gathered = lax.all_gather(pq, 'gy', axis=0)]
    ppermute x6 -> x22, starting transfers between devices: 10.9 us -> 26.4 us  [the longest x3 9.3 us: on_device(): ahead = lax.ppermute(yp, 'gx', back_x)]
    pallas_call x9 -> x10, Pallas kernels: 33.3 us -> 20.4 us  [the longest x3 13.1 us: on_device(): call(functools.partial(section_kernel, k, TIME_STEP * SECTION_WEIGHTS[k],...]
    ppermute x3 -> x1, starting transfers between devices: 11.4 us -> 2.09 us  [on_device(): xp = lax.ppermute(u, 'gx', back_x)]
    ppermute x6 -> x22, waiting for transfers between devices: 10.3 us -> 18.1 us  [the longest x3 7.37 us: on_device(): side = lax.ppermute(pair, 'gy', mixed)]
    ppermute x3 -> x1, starting transfers between devices: 0.12 us -> 3.08 us  [on_device(): xm = lax.ppermute(u, 'gx', ring_x)]
    unnamed x24, local copies, waits for them, and re-layouts: 3.8 us -> 1.6 us
    ppermute x1, waiting for transfers between devices: 0.01 us -> 1.43 us  [on_device(): yp = lax.ppermute(first, 'gy', back_y)]
  transfers between devices with their start and end apart: 14 -> 26, of which waited for: 2 -> 10; matrix products, arithmetic and copies ran while one was open for 2% -> 1% of each run, Pallas kernels for 10% -> 8%
where the time goes in v2:
time: 76.9 us; the launch traced here: 76.7 us
  starting transfers between devices  33.3 us (43%)
  Pallas kernels  20.4 us (27%)
  waiting for transfers between devices  19.5 us (25%)
  local copies, waits for them, and re-layouts  2.61 us (3%)
  between operations  0.95 us (1%)
    pallas_call x3, Pallas kernels, on_device(): call(functools.partial(section_kernel, k, TIME_STEP * SECTION_WEIGHTS[k],...  13.1 us
    ppermute x3, starting transfers between devices, on_device(): ahead = lax.ppermute(yp, 'gx', back_x)  9.3 us
    ppermute x3, waiting for transfers between devices, on_device(): side = lax.ppermute(pair, 'gy', mixed)  7.37 us
    ppermute x2, starting transfers between devices, on_device(): xp = lax.ppermute(w, 'gx', back_x)  7.35 us
    ppermute x1, waiting for transfers between devices, on_device(): from_x = lax.ppermute(out[3], 'gx', ring_x)  5.45 us
    pallas_call x3, Pallas kernels, on_device(): call(own_plane_kernel, slots_like, whole_in_vmem(3), 'own_plane', [pltpu....  5.07 us
    ppermute x3, starting transfers between devices, on_device(): far = lax.ppermute(pair, 'gy', flip(6))  4.94 us
    ppermute x3, starting transfers between devices, on_device(): side = lax.ppermute(pair, 'gy', mixed)  3.66 us
  transfers between devices with their start and end apart: 26, of which 10 were waited for; matrix products, arithmetic and copies ran while one was open for 1% of the time, Pallas kernels for 8%

profile of v2, /device:TPU:0, one launch (start us, length us, event | category | flops | bytes accessed | tf_op | source)
XLA Modules:
  0.0 76.7 jit_solution(1554488068933101113)
XLA Ops:
  0.6 3.1 %collective-permute-start.2 = (f32[48,1024]{1,0:T(8,128)}, f32[48,1024]{1,0:T(8,128)S(1)}, u32[]{:S(2)}, u32[]{:S(2)}) collective-permute-start(f32[48,1024]{1,0:T(8,128)} %bitcast.16), channel_id=1, source_target_pairs={{0,8},{8,16},{16,24},{24,0},{1,9},{9,17},{17,25},{25,1},{2,10},{10... | collective-permute-start | bytes 589832 | tf_op jit(solution)/shard_map/ppermute | solution.py:355
  3.7 2.1 %collective-permute-start.1 = (f32[48,1024]{1,0:T(8,128)}, f32[48,1024]{1,0:T(8,128)S(1)}, u32[]{:S(2)}, u32[]{:S(2)}) collective-permute-start(f32[48,1024]{1,0:T(8,128)} %bitcast.17), channel_id=1, source_target_pairs={{8,0},{16,8},{24,16},{0,24},{9,1},{17,9},{25,17},{1,25},{10,2},{18... | collective-permute-start | bytes 589832 | tf_op jit(solution)/shard_map/ppermute | solution.py:354
  5.8 1.0 %fusion = (f32[3,1,1,1024]{3,2,1,0:T(1,128)S(1)}, f32[3,1,1,1024]{3,2,1,0:T(1,128)S(1)}) fusion(f32[3,1,16,1024]{3,2,1,0:T(8,128)} %param.10), kind=kLoop, calls=%fused_computation.5 | loop fusion | bytes 49152 | tf_op jit(solution)/shard_map/slice | solution.py:352
  6.8 1.7 %collective-permute-start.3 = (f32[3,1024]{1,0:T(4,128)S(1)}, f32[3,1024]{1,0:T(4,128)S(1)}, u32[]{:S(2)}, u32[]{:S(2)}) collective-permute-start(f32[3,1024]{1,0:T(4,128)S(1)} %bitcast.27), channel_id=1, source_target_pairs={{1,0},{2,1},{3,2},{4,3},{5,4},{6,5},{7,6},{0,7},{9,8},{10,9},{11,1... | collective-permute-start | bytes 36872 | tf_op jit(solution)/shard_map/ppermute | solution.py:356
  8.5 1.4 %collective-permute-done.3.refs_5_ = f32[3,1024]{1,0:T(4,128)S(1)} collective-permute-done((f32[3,1024]{1,0:T(4,128)S(1)}, f32[3,1024]{1,0:T(4,128)S(1)}, u32[]{:S(2)}, u32[]{:S(2)}) %collective-permute-start.3) | collective-permute-done | bytes 12320 | tf_op jit(solution)/shard_map/ppermute | solution.py:356
  9.9 1.7 %collective-permute-start.4 = (f32[3,1024]{1,0:T(4,128)S(1)}, f32[3,1024]{1,0:T(4,128)S(1)}, u32[]{:S(2)}, u32[]{:S(2)}) collective-permute-start(f32[3,1024]{1,0:T(4,128)S(1)} %collective-permute-done.3.refs_5_), channel_id=1, source_target_pairs={{8,0},{16,8},{24,16},{0,24},{9,1},{17,9},{25,17},{1,25},{10,2},{18... | collective-permute-start | bytes 36872 | tf_op jit(solution)/shard_map/ppermute | solution.py:358
  11.7 0.9 %copy-done.1 = f32[3,1,16,1024]{3,2,1,0:T(8,128)S(1)} copy-done((f32[3,1,16,1024]{3,2,1,0:T(8,128)S(1)}, f32[3,1,16,1024]{3,2,1,0:T(8,128)}, u32[]{:S(2)}) %copy-start.1) | copy-done | bytes 196632
  12.6 1.7 %own_plane.3.refs_11_ = f32[3,3584]{1,0:T(4,128)S(1)} custom-call(f32[48,1024]{1,0:T(8,128)S(1)} %bitcast.18, s32[1,3584]{1,0:T(1,128)S(1)} %reshape.17.cell_ref.refs_7_.refs_8_, f32[3,3584]{1,0:T(4,128)S(1)} %copy-done), custom_call_target="tpu_custom_call" | custom-call | tf_op jit(solution)/shard_map/own_plane/pallas_call | solution.py:374
  14.4 0.9 %tables.1 = (f32[3,56,128]{2,1,0:T(8,128)S(1)}, f32[3,16,128]{2,1,0:T(8,128)S(1)}, f32[3,2,128]{2,1,0:T(2,128)S(1)}) custom-call(f32[3,16]{1,0:T(4,128)S(1)} %copy-done.5, f32[3,16]{1,0:T(4,128)S(1)} %copy-done.6, f32[3,16]{1,0:T(4,128)S(1)} %copy-done.7, f32[16]{0:T(128)S(1)} %copy-done.8), custom_call_target="tpu_custom_call" | custom-call | tf_op jit(solution)/shard_map/tables/pallas_call | solution.py:363
  15.9 4.2 %section.3 = (f32[48,1024]{1,0:T(8,128)S(1)}, f32[8,1024]{1,0:T(8,128)S(1)}, f32[3,3584]{1,0:T(4,128)S(1)}) custom-call(s32[1,1,3]{2,1,0:T(1,128)S(1)} %copy-done.4, f32[48,1024]{1,0:T(8,128)S(1)} %bitcast.19, f32[3,1024]{1,0:T(4,128)S(1)} %collective-permute-done.refs_2_, f32[48,1024]{1,0:T(8,128)S(1)} %collective-permute-done.1.refs_3_, ...), custom_call_target="tpu_custom_call" | custom-call | tf_op jit(solution)/shard_map/section/pallas_call | solution.py:382
  21.0 3.3 %collective-permute-start.9 = (f32[48,1024]{1,0:T(8,128)S(1)}, f32[48,1024]{1,0:T(8,128)S(1)}, u32[]{:S(2)}, u32[]{:S(2)}) collective-permute-start(f32[48,1024]{1,0:T(8,128)S(1)} %get-tuple-element.27.refs_5_), channel_id=1, source_target_pairs={{8,0},{16,8},{24,16},{0,24},{9,1},{17,9},{25,17},{1,25},{10,2},{18... | collective-permute-start | bytes 589832 | tf_op jit(solution)/shard_map/ppermute | solution.py:410
  24.4 1.6 %collective-permute-start.6 = (f32[2,8,1024]{2,1,0:T(8,128)S(1)}, f32[2,8,1024]{2,1,0:T(8,128)S(1)}, u32[]{:S(2)}, u32[]{:S(2)}) collective-permute-start(f32[2,8,1024]{2,1,0:T(8,128)S(1)} %pad_maximum_fusion.1), channel_id=1, source_target_pairs={{0,2},{1,5},{2,0},{3,7},{4,6},{5,1},{6,4},{7,3},{8,10},{9,13},{10,... | collective-permute-start | bytes 196616 | tf_op jit(solution)/shard_map/ppermute | solution.py:398
  25.9 1.5 %collective-permute-start.8 = (f32[2,8,1024]{2,1,0:T(8,128)S(1)}, f32[2,8,1024]{2,1,0:T(8,128)S(1)}, u32[]{:S(2)}, u32[]{:S(2)}) collective-permute-start(f32[2,8,1024]{2,1,0:T(8,128)S(1)} %pad_maximum_fusion.1), channel_id=1, source_target_pairs={{0,6},{1,7},{2,4},{3,5},{4,2},{5,3},{6,0},{7,1},{8,14},{9,15},{10,... | collective-permute-start | bytes 196616 | tf_op jit(solution)/shard_map/ppermute | solution.py:399
  27.4 1.9 %collective-permute-done.6.refs_2_ = f32[2,8,1024]{2,1,0:T(8,128)S(1)} collective-permute-done((f32[2,8,1024]{2,1,0:T(8,128)S(1)}, f32[2,8,1024]{2,1,0:T(8,128)S(1)}, u32[]{:S(2)}, u32[]{:S(2)}) %collective-permute-start.6) | collective-permute-done | bytes 65568 | tf_op jit(solution)/shard_map/ppermute | solution.py:398
  29.3 1.8 %collective-permute-done.8.refs_4_ = f32[2,8,1024]{2,1,0:T(8,128)S(1)} collective-permute-done((f32[2,8,1024]{2,1,0:T(8,128)S(1)}, f32[2,8,1024]{2,1,0:T(8,128)S(1)}, u32[]{:S(2)}, u32[]{:S(2)}) %collective-permute-start.8) | collective-permute-done | bytes 65568 | tf_op jit(solution)/shard_map/ppermute | solution.py:399
  31.4 3.8 %collective-permute-start.11 = (f32[8,1024]{1,0:T(8,128)S(1)}, f32[8,1024]{1,0:T(8,128)S(1)}, u32[]{:S(2)}, u32[]{:S(2)}) collective-permute-start(f32[8,1024]{1,0:T(8,128)S(1)} %get-tuple-element.30.refs_5_), channel_id=1, source_target_pairs={{8,0},{16,8},{24,16},{0,24},{9,1},{17,9},{25,17},{1,25},{10,2},{18... | collective-permute-start | bytes 98312 | tf_op jit(solution)/shard_map/ppermute | solution.py:422
  35.2 1.7 %own_plane.4.refs_12_ = f32[3,3584]{1,0:T(4,128)S(1)} custom-call(f32[48,1024]{1,0:T(8,128)S(1)} %get-tuple-element.28.u_ref.refs_1_, s32[1,3584]{1,0:T(1,128)S(1)} %reshape.17.cell_ref.refs_7_.refs_8_, f32[3,3584]{1,0:T(4,128)S(1)} %copy-done), custom_call_target="tpu_custom_call" | custom-call | tf_op jit(solution)/shard_map/own_plane/pallas_call | solution.py:374
  37.1 4.4 %section.4 = (f32[48,1024]{1,0:T(8,128)S(1)}, f32[8,1024]{1,0:T(8,128)S(1)}, f32[3,3584]{1,0:T(4,128)S(1)}) custom-call(s32[1,1,3]{2,1,0:T(1,128)S(1)} %copy-done.4, f32[48,1024]{1,0:T(8,128)S(1)} %get-tuple-element.28.u_ref.refs_1_, f32[3,1024]{1,0:T(4,128)S(1)} %get-tuple-element.29.refs_2_, f32[48,1024]{1,0:T(8,128)S(1)} %collective-permute-done.9.refs_3_, ...), custom_call_target="tpu_custom_call" | custom-call | tf_op jit(solution)/shard_map/section/pallas_call | solution.py:382
  41.7 4.0 %collective-permute-start.17 = (f32[48,1024]{1,0:T(8,128)S(1)}, f32[48,1024]{1,0:T(8,128)S(1)}, u32[]{:S(2)}, u32[]{:S(2)}) collective-permute-start(f32[48,1024]{1,0:T(8,128)S(1)} %get-tuple-element.33.refs_5_), channel_id=1, source_target_pairs={{8,0},{16,8},{24,16},{0,24},{9,1},{17,9},{25,17},{1,25},{10,2},{18... | collective-permute-start | bytes 589832 | tf_op jit(solution)/shard_map/ppermute | solution.py:410
  45.7 1.2 %collective-permute-start.14 = (f32[2,8,1024]{2,1,0:T(8,128)S(1)}, f32[2,8,1024]{2,1,0:T(8,128)S(1)}, u32[]{:S(2)}, u32[]{:S(2)}) collective-permute-start(f32[2,8,1024]{2,1,0:T(8,128)S(1)} %pad_maximum_fusion.2), channel_id=1, source_target_pairs={{0,2},{1,5},{2,0},{3,7},{4,6},{5,1},{6,4},{7,3},{8,10},{9,13},{10,... | collective-permute-start | bytes 196616 | tf_op jit(solution)/shard_map/ppermute | solution.py:398
  47.0 1.8 %collective-permute-start.16 = (f32[2,8,1024]{2,1,0:T(8,128)S(1)}, f32[2,8,1024]{2,1,0:T(8,128)S(1)}, u32[]{:S(2)}, u32[]{:S(2)}) collective-permute-start(f32[2,8,1024]{2,1,0:T(8,128)S(1)} %pad_maximum_fusion.2), channel_id=1, source_target_pairs={{0,6},{1,7},{2,4},{3,5},{4,2},{5,3},{6,0},{7,1},{8,14},{9,15},{10,... | collective-permute-start | bytes 196616 | tf_op jit(solution)/shard_map/ppermute | solution.py:399
  48.8 1.9 %collective-permute-done.14.refs_2_ = f32[2,8,1024]{2,1,0:T(8,128)S(1)} collective-permute-done((f32[2,8,1024]{2,1,0:T(8,128)S(1)}, f32[2,8,1024]{2,1,0:T(8,128)S(1)}, u32[]{:S(2)}, u32[]{:S(2)}) %collective-permute-start.14) | collective-permute-done | bytes 65568 | tf_op jit(solution)/shard_map/ppermute | solution.py:398
  50.6 1.8 %collective-permute-done.16.refs_4_ = f32[2,8,1024]{2,1,0:T(8,128)S(1)} collective-permute-done((f32[2,8,1024]{2,1,0:T(8,128)S(1)}, f32[2,8,1024]{2,1,0:T(8,128)S(1)}, u32[]{:S(2)}, u32[]{:S(2)}) %collective-permute-start.16) | collective-permute-done | bytes 65568 | tf_op jit(solution)/shard_map/ppermute | solution.py:399
  52.7 3.8 %collective-permute-start.19 = (f32[8,1024]{1,0:T(8,128)S(1)}, f32[8,1024]{1,0:T(8,128)S(1)}, u32[]{:S(2)}, u32[]{:S(2)}) collective-permute-start(f32[8,1024]{1,0:T(8,128)S(1)} %get-tuple-element.36.refs_5_), channel_id=1, source_target_pairs={{8,0},{16,8},{24,16},{0,24},{9,1},{17,9},{25,17},{1,25},{10,2},{18... | collective-permute-start | bytes 98312 | tf_op jit(solution)/shard_map/ppermute | solution.py:422
  56.5 1.7 %own_plane.5.refs_12_ = f32[3,3584]{1,0:T(4,128)S(1)} custom-call(f32[48,1024]{1,0:T(8,128)S(1)} %get-tuple-element.34.u_ref.refs_1_, s32[1,3584]{1,0:T(1,128)S(1)} %reshape.17.cell_ref.refs_7_.refs_8_, f32[3,3584]{1,0:T(4,128)S(1)} %copy-done), custom_call_target="tpu_custom_call" | custom-call | tf_op jit(solution)/shard_map/own_plane/pallas_call | solution.py:374
  58.4 4.4 %section.5 = (f32[48,1024]{1,0:T(8,128)S(1)}, f32[16,1024]{1,0:T(8,128)S(1)}, f32[3,3584]{1,0:T(4,128)S(1)}, f32[3,512]{1,0:T(4,128)S(1)}) custom-call(s32[1,1,3]{2,1,0:T(1,128)S(1)} %copy-done.4, f32[48,1024]{1,0:T(8,128)S(1)} %get-tuple-element.34.u_ref.refs_1_, f32[3,1024]{1,0:T(4,128)S(1)} %get-tuple-element.35.refs_2_, ...), custom_call_target="tpu_custom_call" | custom-call | tf_op jit(solution)/shard_map/section/pallas_call | solution.py:382
  63.0 1.2 %collective-permute-done.21.refs_1_ = f32[16,1024]{1,0:T(8,128)S(1)} collective-permute-done((f32[16,1024]{1,0:T(8,128)S(1)}, f32[16,1024]{1,0:T(8,128)S(1)}, u32[]{:S(2)}, u32[]{:S(2)}) %collective-permute-start.21) | collective-permute-done | bytes 65568 | tf_op jit(solution)/shard_map/ppermute | solution.py:396
  64.2 0.8 %collective-permute-start.22 = (f32[2,16,1024]{2,1,0:T(8,128)S(1)}, f32[2,16,1024]{2,1,0:T(8,128)S(1)}, u32[]{:S(2)}, u32[]{:S(2)}) collective-permute-start(f32[2,16,1024]{2,1,0:T(8,128)S(1)} %pad_maximum_fusion), channel_id=1, source_target_pairs={{0,2},{1,5},{2,0},{3,7},{4,6},{5,1},{6,4},{7,3},{8,10},{9,13},{10,... | collective-permute-start | bytes 393224 | tf_op jit(solution)/shard_map/ppermute | solution.py:398
  65.1 1.7 %collective-permute-start.24 = (f32[2,16,1024]{2,1,0:T(8,128)S(1)}, f32[2,16,1024]{2,1,0:T(8,128)S(1)}, u32[]{:S(2)}, u32[]{:S(2)}) collective-permute-start(f32[2,16,1024]{2,1,0:T(8,128)S(1)} %pad_maximum_fusion), channel_id=1, source_target_pairs={{0,6},{1,7},{2,4},{3,5},{4,2},{5,3},{6,0},{7,1},{8,14},{9,15},{10,... | collective-permute-start | bytes 393224 | tf_op jit(solution)/shard_map/ppermute | solution.py:399
  66.7 3.6 %collective-permute-done.22.refs_2_ = f32[2,16,1024]{2,1,0:T(8,128)S(1)} collective-permute-done((f32[2,16,1024]{2,1,0:T(8,128)S(1)}, f32[2,16,1024]{2,1,0:T(8,128)S(1)}, u32[]{:S(2)}, u32[]{:S(2)}) %collective-permute-start.22) | collective-permute-done | bytes 131104 | tf_op jit(solution)/shard_map/ppermute | solution.py:398
  70.4 5.5 %collective-permute-done.25.refs_8_ = f32[3,512]{1,0:T(4,128)S(1)} collective-permute-done((f32[3,512]{1,0:T(4,128)S(1)}, f32[3,512]{1,0:T(4,128)S(1)}, u32[]{:S(2)}, u32[]{:S(2)}) %collective-permute-start.25) | collective-permute-done | bytes 6176 | tf_op jit(solution)/shard_map/ppermute | solution.py:407
  75.8 0.9 %join.5 = (f32[48,1024]{1,0:T(8,128)}, f32[3,3584]{1,0:T(4,128)}) custom-call(f32[16,1024]{1,0:T(8,128)S(1)} %get-tuple-element.38.refs_0_, f32[16,1024]{1,0:T(8,128)S(1)} %collective-permute-done.21.refs_1_, f32[2,16,1024]{2,1,0:T(8,128)S(1)} %collective-permute-done.22.refs_2_, f32[2,16,1024]{2,1,0:T(8,128)S(1)} %collective-permute-done.23.refs_3_, ...), custom_call_target="tpu_custom_call" | custom-call | tf_op jit(solution)/shard_map/join/pallas_call | solution.py:413
  (60 shorter events, 2.8 us)
Async XLA Ops:
  0.6 14.6 %collective-permute-start.2 = (f32[48,1024]{1,0:T(8,128)}, f32[48,1024]{1,0:T(8,128)S(1)}, u32[]{:S(2)}, u32[]{:S(2)}) collective-permute-start(f32[48,1024]{1,0:T(8,128)} %bitcast.16), channel_id=1, source_target_pairs={{0,8},{8,16},{16,24},{24,0},{1,9},{9,17},{17,25},{25,1},{2,10},{10... | collective-permute-start | bytes 589832 | tf_op jit(solution)/shard_map/ppermute | solution.py:355
  3.7 11.6 %collective-permute-start.1 = (f32[48,1024]{1,0:T(8,128)}, f32[48,1024]{1,0:T(8,128)S(1)}, u32[]{:S(2)}, u32[]{:S(2)}) collective-permute-start(f32[48,1024]{1,0:T(8,128)} %bitcast.17), channel_id=1, source_target_pairs={{8,0},{16,8},{24,16},{0,24},{9,1},{17,9},{25,17},{1,25},{10,2},{18... | collective-permute-start | bytes 589832 | tf_op jit(solution)/shard_map/ppermute | solution.py:354
  6.8 4.8 %copy-start.9 = (s32[3584]{0:T(1024)S(1)}, s32[3584]{0:T(1024)}, u32[]{:S(2)}) copy-start(s32[3584]{0:T(1024)} %param.16) | copy-start | bytes 43012
  6.8 4.9 %copy-start = (f32[3,3584]{1,0:T(4,128)S(1)}, f32[3,3584]{1,0:T(4,128)}, u32[]{:S(2)}) copy-start(f32[3,3584]{1,0:T(4,128)} %refs_9_.3) | copy-start | bytes 129028
  6.8 3.1 %collective-permute-start.3 = (f32[3,1024]{1,0:T(4,128)S(1)}, f32[3,1024]{1,0:T(4,128)S(1)}, u32[]{:S(2)}, u32[]{:S(2)}) collective-permute-start(f32[3,1024]{1,0:T(4,128)S(1)} %bitcast.27), channel_id=1, source_target_pairs={{1,0},{2,1},{3,2},{4,3},{5,4},{6,5},{7,6},{0,7},{9,8},{10,9},{11,1... | collective-permute-start | bytes 36872 | tf_op jit(solution)/shard_map/ppermute | solution.py:356
  8.5 3.1 %copy-start.10 = (f32[3584]{0:T(1024)S(1)}, f32[3584]{0:T(1024)}, u32[]{:S(2)}) copy-start(f32[3584]{0:T(1024)} %param.18) | copy-start | bytes 43012
  8.5 6.7 %collective-permute-start = (f32[3,1024]{1,0:T(4,128)S(1)}, f32[3,1024]{1,0:T(4,128)S(1)}, u32[]{:S(2)}, u32[]{:S(2)}) collective-permute-start(f32[3,1024]{1,0:T(4,128)S(1)} %bitcast.26), channel_id=1, source_target_pairs={{0,1},{1,2},{2,3},{3,4},{4,5},{5,6},{6,7},{7,0},{8,9},{9,10},{10,1... | collective-permute-start | bytes 36872 | tf_op jit(solution)/shard_map/ppermute | solution.py:357
  9.9 5.3 %collective-permute-start.4 = (f32[3,1024]{1,0:T(4,128)S(1)}, f32[3,1024]{1,0:T(4,128)S(1)}, u32[]{:S(2)}, u32[]{:S(2)}) collective-permute-start(f32[3,1024]{1,0:T(4,128)S(1)} %collective-permute-done.3.refs_5_), channel_id=1, source_target_pairs={{8,0},{16,8},{24,16},{0,24},{9,1},{17,9},{25,17},{1,25},{10,2},{18... | collective-permute-start | bytes 36872 | tf_op jit(solution)/shard_map/ppermute | solution.py:358
  12.6 1.8 %copy-start.8 = (f32[16]{0:T(128)S(1)}, f32[16]{0:T(128)}, u32[]{:S(2)}) copy-start(f32[16]{0:T(128)} %metric_ref.1) | copy-start | bytes 196
  12.6 2.7 %copy-start.2 = (f32[3,1,16,1024]{3,2,1,0:T(8,128)S(1)}, f32[3,1,16,1024]{3,2,1,0:T(8,128)}, u32[]{:S(2)}) copy-start(f32[3,1,16,1024]{3,2,1,0:T(8,128)} %param.10) | copy-start | bytes 589828
  12.6 2.7 %copy-start.3 = (f32[3,3584]{1,0:T(4,128)S(1)}, f32[3,3584]{1,0:T(4,128)}, u32[]{:S(2)}) copy-start(f32[3,3584]{1,0:T(4,128)} %refs_10_.1) | copy-start | bytes 129028
  20.2 4.2 %collective-permute-start.5 = (f32[8,1024]{1,0:T(8,128)S(1)}, f32[8,1024]{1,0:T(8,128)S(1)}, u32[]{:S(2)}, u32[]{:S(2)}) collective-permute-start(f32[8,1024]{1,0:T(8,128)S(1)} %get-tuple-element.26.refs_0_), channel_id=1, source_target_pairs={{0,1},{1,0},{2,3},{3,2},{4,5},{5,4},{6,7},{7,6},{8,9},{9,8},{10,11... | collective-permute-start | bytes 98312 | tf_op jit(solution)/shard_map/ppermute | solution.py:396
  20.5 16.6 %collective-permute-start.10 = (f32[48,1024]{1,0:T(8,128)S(1)}, f32[48,1024]{1,0:T(8,128)S(1)}, u32[]{:S(2)}, u32[]{:S(2)}) collective-permute-start(f32[48,1024]{1,0:T(8,128)S(1)} %get-tuple-element.27.refs_5_), channel_id=1, source_target_pairs={{0,8},{8,16},{16,24},{24,0},{1,9},{9,17},{17,25},{25,1},{2,10},{10... | collective-permute-start | bytes 589832 | tf_op jit(solution)/shard_map/ppermute | solution.py:411
  21.0 16.1 %collective-permute-start.9 = (f32[48,1024]{1,0:T(8,128)S(1)}, f32[48,1024]{1,0:T(8,128)S(1)}, u32[]{:S(2)}, u32[]{:S(2)}) collective-permute-start(f32[48,1024]{1,0:T(8,128)S(1)} %get-tuple-element.27.refs_5_), channel_id=1, source_target_pairs={{8,0},{16,8},{24,16},{0,24},{9,1},{17,9},{25,17},{1,25},{10,2},{18... | collective-permute-start | bytes 589832 | tf_op jit(solution)/shard_map/ppermute | solution.py:410
  24.4 4.9 %collective-permute-start.6 = (f32[2,8,1024]{2,1,0:T(8,128)S(1)}, f32[2,8,1024]{2,1,0:T(8,128)S(1)}, u32[]{:S(2)}, u32[]{:S(2)}) collective-permute-start(f32[2,8,1024]{2,1,0:T(8,128)S(1)} %pad_maximum_fusion.1), channel_id=1, source_target_pairs={{0,2},{1,5},{2,0},{3,7},{4,6},{5,1},{6,4},{7,3},{8,10},{9,13},{10,... | collective-permute-start | bytes 196616 | tf_op jit(solution)/shard_map/ppermute | solution.py:398
  25.9 5.2 %collective-permute-start.8 = (f32[2,8,1024]{2,1,0:T(8,128)S(1)}, f32[2,8,1024]{2,1,0:T(8,128)S(1)}, u32[]{:S(2)}, u32[]{:S(2)}) collective-permute-start(f32[2,8,1024]{2,1,0:T(8,128)S(1)} %pad_maximum_fusion.1), channel_id=1, source_target_pairs={{0,6},{1,7},{2,4},{3,5},{4,2},{5,3},{6,0},{7,1},{8,14},{9,15},{10,... | collective-permute-start | bytes 196616 | tf_op jit(solution)/shard_map/ppermute | solution.py:399
  29.3 1.8 %collective-permute-start.7 = (f32[2,8,1024]{2,1,0:T(8,128)S(1)}, f32[2,8,1024]{2,1,0:T(8,128)S(1)}, u32[]{:S(2)}, u32[]{:S(2)}) collective-permute-start(f32[2,8,1024]{2,1,0:T(8,128)S(1)} %collective-permute-done.6.refs_2_), channel_id=1, source_target_pairs={{0,1},{1,0},{2,3},{3,2},{4,5},{5,4},{6,7},{7,6},{8,9},{9,8},{10,11... | collective-permute-start | bytes 196616 | tf_op jit(solution)/shard_map/ppermute | solution.py:400
  31.3 5.8 %collective-permute-start.12 = (f32[8,1024]{1,0:T(8,128)S(1)}, f32[8,1024]{1,0:T(8,128)S(1)}, u32[]{:S(2)}, u32[]{:S(2)}) collective-permute-start(f32[8,1024]{1,0:T(8,128)S(1)} %get-tuple-element.30.refs_5_), channel_id=1, source_target_pairs={{0,8},{8,16},{16,24},{24,0},{1,9},{9,17},{17,25},{25,1},{2,10},{10... | collective-permute-start | bytes 98312 | tf_op jit(solution)/shard_map/ppermute | solution.py:423
  31.4 5.7 %collective-permute-start.11 = (f32[8,1024]{1,0:T(8,128)S(1)}, f32[8,1024]{1,0:T(8,128)S(1)}, u32[]{:S(2)}, u32[]{:S(2)}) collective-permute-start(f32[8,1024]{1,0:T(8,128)S(1)} %get-tuple-element.30.refs_5_), channel_id=1, source_target_pairs={{8,0},{16,8},{24,16},{0,24},{9,1},{17,9},{25,17},{1,25},{10,2},{18... | collective-permute-start | bytes 98312 | tf_op jit(solution)/shard_map/ppermute | solution.py:422
  41.6 4.2 %collective-permute-start.13 = (f32[8,1024]{1,0:T(8,128)S(1)}, f32[8,1024]{1,0:T(8,128)S(1)}, u32[]{:S(2)}, u32[]{:S(2)}) collective-permute-start(f32[8,1024]{1,0:T(8,128)S(1)} %get-tuple-element.32.refs_0_), channel_id=1, source_target_pairs={{0,1},{1,0},{2,3},{3,2},{4,5},{5,4},{6,7},{7,6},{8,9},{9,8},{10,11... | collective-permute-start | bytes 98312 | tf_op jit(solution)/shard_map/ppermute | solution.py:396
  41.6 16.8 %collective-permute-start.18 = (f32[48,1024]{1,0:T(8,128)S(1)}, f32[48,1024]{1,0:T(8,128)S(1)}, u32[]{:S(2)}, u32[]{:S(2)}) collective-permute-start(f32[48,1024]{1,0:T(8,128)S(1)} %get-tuple-element.33.refs_5_), channel_id=1, source_target_pairs={{0,8},{8,16},{16,24},{24,0},{1,9},{9,17},{17,25},{25,1},{2,10},{10... | collective-permute-start | bytes 589832 | tf_op jit(solution)/shard_map/ppermute | solution.py:411
  41.7 16.7 %collective-permute-start.17 = (f32[48,1024]{1,0:T(8,128)S(1)}, f32[48,1024]{1,0:T(8,128)S(1)}, u32[]{:S(2)}, u32[]{:S(2)}) collective-permute-start(f32[48,1024]{1,0:T(8,128)S(1)} %get-tuple-element.33.refs_5_), channel_id=1, source_target_pairs={{8,0},{16,8},{24,16},{0,24},{9,1},{17,9},{25,17},{1,25},{10,2},{18... | collective-permute-start | bytes 589832 | tf_op jit(solution)/shard_map/ppermute | solution.py:410
  45.7 4.9 %collective-permute-start.14 = (f32[2,8,1024]{2,1,0:T(8,128)S(1)}, f32[2,8,1024]{2,1,0:T(8,128)S(1)}, u32[]{:S(2)}, u32[]{:S(2)}) collective-permute-start(f32[2,8,1024]{2,1,0:T(8,128)S(1)} %pad_maximum_fusion.2), channel_id=1, source_target_pairs={{0,2},{1,5},{2,0},{3,7},{4,6},{5,1},{6,4},{7,3},{8,10},{9,13},{10,... | collective-permute-start | bytes 196616 | tf_op jit(solution)/shard_map/ppermute | solution.py:398
  47.0 5.4 %collective-permute-start.16 = (f32[2,8,1024]{2,1,0:T(8,128)S(1)}, f32[2,8,1024]{2,1,0:T(8,128)S(1)}, u32[]{:S(2)}, u32[]{:S(2)}) collective-permute-start(f32[2,8,1024]{2,1,0:T(8,128)S(1)} %pad_maximum_fusion.2), channel_id=1, source_target_pairs={{0,6},{1,7},{2,4},{3,5},{4,2},{5,3},{6,0},{7,1},{8,14},{9,15},{10,... | collective-permute-start | bytes 196616 | tf_op jit(solution)/shard_map/ppermute | solution.py:399
  50.6 1.8 %collective-permute-start.15 = (f32[2,8,1024]{2,1,0:T(8,128)S(1)}, f32[2,8,1024]{2,1,0:T(8,128)S(1)}, u32[]{:S(2)}, u32[]{:S(2)}) collective-permute-start(f32[2,8,1024]{2,1,0:T(8,128)S(1)} %collective-permute-done.14.refs_2_), channel_id=1, source_target_pairs={{0,1},{1,0},{2,3},{3,2},{4,5},{5,4},{6,7},{7,6},{8,9},{9,8},{10,11... | collective-permute-start | bytes 196616 | tf_op jit(solution)/shard_map/ppermute | solution.py:400
  52.7 5.8 %collective-permute-start.20 = (f32[8,1024]{1,0:T(8,128)S(1)}, f32[8,1024]{1,0:T(8,128)S(1)}, u32[]{:S(2)}, u32[]{:S(2)}) collective-permute-start(f32[8,1024]{1,0:T(8,128)S(1)} %get-tuple-element.36.refs_5_), channel_id=1, source_target_pairs={{0,8},{8,16},{16,24},{24,0},{1,9},{9,17},{17,25},{25,1},{2,10},{10... | collective-permute-start | bytes 98312 | tf_op jit(solution)/shard_map/ppermute | solution.py:423
  52.7 5.7 %collective-permute-start.19 = (f32[8,1024]{1,0:T(8,128)S(1)}, f32[8,1024]{1,0:T(8,128)S(1)}, u32[]{:S(2)}, u32[]{:S(2)}) collective-permute-start(f32[8,1024]{1,0:T(8,128)S(1)} %get-tuple-element.36.refs_5_), channel_id=1, source_target_pairs={{8,0},{16,8},{24,16},{0,24},{9,1},{17,9},{25,17},{1,25},{10,2},{18... | collective-permute-start | bytes 98312 | tf_op jit(solution)/shard_map/ppermute | solution.py:422
  62.9 1.3 %collective-permute-start.21 = (f32[16,1024]{1,0:T(8,128)S(1)}, f32[16,1024]{1,0:T(8,128)S(1)}, u32[]{:S(2)}, u32[]{:S(2)}) collective-permute-start(f32[16,1024]{1,0:T(8,128)S(1)} %get-tuple-element.38.refs_0_), channel_id=1, source_target_pairs={{0,1},{1,0},{2,3},{3,2},{4,5},{5,4},{6,7},{7,6},{8,9},{9,8},{10,11... | collective-permute-start | bytes 196616 | tf_op jit(solution)/shard_map/ppermute | solution.py:396
  64.2 6.2 %collective-permute-start.22 = (f32[2,16,1024]{2,1,0:T(8,128)S(1)}, f32[2,16,1024]{2,1,0:T(8,128)S(1)}, u32[]{:S(2)}, u32[]{:S(2)}) collective-permute-start(f32[2,16,1024]{2,1,0:T(8,128)S(1)} %pad_maximum_fusion), channel_id=1, source_target_pairs={{0,2},{1,5},{2,0},{3,7},{4,6},{5,1},{6,4},{7,3},{8,10},{9,13},{10,... | collective-permute-start | bytes 393224 | tf_op jit(solution)/shard_map/ppermute | solution.py:398
  65.1 10.8 %collective-permute-start.24 = (f32[2,16,1024]{2,1,0:T(8,128)S(1)}, f32[2,16,1024]{2,1,0:T(8,128)S(1)}, u32[]{:S(2)}, u32[]{:S(2)}) collective-permute-start(f32[2,16,1024]{2,1,0:T(8,128)S(1)} %pad_maximum_fusion), channel_id=1, source_target_pairs={{0,6},{1,7},{2,4},{3,5},{4,2},{5,3},{6,0},{7,1},{8,14},{9,15},{10,... | collective-permute-start | bytes 393224 | tf_op jit(solution)/shard_map/ppermute | solution.py:399
  70.4 5.5 %collective-permute-start.23 = (f32[2,16,1024]{2,1,0:T(8,128)S(1)}, f32[2,16,1024]{2,1,0:T(8,128)S(1)}, u32[]{:S(2)}, u32[]{:S(2)}) collective-permute-start(f32[2,16,1024]{2,1,0:T(8,128)S(1)} %collective-permute-done.22.refs_2_), channel_id=1, source_target_pairs={{0,1},{1,0},{2,3},{3,2},{4,5},{5,4},{6,7},{7,6},{8,9},{9,8},{10,11... | collective-permute-start | bytes 393224 | tf_op jit(solution)/shard_map/ppermute | solution.py:400
  70.4 5.5 %collective-permute-start.25 = (f32[3,512]{1,0:T(4,128)S(1)}, f32[3,512]{1,0:T(4,128)S(1)}, u32[]{:S(2)}, u32[]{:S(2)}) collective-permute-start(f32[3,512]{1,0:T(4,128)S(1)} %get-tuple-element.41), channel_id=1, source_target_pairs={{0,8},{8,16},{16,24},{24,0},{1,9},{9,17},{17,25},{25,1},{2,10},{10... | collective-permute-start | bytes 18440 | tf_op jit(solution)/shard_map/ppermute | solution.py:407
  (5 other events, 6.8 us)

commit v3 on v2

--- a/solution.py
+++ b/solution.py
@@ -141,11 +141,11 @@
     first = number == 0
     refs = list(refs)
     take = lambda count: [refs.pop(0) for _ in range(count)]
-    count_ref, u_ref, ym_ref, xp_ref, xm_ref, yp_ref, ahead_ref = take(7)
-    behind_ref = None if first else refs.pop(0)
+    count_ref, u_ref, ym_ref, near_x_ref, far_x_ref, yp_ref, near_ef_ref, far_ef_ref = take(8)
     cell_ref, off_ref, tau_ref, v_ref, near_ref, matrix_ref, answer_ref, scal_ref = take(8)
     w_ref, pq_ref, v_out_ref = take(3)
-    leaving_ref = refs.pop(0) if last else None
+    if last:
+        leaving_x_ref, leaving_y_ref = take(2)
     table_ref, spread_ref, chosen_ref = refs
 
     cells_z = u_ref.shape[1]
@@ -155,28 +155,34 @@
     top = jnp.where(position == lax.axis_size("gy") - 1, 0.0, 1.0).astype(F32)
     bottom = jnp.where(position == 0, 0.0, 1.0).astype(F32)
     y_minus = ym_ref[...] * bottom
-    x_plus, x_minus = xp_ref[...], xm_ref[...]
+    even = lax.axis_index("gx") % 2 == 0
+
+    def sides(one, other):
+        return jnp.where(even, one, other), jnp.where(even, other, one)
+
+    x_plus, x_minus = sides(near_x_ref[...], far_x_ref[...])
+    ahead, behind = sides(near_ef_ref[...], far_ef_ref[...])
     if first:
         y_plus = yp_ref[...] * top
-        corner = ahead_ref[...] * top
+        corner = ahead * top
     else:
         y_plus = yp_ref[COMPS : 2 * COMPS, :]
-        corner = ahead_ref[COMPS : 2 * COMPS, :]
+        corner = ahead[COMPS : 2 * COMPS]
         enter = answer_ref[number - 1, :, ENTER : ENTER + 1]
         leave = answer_ref[number - 1, :, LEAVE : LEAVE + 1]
 
-        def joined(plane, ref):
+        def joined(plane, ef):
             return jnp.concatenate(
                 [
                     plane[rows * c : rows * (c + 1)]
-                    + enter * ref[c : c + 1, :]
-                    + leave * ref[COMPS + c : COMPS + c + 1, :]
+                    + enter * ef[c : c + 1]
+                    + leave * ef[COMPS + c : COMPS + c + 1]
                     for c in range(COMPS)
                 ],
                 axis=0,
             )
 
-        x_plus, x_minus = joined(x_plus, ahead_ref), joined(x_minus, behind_ref)
+        x_plus, x_minus = joined(x_plus, ahead), joined(x_minus, behind)
     pad = jnp.zeros((2, cells_z), F32)
     table_ref[...] = split_rows(jnp.concatenate([x_plus, y_plus, corner, pad], axis=0))
     order = lax.broadcasted_iota(jnp.int32, (rows, TILE), 0)
@@ -246,9 +252,8 @@
     pq_ref[6:8, :] = jnp.zeros((2, cells_z), F32)
     pq_ref[6:8, 0:128] = scal_ref[number]
     if last:
-        leaving_ref[...] = v_out_ref[:, RESIDENT : RESIDENT + CAP]
-        pq_ref[8 : 8 + COMPS, :] = v_out_ref[:, RESIDENT + CAP : RESIDENT + 3 * CAP]
-        pq_ref[8 + COMPS :, :] = jnp.zeros((8 - COMPS, cells_z), F32)
+        leaving_y_ref[...] = v_out_ref[:, RESIDENT + CAP : RESIDENT + 3 * CAP]
+        leaving_x_ref[...] = v_out_ref[:, RESIDENT : RESIDENT + CAP]
 
 
 def join_kernel(number, last, blocks, direct, *refs):
@@ -261,7 +266,7 @@
         (all_ref,) = take(1)
     w_ref, answer_ref = take(2)
     if last:
-        v_ref, from_x_ref, u_ref, moved_ref = take(4)
+        v_ref, from_x_ref, chip_ref, beside_ref, u_ref, moved_ref = take(6)
     else:
         u_ref, ef_ref, ym_ref = take(3)
     if direct:
@@ -302,17 +307,16 @@
         u_ref[own, :] = w_ref[own, :] + enter * own_in[c : c + 1] + leave * own_out[c : c + 1]
     below = jnp.maximum(here - 1, 0)
     if last:
-        above = jnp.minimum(here + 1, blocks - 1)
+        even = here % 2 == 0
         keep_above = jnp.where(here == blocks - 1, 0.0, 1.0).astype(F32)
         keep_below = jnp.where(here == 0, 0.0, 1.0).astype(F32)
+        chip, beside = chip_ref[...], beside_ref[...]
         moved_ref[:, :RESIDENT] = v_ref[:, :RESIDENT]
         moved_ref[:, RESIDENT : RESIDENT + CAP] = from_x_ref[...]
         moved_ref[:, RESIDENT + CAP : RESIDENT + 2 * CAP] = (
-            all_ref[above, 8 : 8 + COMPS, 0:CAP] * keep_above
+            jnp.where(even, chip, beside)[:, :CAP] * keep_above
         )
-        moved_ref[:, RESIDENT + 2 * CAP :] = (
-            all_ref[below, 8 : 8 + COMPS, CAP : 2 * CAP] * keep_below
-        )
+        moved_ref[:, RESIDENT + 2 * CAP :] = jnp.where(even, beside, chip)[:, CAP:] * keep_below
     else:
         ef_ref[0:COMPS, :] = own_in
         ef_ref[COMPS : 2 * COMPS, :] = own_out
@@ -340,8 +344,16 @@
     assert (comps, cells_x, cells_y) == (COMPS, 1, 16)
     slots = particle_vel.shape[1]
     size_x, size_y = lax.axis_size("gx"), lax.axis_size("gy")
+    assert size_x % 2 == 0 and size_y % 2 == 0
     ring_x = [(i, (i + 1) % size_x) for i in range(size_x)]
-    back_x = [(b, a) for a, b in ring_x]
+    next_to = [(i, (i + (1 if i % 2 else -1)) % size_y) for i in range(size_y)]
+    same_pair = [(i, i ^ 1) for i in range(size_x)]
+    next_pair = [(i, (i + (1 if i % 2 else -1)) % size_x) for i in range(size_x)]
+
+    def both_sides(block):
+        far = lax.ppermute(block, "gx", next_pair)
+        return lax.ppermute(block, "gx", same_pair), far
+
     ring_y = [(i, (i + 1) % size_y) for i in range(size_y)]
     back_y = [(b, a) for a, b in ring_y]
     flip = lambda bits: [(i, i ^ bits) for i in range(size_y)]
@@ -351,11 +363,10 @@
     u = velocity.reshape(COMPS * cells_y, cells_z)
     first = velocity[:, 0, 0, :]
     final = velocity[:, 0, cells_y - 1, :]
-    xp = lax.ppermute(u, "gx", back_x)
-    xm = lax.ppermute(u, "gx", ring_x)
+    planes = both_sides(u)
     yp = lax.ppermute(first, "gy", back_y)
     ym = lax.ppermute(final, "gy", ring_y)
-    ahead = lax.ppermute(yp, "gx", back_x)
+    edges = both_sides(yp)
 
     cell = particle_cell.reshape(1, slots)
     tau = inverse_tau.reshape(1, slots)
@@ -378,11 +389,11 @@
             "own_plane",
             [pltpu.VMEM((4 * rows, cells_z), BF16)],
         )(u, cell, particle_offset)
-        sides = (u, ym, xp, xm, yp, ahead) + (() if k == 0 else (behind,))
+        sides = (u, ym, *planes, yp, *edges)
         out = call(
             functools.partial(section_kernel, k, TIME_STEP * SECTION_WEIGHTS[k], last),
-            (field_like, like(16 if last else 8, cells_z), slots_like)
-            + ((like(COMPS, CAP),) if last else ()),
+            (field_like, like(8, cells_z), slots_like)
+            + ((like(COMPS, CAP), like(COMPS, 2 * CAP)) if last else ()),
             scalars(1) + whole_in_vmem(len(sides) + 8),
             "section",
             [
@@ -392,11 +403,17 @@
             ],
         )(outgoing_count, *sides, cell, particle_offset, tau, v, near, matrix, answer, scal)
         w, pq, v = out[:3]
+        if last:
+            from_x = lax.ppermute(out[3], "gx", ring_x)
+            chip = lax.ppermute(out[4], "gy", flip(1))
+            beside = lax.ppermute(out[4], "gy", next_to)
         if direct:
             partner = lax.ppermute(pq, "gy", flip(1))
             pair = jnp.stack([pq, partner])
             side = lax.ppermute(pair, "gy", mixed)
             far = lax.ppermute(pair, "gy", flip(6))
+            if last:
+                side, from_x, beside = lax.optimization_barrier((side, from_x, beside))
             other = lax.ppermute(side, "gy", flip(1))
             gathered = (pq, partner, side, other, far)
             scratch = [pltpu.VMEM((size_y,) + pq.shape, F32)]
@@ -404,11 +421,9 @@
             gathered = (lax.all_gather(pq, "gy", axis=0),)
             scratch = []
         if last:
-            from_x = lax.ppermute(out[3], "gx", ring_x)
-            more, shapes = (v, from_x), (field_like, slots_like)
+            more, shapes = (v, from_x, chip, beside), (field_like, slots_like)
         else:
-            xp = lax.ppermute(w, "gx", back_x)
-            xm = lax.ppermute(w, "gx", ring_x)
+            planes = both_sides(w)
             more, shapes = (), (field_like, like(8, cells_z), like(COMPS, cells_z))
         joined = call(
             functools.partial(join_kernel, k, last, size_y, direct),
@@ -419,8 +434,7 @@
         )(*gathered, w, answer, *more)
         if not last:
             u, yp, ym = joined
-            ahead = lax.ppermute(yp, "gx", back_x)
-            behind = lax.ppermute(yp, "gx", ring_x)
+            edges = both_sides(yp)
     u, moved = joined
     return (u.reshape(velocity.shape), moved)
 

time: 76.9 us -> 72.3 us (0.940)
  starting transfers between devices: 33.3 us -> 29.7 us
  waiting for transfers between devices: 19.5 us -> 18.3 us
    ppermute x11 -> x14, waiting for transfers between devices: 0.4 us -> 4.67 us  [the longest x6 3.47 us: both_sides(): far = lax.ppermute(block, 'gx', next_pair)]
    ppermute x3, waiting for transfers between devices: 7.37 us -> 3.53 us  [on_device(): side = lax.ppermute(pair, 'gy', mixed)]
    ppermute x11 -> x14, starting transfers between devices: 22.5 us -> 18.9 us  [the longest x6 14.2 us: both_sides(): far = lax.ppermute(block, 'gx', next_pair)]
    ppermute x1, waiting for transfers between devices: 5.45 us -> 3.63 us  [on_device(): from_x = lax.ppermute(out[3], 'gx', ring_x)]
    ppermute x3, starting transfers between devices: 4.94 us -> 4.07 us  [on_device(): far = lax.ppermute(pair, 'gy', flip(6))]
  transfers between devices with their start and end apart: 26 -> 29, of which waited for: 10 -> 12; matrix products, arithmetic and copies ran while one was open for 1% -> 1% of each run, Pallas kernels for 8% -> 9%
where the time goes in v3:
time: 72.3 us; the launch traced here: 72.1 us
  starting transfers between devices  29.7 us (41%)
  Pallas kernels  20.6 us (28%)
  waiting for transfers between devices  18.3 us (25%)
  local copies, waits for them, and re-layouts  2.61 us (4%)
  between operations  0.9 us (1%)
    ppermute x6, starting transfers between devices, both_sides(): far = lax.ppermute(block, 'gx', next_pair)  14.2 us
    pallas_call x3, Pallas kernels, on_device(): call(functools.partial(section_kernel, k, TIME_STEP * SECTION_WEIGHTS[k],...  13.1 us
    pallas_call x3, Pallas kernels, on_device(): call(own_plane_kernel, slots_like, whole_in_vmem(3), 'own_plane', [pltpu....  5.25 us
    ppermute x3, starting transfers between devices, on_device(): far = lax.ppermute(pair, 'gy', flip(6))  4.07 us
    ppermute x3, starting transfers between devices, on_device(): side = lax.ppermute(pair, 'gy', mixed)  4.06 us
    ppermute x3, waiting for transfers between devices, on_device(): far = lax.ppermute(pair, 'gy', flip(6))  3.81 us
    ppermute x1, waiting for transfers between devices, on_device(): from_x = lax.ppermute(out[3], 'gx', ring_x)  3.63 us
    ppermute x3, waiting for transfers between devices, on_device(): side = lax.ppermute(pair, 'gy', mixed)  3.53 us
  transfers between devices with their start and end apart: 29, of which 12 were waited for; matrix products, arithmetic and copies ran while one was open for 1% of the time, Pallas kernels for 9%

profile of v3, /device:TPU:0, one launch (start us, length us, event | category | flops | bytes accessed | tf_op | source)
XLA Modules:
  0.0 72.1 jit_solution(17285752879461894726)
XLA Ops:
  0.6 5.1 %collective-permute-start.2 = (f32[48,1024]{1,0:T(8,128)}, f32[48,1024]{1,0:T(8,128)S(1)}, u32[]{:S(2)}, u32[]{:S(2)}) collective-permute-start(f32[48,1024]{1,0:T(8,128)} %bitcast.16), channel_id=1, source_target_pairs={{0,24},{8,16},{16,8},{24,0},{1,25},{9,17},{17,9},{25,1},{2,26},{10... | collective-permute-start | bytes 589832 | tf_op jit(solution)/shard_map/ppermute | solution.py:354
  5.7 1.0 %fusion = (f32[3,1,1,1024]{3,2,1,0:T(1,128)S(1)}, f32[3,1,1,1024]{3,2,1,0:T(1,128)S(1)}) fusion(f32[3,1,16,1024]{3,2,1,0:T(8,128)} %param.10), kind=kLoop, calls=%fused_computation.5 | loop fusion | bytes 49152 | tf_op jit(solution)/shard_map/slice | solution.py:364
  6.8 1.7 %collective-permute-start.3 = (f32[3,1024]{1,0:T(4,128)S(1)}, f32[3,1024]{1,0:T(4,128)S(1)}, u32[]{:S(2)}, u32[]{:S(2)}) collective-permute-start(f32[3,1024]{1,0:T(4,128)S(1)} %bitcast.27), channel_id=1, source_target_pairs={{1,0},{2,1},{3,2},{4,3},{5,4},{6,5},{7,6},{0,7},{9,8},{10,9},{11,1... | collective-permute-start | bytes 36872 | tf_op jit(solution)/shard_map/ppermute | solution.py:367
  8.4 1.4 %collective-permute-done.3.refs_5_ = f32[3,1024]{1,0:T(4,128)S(1)} collective-permute-done((f32[3,1024]{1,0:T(4,128)S(1)}, f32[3,1024]{1,0:T(4,128)S(1)}, u32[]{:S(2)}, u32[]{:S(2)}) %collective-permute-start.3) | collective-permute-done | bytes 12320 | tf_op jit(solution)/shard_map/ppermute | solution.py:367
  10.5 1.1 %collective-permute-start.4 = (f32[3,1024]{1,0:T(4,128)S(1)}, f32[3,1024]{1,0:T(4,128)S(1)}, u32[]{:S(2)}, u32[]{:S(2)}) collective-permute-start(f32[3,1024]{1,0:T(4,128)S(1)} %collective-permute-done.3.refs_5_), channel_id=1, source_target_pairs={{0,8},{8,0},{16,24},{24,16},{1,9},{9,1},{17,25},{25,17},{2,10},{10... | collective-permute-start | bytes 36872 | tf_op jit(solution)/shard_map/ppermute | solution.py:355
  11.7 0.9 %copy-done.1 = f32[3,1,16,1024]{3,2,1,0:T(8,128)S(1)} copy-done((f32[3,1,16,1024]{3,2,1,0:T(8,128)S(1)}, f32[3,1,16,1024]{3,2,1,0:T(8,128)}, u32[]{:S(2)}) %copy-start.1) | copy-done | bytes 196632
  12.6 1.7 %own_plane.3.refs_12_ = f32[3,3584]{1,0:T(4,128)S(1)} custom-call(f32[48,1024]{1,0:T(8,128)S(1)} %bitcast.18, s32[1,3584]{1,0:T(1,128)S(1)} %reshape.17.cell_ref.refs_8_, f32[3,3584]{1,0:T(4,128)S(1)} %copy-done), custom_call_target="tpu_custom_call" | custom-call | tf_op jit(solution)/shard_map/own_plane/pallas_call | solution.py:385
  16.5 4.3 %section.3 = (f32[48,1024]{1,0:T(8,128)S(1)}, f32[8,1024]{1,0:T(8,128)S(1)}, f32[3,3584]{1,0:T(4,128)S(1)}) custom-call(s32[1,1,3]{2,1,0:T(1,128)S(1)} %copy-done.4, f32[48,1024]{1,0:T(8,128)S(1)} %bitcast.19, f32[3,1024]{1,0:T(4,128)S(1)} %collective-permute-done.refs_2_, f32[48,1024]{1,0:T(8,128)S(1)} %collective-permute-done.1.refs_3_, ...), custom_call_target="tpu_custom_call" | custom-call | tf_op jit(solution)/shard_map/section/pallas_call | solution.py:393
  20.9 3.4 %collective-permute-start.11 = (f32[48,1024]{1,0:T(8,128)S(1)}, f32[48,1024]{1,0:T(8,128)S(1)}, u32[]{:S(2)}, u32[]{:S(2)}) collective-permute-start(f32[48,1024]{1,0:T(8,128)S(1)} %get-tuple-element.31.refs_5_), channel_id=1, source_target_pairs={{0,24},{8,16},{16,8},{24,0},{1,25},{9,17},{17,9},{25,1},{2,26},{10... | collective-permute-start | bytes 589832 | tf_op jit(solution)/shard_map/ppermute | solution.py:354
  24.3 1.6 %collective-permute-start.7 = (f32[2,8,1024]{2,1,0:T(8,128)S(1)}, f32[2,8,1024]{2,1,0:T(8,128)S(1)}, u32[]{:S(2)}, u32[]{:S(2)}) collective-permute-start(f32[2,8,1024]{2,1,0:T(8,128)S(1)} %pad_maximum_fusion), channel_id=1, source_target_pairs={{0,2},{1,5},{2,0},{3,7},{4,6},{5,1},{6,4},{7,3},{8,10},{9,13},{10,... | collective-permute-start | bytes 196616 | tf_op jit(solution)/shard_map/ppermute | solution.py:413
  25.9 1.5 %collective-permute-start.9 = (f32[2,8,1024]{2,1,0:T(8,128)S(1)}, f32[2,8,1024]{2,1,0:T(8,128)S(1)}, u32[]{:S(2)}, u32[]{:S(2)}) collective-permute-start(f32[2,8,1024]{2,1,0:T(8,128)S(1)} %pad_maximum_fusion), channel_id=1, source_target_pairs={{0,6},{1,7},{2,4},{3,5},{4,2},{5,3},{6,0},{7,1},{8,14},{9,15},{10,... | collective-permute-start | bytes 196616 | tf_op jit(solution)/shard_map/ppermute | solution.py:414
  27.3 1.7 %collective-permute-done.7.refs_2_ = f32[2,8,1024]{2,1,0:T(8,128)S(1)} collective-permute-done((f32[2,8,1024]{2,1,0:T(8,128)S(1)}, f32[2,8,1024]{2,1,0:T(8,128)S(1)}, u32[]{:S(2)}, u32[]{:S(2)}) %collective-permute-start.7) | collective-permute-done | bytes 65568 | tf_op jit(solution)/shard_map/ppermute | solution.py:413
  29.0 2.0 %collective-permute-done.9.refs_4_ = f32[2,8,1024]{2,1,0:T(8,128)S(1)} collective-permute-done((f32[2,8,1024]{2,1,0:T(8,128)S(1)}, f32[2,8,1024]{2,1,0:T(8,128)S(1)}, u32[]{:S(2)}, u32[]{:S(2)}) %collective-permute-start.9) | collective-permute-done | bytes 65568 | tf_op jit(solution)/shard_map/ppermute | solution.py:414
  31.3 1.3 %collective-permute-start.13 = (f32[8,1024]{1,0:T(8,128)S(1)}, f32[8,1024]{1,0:T(8,128)S(1)}, u32[]{:S(2)}, u32[]{:S(2)}) collective-permute-start(f32[8,1024]{1,0:T(8,128)S(1)} %get-tuple-element.34.refs_5_), channel_id=1, source_target_pairs={{0,24},{8,16},{16,8},{24,0},{1,25},{9,17},{17,9},{25,1},{2,26},{10... | collective-permute-start | bytes 98312 | tf_op jit(solution)/shard_map/ppermute | solution.py:354
  33.4 1.7 %own_plane.4.refs_12_ = f32[3,3584]{1,0:T(4,128)S(1)} custom-call(f32[48,1024]{1,0:T(8,128)S(1)} %get-tuple-element.32.u_ref.refs_1_, s32[1,3584]{1,0:T(1,128)S(1)} %reshape.17.cell_ref.refs_8_, f32[3,3584]{1,0:T(4,128)S(1)} %copy-done), custom_call_target="tpu_custom_call" | custom-call | tf_op jit(solution)/shard_map/own_plane/pallas_call | solution.py:385
  35.1 1.9 %collective-permute-done.13.refs_7_ = f32[8,1024]{1,0:T(8,128)S(1)} collective-permute-done((f32[8,1024]{1,0:T(8,128)S(1)}, f32[8,1024]{1,0:T(8,128)S(1)}, u32[]{:S(2)}, u32[]{:S(2)}) %collective-permute-start.13) | collective-permute-done | bytes 32800 | tf_op jit(solution)/shard_map/ppermute | solution.py:354
  37.1 4.4 %section.4 = (f32[48,1024]{1,0:T(8,128)S(1)}, f32[8,1024]{1,0:T(8,128)S(1)}, f32[3,3584]{1,0:T(4,128)S(1)}) custom-call(s32[1,1,3]{2,1,0:T(1,128)S(1)} %copy-done.4, f32[48,1024]{1,0:T(8,128)S(1)} %get-tuple-element.32.u_ref.refs_1_, f32[3,1024]{1,0:T(4,128)S(1)} %get-tuple-element.33.refs_2_, f32[48,1024]{1,0:T(8,128)S(1)} %collective-permute-done.10.refs_3_, ...), custom_call_target="tpu_custom_call" | custom-call | tf_op jit(solution)/shard_map/section/pallas_call | solution.py:393
  41.6 2.1 %collective-permute-start.19 = (f32[48,1024]{1,0:T(8,128)S(1)}, f32[48,1024]{1,0:T(8,128)S(1)}, u32[]{:S(2)}, u32[]{:S(2)}) collective-permute-start(f32[48,1024]{1,0:T(8,128)S(1)} %get-tuple-element.37.refs_5_), channel_id=1, source_target_pairs={{0,24},{8,16},{16,8},{24,0},{1,25},{9,17},{17,9},{25,1},{2,26},{10... | collective-permute-start | bytes 589832 | tf_op jit(solution)/shard_map/ppermute | solution.py:354
  43.9 1.5 %collective-permute-start.15 = (f32[2,8,1024]{2,1,0:T(8,128)S(1)}, f32[2,8,1024]{2,1,0:T(8,128)S(1)}, u32[]{:S(2)}, u32[]{:S(2)}) collective-permute-start(f32[2,8,1024]{2,1,0:T(8,128)S(1)} %pad_maximum_fusion.1), channel_id=1, source_target_pairs={{0,2},{1,5},{2,0},{3,7},{4,6},{5,1},{6,4},{7,3},{8,10},{9,13},{10,... | collective-permute-start | bytes 196616 | tf_op jit(solution)/shard_map/ppermute | solution.py:413
  45.4 1.5 %collective-permute-start.17 = (f32[2,8,1024]{2,1,0:T(8,128)S(1)}, f32[2,8,1024]{2,1,0:T(8,128)S(1)}, u32[]{:S(2)}, u32[]{:S(2)}) collective-permute-start(f32[2,8,1024]{2,1,0:T(8,128)S(1)} %pad_maximum_fusion.1), channel_id=1, source_target_pairs={{0,6},{1,7},{2,4},{3,5},{4,2},{5,3},{6,0},{7,1},{8,14},{9,15},{10,... | collective-permute-start | bytes 196616 | tf_op jit(solution)/shard_map/ppermute | solution.py:414
  46.9 1.8 %collective-permute-done.15.refs_2_ = f32[2,8,1024]{2,1,0:T(8,128)S(1)} collective-permute-done((f32[2,8,1024]{2,1,0:T(8,128)S(1)}, f32[2,8,1024]{2,1,0:T(8,128)S(1)}, u32[]{:S(2)}, u32[]{:S(2)}) %collective-permute-start.15) | collective-permute-done | bytes 65568 | tf_op jit(solution)/shard_map/ppermute | solution.py:413
  48.8 1.8 %collective-permute-done.17.refs_4_ = f32[2,8,1024]{2,1,0:T(8,128)S(1)} collective-permute-done((f32[2,8,1024]{2,1,0:T(8,128)S(1)}, f32[2,8,1024]{2,1,0:T(8,128)S(1)}, u32[]{:S(2)}, u32[]{:S(2)}) %collective-permute-start.17) | collective-permute-done | bytes 65568 | tf_op jit(solution)/shard_map/ppermute | solution.py:414
  50.8 1.7 %collective-permute-start.21 = (f32[8,1024]{1,0:T(8,128)S(1)}, f32[8,1024]{1,0:T(8,128)S(1)}, u32[]{:S(2)}, u32[]{:S(2)}) collective-permute-start(f32[8,1024]{1,0:T(8,128)S(1)} %get-tuple-element.40.refs_5_), channel_id=1, source_target_pairs={{0,24},{8,16},{16,8},{24,0},{1,25},{9,17},{17,9},{25,1},{2,26},{10... | collective-permute-start | bytes 98312 | tf_op jit(solution)/shard_map/ppermute | solution.py:354
  52.5 1.1 %collective-permute-start.20 = (f32[8,1024]{1,0:T(8,128)S(1)}, f32[8,1024]{1,0:T(8,128)S(1)}, u32[]{:S(2)}, u32[]{:S(2)}) collective-permute-start(f32[8,1024]{1,0:T(8,128)S(1)} %get-tuple-element.40.refs_5_), channel_id=1, source_target_pairs={{0,8},{8,0},{16,24},{24,16},{1,9},{9,1},{17,25},{25,17},{2,10},{10... | collective-permute-start | bytes 98312 | tf_op jit(solution)/shard_map/ppermute | solution.py:355
  53.6 1.9 %own_plane.5.refs_12_ = f32[3,3584]{1,0:T(4,128)S(1)} custom-call(f32[48,1024]{1,0:T(8,128)S(1)} %get-tuple-element.38.u_ref.refs_1_, s32[1,3584]{1,0:T(1,128)S(1)} %reshape.17.cell_ref.refs_8_, f32[3,3584]{1,0:T(4,128)S(1)} %copy-done), custom_call_target="tpu_custom_call" | custom-call | tf_op jit(solution)/shard_map/own_plane/pallas_call | solution.py:385
  55.5 1.2 %collective-permute-done.21.refs_7_ = f32[8,1024]{1,0:T(8,128)S(1)} collective-permute-done((f32[8,1024]{1,0:T(8,128)S(1)}, f32[8,1024]{1,0:T(8,128)S(1)}, u32[]{:S(2)}, u32[]{:S(2)}) %collective-permute-start.21) | collective-permute-done | bytes 32800 | tf_op jit(solution)/shard_map/ppermute | solution.py:354
  56.8 4.4 %section.5 = (f32[48,1024]{1,0:T(8,128)S(1)}, f32[8,1024]{1,0:T(8,128)S(1)}, f32[3,3584]{1,0:T(4,128)S(1)}, f32[3,512]{1,0:T(4,128)S(1)}, f32[3,1024]{1,0:T(4,128)S(1)}) custom-call(s32[1,1,3]{2,1,0:T(1,128)S(1)} %copy-done.4, f32[48,1024]{1,0:T(8,128)S(1)} %get-tuple-element.38.u_ref.refs_1_, f32[3,1024]{1,0:T(4,128)S(1)} %get-tuple-element.39.refs_2_, ...), custom_call_target="tpu_custom_call" | custom-call | tf_op jit(solution)/shard_map/section/pallas_call | solution.py:393
  61.3 1.2 %collective-permute-done.22.refs_1_ = f32[8,1024]{1,0:T(8,128)S(1)} collective-permute-done((f32[8,1024]{1,0:T(8,128)S(1)}, f32[8,1024]{1,0:T(8,128)S(1)}, u32[]{:S(2)}, u32[]{:S(2)}) %collective-permute-start.22) | collective-permute-done | bytes 32800 | tf_op jit(solution)/shard_map/ppermute | solution.py:411
  62.5 1.0 %collective-permute-start.23 = (f32[2,8,1024]{2,1,0:T(8,128)S(1)}, f32[2,8,1024]{2,1,0:T(8,128)S(1)}, u32[]{:S(2)}, u32[]{:S(2)}) collective-permute-start(f32[2,8,1024]{2,1,0:T(8,128)S(1)} %pad_maximum_fusion.2), channel_id=1, source_target_pairs={{0,2},{1,5},{2,0},{3,7},{4,6},{5,1},{6,4},{7,3},{8,10},{9,13},{10,... | collective-permute-start | bytes 196616 | tf_op jit(solution)/shard_map/ppermute | solution.py:413
  63.5 0.9 %collective-permute-start.25 = (f32[3,1024]{1,0:T(4,128)S(1)}, f32[3,1024]{1,0:T(4,128)S(1)}, u32[]{:S(2)}, u32[]{:S(2)}) collective-permute-start(f32[3,1024]{1,0:T(4,128)S(1)} %get-tuple-element.44), channel_id=1, source_target_pairs={{0,7},{1,2},{2,1},{3,4},{4,3},{5,6},{6,5},{7,0},{8,15},{9,10},{10,... | collective-permute-start | bytes 36872 | tf_op jit(solution)/shard_map/ppermute | solution.py:409
  65.1 1.1 %collective-permute-start.27 = (f32[2,8,1024]{2,1,0:T(8,128)S(1)}, f32[2,8,1024]{2,1,0:T(8,128)S(1)}, u32[]{:S(2)}, u32[]{:S(2)}) collective-permute-start(f32[2,8,1024]{2,1,0:T(8,128)S(1)} %pad_maximum_fusion.2), channel_id=1, source_target_pairs={{0,6},{1,7},{2,4},{3,5},{4,2},{5,3},{6,0},{7,1},{8,14},{9,15},{10,... | collective-permute-start | bytes 196616 | tf_op jit(solution)/shard_map/ppermute | solution.py:414
  66.2 3.6 %collective-permute-done.24.refs_8_ = f32[3,512]{1,0:T(4,128)S(1)} collective-permute-done((f32[3,512]{1,0:T(4,128)S(1)}, f32[3,512]{1,0:T(4,128)S(1)}, u32[]{:S(2)}, u32[]{:S(2)}) %collective-permute-start.24) | collective-permute-done | bytes 6176 | tf_op jit(solution)/shard_map/ppermute | solution.py:407
  (66 shorter events, 7.6 us)
Async XLA Ops:
  0.6 15.3 %collective-permute-start.2 = (f32[48,1024]{1,0:T(8,128)}, f32[48,1024]{1,0:T(8,128)S(1)}, u32[]{:S(2)}, u32[]{:S(2)}) collective-permute-start(f32[48,1024]{1,0:T(8,128)} %bitcast.16), channel_id=1, source_target_pairs={{0,24},{8,16},{16,8},{24,0},{1,25},{9,17},{17,9},{25,1},{2,26},{10... | collective-permute-start | bytes 589832 | tf_op jit(solution)/shard_map/ppermute | solution.py:354
  5.7 10.1 %collective-permute-start.1 = (f32[48,1024]{1,0:T(8,128)}, f32[48,1024]{1,0:T(8,128)S(1)}, u32[]{:S(2)}, u32[]{:S(2)}) collective-permute-start(f32[48,1024]{1,0:T(8,128)} %bitcast.17), channel_id=1, source_target_pairs={{0,8},{8,0},{16,24},{24,16},{1,9},{9,1},{17,25},{25,17},{2,10},{10... | collective-permute-start | bytes 589832 | tf_op jit(solution)/shard_map/ppermute | solution.py:355
  6.7 4.9 %copy-start.9 = (s32[3584]{0:T(1024)S(1)}, s32[3584]{0:T(1024)}, u32[]{:S(2)}) copy-start(s32[3584]{0:T(1024)} %param.16) | copy-start | bytes 43012
  6.7 4.9 %copy-start = (f32[3,3584]{1,0:T(4,128)S(1)}, f32[3,3584]{1,0:T(4,128)}, u32[]{:S(2)}) copy-start(f32[3,3584]{1,0:T(4,128)} %refs_9_.5) | copy-start | bytes 129028
  6.8 3.1 %collective-permute-start.3 = (f32[3,1024]{1,0:T(4,128)S(1)}, f32[3,1024]{1,0:T(4,128)S(1)}, u32[]{:S(2)}, u32[]{:S(2)}) collective-permute-start(f32[3,1024]{1,0:T(4,128)S(1)} %bitcast.27), channel_id=1, source_target_pairs={{1,0},{2,1},{3,2},{4,3},{5,4},{6,5},{7,6},{0,7},{9,8},{10,9},{11,1... | collective-permute-start | bytes 36872 | tf_op jit(solution)/shard_map/ppermute | solution.py:367
  8.4 6.8 %collective-permute-start = (f32[3,1024]{1,0:T(4,128)S(1)}, f32[3,1024]{1,0:T(4,128)S(1)}, u32[]{:S(2)}, u32[]{:S(2)}) collective-permute-start(f32[3,1024]{1,0:T(4,128)S(1)} %bitcast.26), channel_id=1, source_target_pairs={{0,1},{1,2},{2,3},{3,4},{4,5},{5,6},{6,7},{7,0},{8,9},{9,10},{10,1... | collective-permute-start | bytes 36872 | tf_op jit(solution)/shard_map/ppermute | solution.py:368
  9.9 5.7 %collective-permute-start.5 = (f32[3,1024]{1,0:T(4,128)S(1)}, f32[3,1024]{1,0:T(4,128)S(1)}, u32[]{:S(2)}, u32[]{:S(2)}) collective-permute-start(f32[3,1024]{1,0:T(4,128)S(1)} %collective-permute-done.3.refs_5_), channel_id=1, source_target_pairs={{0,24},{8,16},{16,8},{24,0},{1,25},{9,17},{17,9},{25,1},{2,26},{10... | collective-permute-start | bytes 36872 | tf_op jit(solution)/shard_map/ppermute | solution.py:354
  10.5 5.4 %collective-permute-start.4 = (f32[3,1024]{1,0:T(4,128)S(1)}, f32[3,1024]{1,0:T(4,128)S(1)}, u32[]{:S(2)}, u32[]{:S(2)}) collective-permute-start(f32[3,1024]{1,0:T(4,128)S(1)} %collective-permute-done.3.refs_5_), channel_id=1, source_target_pairs={{0,8},{8,0},{16,24},{24,16},{1,9},{9,1},{17,25},{25,17},{2,10},{10... | collective-permute-start | bytes 36872 | tf_op jit(solution)/shard_map/ppermute | solution.py:355
  12.6 3.3 %copy-start.2 = (f32[3,1,16,1024]{3,2,1,0:T(8,128)S(1)}, f32[3,1,16,1024]{3,2,1,0:T(8,128)}, u32[]{:S(2)}) copy-start(f32[3,1,16,1024]{3,2,1,0:T(8,128)} %param.10) | copy-start | bytes 589828
  20.8 3.5 %collective-permute-start.6 = (f32[8,1024]{1,0:T(8,128)S(1)}, f32[8,1024]{1,0:T(8,128)S(1)}, u32[]{:S(2)}, u32[]{:S(2)}) collective-permute-start(f32[8,1024]{1,0:T(8,128)S(1)} %get-tuple-element.30.refs_0_), channel_id=1, source_target_pairs={{0,1},{1,0},{2,3},{3,2},{4,5},{5,4},{6,7},{7,6},{8,9},{9,8},{10,11... | collective-permute-start | bytes 98312 | tf_op jit(solution)/shard_map/ppermute | solution.py:411
  20.9 16.2 %collective-permute-start.11 = (f32[48,1024]{1,0:T(8,128)S(1)}, f32[48,1024]{1,0:T(8,128)S(1)}, u32[]{:S(2)}, u32[]{:S(2)}) collective-permute-start(f32[48,1024]{1,0:T(8,128)S(1)} %get-tuple-element.31.refs_5_), channel_id=1, source_target_pairs={{0,24},{8,16},{16,8},{24,0},{1,25},{9,17},{17,9},{25,1},{2,26},{10... | collective-permute-start | bytes 589832 | tf_op jit(solution)/shard_map/ppermute | solution.py:354
  24.3 12.8 %collective-permute-start.10 = (f32[48,1024]{1,0:T(8,128)S(1)}, f32[48,1024]{1,0:T(8,128)S(1)}, u32[]{:S(2)}, u32[]{:S(2)}) collective-permute-start(f32[48,1024]{1,0:T(8,128)S(1)} %get-tuple-element.31.refs_5_), channel_id=1, source_target_pairs={{0,8},{8,0},{16,24},{24,16},{1,9},{9,1},{17,25},{25,17},{2,10},{10... | collective-permute-start | bytes 589832 | tf_op jit(solution)/shard_map/ppermute | solution.py:355
  24.3 4.7 %collective-permute-start.7 = (f32[2,8,1024]{2,1,0:T(8,128)S(1)}, f32[2,8,1024]{2,1,0:T(8,128)S(1)}, u32[]{:S(2)}, u32[]{:S(2)}) collective-permute-start(f32[2,8,1024]{2,1,0:T(8,128)S(1)} %pad_maximum_fusion), channel_id=1, source_target_pairs={{0,2},{1,5},{2,0},{3,7},{4,6},{5,1},{6,4},{7,3},{8,10},{9,13},{10,... | collective-permute-start | bytes 196616 | tf_op jit(solution)/shard_map/ppermute | solution.py:413
  25.9 5.2 %collective-permute-start.9 = (f32[2,8,1024]{2,1,0:T(8,128)S(1)}, f32[2,8,1024]{2,1,0:T(8,128)S(1)}, u32[]{:S(2)}, u32[]{:S(2)}) collective-permute-start(f32[2,8,1024]{2,1,0:T(8,128)S(1)} %pad_maximum_fusion), channel_id=1, source_target_pairs={{0,6},{1,7},{2,4},{3,5},{4,2},{5,3},{6,0},{7,1},{8,14},{9,15},{10,... | collective-permute-start | bytes 196616 | tf_op jit(solution)/shard_map/ppermute | solution.py:414
  29.0 2.0 %collective-permute-start.8 = (f32[2,8,1024]{2,1,0:T(8,128)S(1)}, f32[2,8,1024]{2,1,0:T(8,128)S(1)}, u32[]{:S(2)}, u32[]{:S(2)}) collective-permute-start(f32[2,8,1024]{2,1,0:T(8,128)S(1)} %collective-permute-done.7.refs_2_), channel_id=1, source_target_pairs={{0,1},{1,0},{2,3},{3,2},{4,5},{5,4},{6,7},{7,6},{8,9},{9,8},{10,11... | collective-permute-start | bytes 196616 | tf_op jit(solution)/shard_map/ppermute | solution.py:417
  31.3 5.8 %collective-permute-start.13 = (f32[8,1024]{1,0:T(8,128)S(1)}, f32[8,1024]{1,0:T(8,128)S(1)}, u32[]{:S(2)}, u32[]{:S(2)}) collective-permute-start(f32[8,1024]{1,0:T(8,128)S(1)} %get-tuple-element.34.refs_5_), channel_id=1, source_target_pairs={{0,24},{8,16},{16,8},{24,0},{1,25},{9,17},{17,9},{25,1},{2,26},{10... | collective-permute-start | bytes 98312 | tf_op jit(solution)/shard_map/ppermute | solution.py:354
  32.6 4.5 %collective-permute-start.12 = (f32[8,1024]{1,0:T(8,128)S(1)}, f32[8,1024]{1,0:T(8,128)S(1)}, u32[]{:S(2)}, u32[]{:S(2)}) collective-permute-start(f32[8,1024]{1,0:T(8,128)S(1)} %get-tuple-element.34.refs_5_), channel_id=1, source_target_pairs={{0,8},{8,0},{16,24},{24,16},{1,9},{9,1},{17,25},{25,17},{2,10},{10... | collective-permute-start | bytes 98312 | tf_op jit(solution)/shard_map/ppermute | solution.py:355
  41.5 2.4 %collective-permute-start.14 = (f32[8,1024]{1,0:T(8,128)S(1)}, f32[8,1024]{1,0:T(8,128)S(1)}, u32[]{:S(2)}, u32[]{:S(2)}) collective-permute-start(f32[8,1024]{1,0:T(8,128)S(1)} %get-tuple-element.36.refs_0_), channel_id=1, source_target_pairs={{0,1},{1,0},{2,3},{3,2},{4,5},{5,4},{6,7},{7,6},{8,9},{9,8},{10,11... | collective-permute-start | bytes 98312 | tf_op jit(solution)/shard_map/ppermute | solution.py:411
  41.6 15.1 %collective-permute-start.19 = (f32[48,1024]{1,0:T(8,128)S(1)}, f32[48,1024]{1,0:T(8,128)S(1)}, u32[]{:S(2)}, u32[]{:S(2)}) collective-permute-start(f32[48,1024]{1,0:T(8,128)S(1)} %get-tuple-element.37.refs_5_), channel_id=1, source_target_pairs={{0,24},{8,16},{16,8},{24,0},{1,25},{9,17},{17,9},{25,1},{2,26},{10... | collective-permute-start | bytes 589832 | tf_op jit(solution)/shard_map/ppermute | solution.py:354
  43.7 13.1 %collective-permute-start.18 = (f32[48,1024]{1,0:T(8,128)S(1)}, f32[48,1024]{1,0:T(8,128)S(1)}, u32[]{:S(2)}, u32[]{:S(2)}) collective-permute-start(f32[48,1024]{1,0:T(8,128)S(1)} %get-tuple-element.37.refs_5_), channel_id=1, source_target_pairs={{0,8},{8,0},{16,24},{24,16},{1,9},{9,1},{17,25},{25,17},{2,10},{10... | collective-permute-start | bytes 589832 | tf_op jit(solution)/shard_map/ppermute | solution.py:355
  43.9 4.9 %collective-permute-start.15 = (f32[2,8,1024]{2,1,0:T(8,128)S(1)}, f32[2,8,1024]{2,1,0:T(8,128)S(1)}, u32[]{:S(2)}, u32[]{:S(2)}) collective-permute-start(f32[2,8,1024]{2,1,0:T(8,128)S(1)} %pad_maximum_fusion.1), channel_id=1, source_target_pairs={{0,2},{1,5},{2,0},{3,7},{4,6},{5,1},{6,4},{7,3},{8,10},{9,13},{10,... | collective-permute-start | bytes 196616 | tf_op jit(solution)/shard_map/ppermute | solution.py:413
  45.4 5.2 %collective-permute-start.17 = (f32[2,8,1024]{2,1,0:T(8,128)S(1)}, f32[2,8,1024]{2,1,0:T(8,128)S(1)}, u32[]{:S(2)}, u32[]{:S(2)}) collective-permute-start(f32[2,8,1024]{2,1,0:T(8,128)S(1)} %pad_maximum_fusion.1), channel_id=1, source_target_pairs={{0,6},{1,7},{2,4},{3,5},{4,2},{5,3},{6,0},{7,1},{8,14},{9,15},{10,... | collective-permute-start | bytes 196616 | tf_op jit(solution)/shard_map/ppermute | solution.py:414
  48.8 1.8 %collective-permute-start.16 = (f32[2,8,1024]{2,1,0:T(8,128)S(1)}, f32[2,8,1024]{2,1,0:T(8,128)S(1)}, u32[]{:S(2)}, u32[]{:S(2)}) collective-permute-start(f32[2,8,1024]{2,1,0:T(8,128)S(1)} %collective-permute-done.15.refs_2_), channel_id=1, source_target_pairs={{0,1},{1,0},{2,3},{3,2},{4,5},{5,4},{6,7},{7,6},{8,9},{9,8},{10,11... | collective-permute-start | bytes 196616 | tf_op jit(solution)/shard_map/ppermute | solution.py:417
  50.8 5.9 %collective-permute-start.21 = (f32[8,1024]{1,0:T(8,128)S(1)}, f32[8,1024]{1,0:T(8,128)S(1)}, u32[]{:S(2)}, u32[]{:S(2)}) collective-permute-start(f32[8,1024]{1,0:T(8,128)S(1)} %get-tuple-element.40.refs_5_), channel_id=1, source_target_pairs={{0,24},{8,16},{16,8},{24,0},{1,25},{9,17},{17,9},{25,1},{2,26},{10... | collective-permute-start | bytes 98312 | tf_op jit(solution)/shard_map/ppermute | solution.py:354
  52.5 4.3 %collective-permute-start.20 = (f32[8,1024]{1,0:T(8,128)S(1)}, f32[8,1024]{1,0:T(8,128)S(1)}, u32[]{:S(2)}, u32[]{:S(2)}) collective-permute-start(f32[8,1024]{1,0:T(8,128)S(1)} %get-tuple-element.40.refs_5_), channel_id=1, source_target_pairs={{0,8},{8,0},{16,24},{24,16},{1,9},{9,1},{17,25},{25,17},{2,10},{10... | collective-permute-start | bytes 98312 | tf_op jit(solution)/shard_map/ppermute | solution.py:355
  61.2 1.3 %collective-permute-start.22 = (f32[8,1024]{1,0:T(8,128)S(1)}, f32[8,1024]{1,0:T(8,128)S(1)}, u32[]{:S(2)}, u32[]{:S(2)}) collective-permute-start(f32[8,1024]{1,0:T(8,128)S(1)} %get-tuple-element.42.refs_0_), channel_id=1, source_target_pairs={{0,1},{1,0},{2,3},{3,2},{4,5},{5,4},{6,7},{7,6},{8,9},{9,8},{10,11... | collective-permute-start | bytes 98312 | tf_op jit(solution)/shard_map/ppermute | solution.py:411
  62.5 7.4 %collective-permute-start.23 = (f32[2,8,1024]{2,1,0:T(8,128)S(1)}, f32[2,8,1024]{2,1,0:T(8,128)S(1)}, u32[]{:S(2)}, u32[]{:S(2)}) collective-permute-start(f32[2,8,1024]{2,1,0:T(8,128)S(1)} %pad_maximum_fusion.2), channel_id=1, source_target_pairs={{0,2},{1,5},{2,0},{3,7},{4,6},{5,1},{6,4},{7,3},{8,10},{9,13},{10,... | collective-permute-start | bytes 196616 | tf_op jit(solution)/shard_map/ppermute | solution.py:413
  63.5 6.4 %collective-permute-start.25 = (f32[3,1024]{1,0:T(4,128)S(1)}, f32[3,1024]{1,0:T(4,128)S(1)}, u32[]{:S(2)}, u32[]{:S(2)}) collective-permute-start(f32[3,1024]{1,0:T(4,128)S(1)} %get-tuple-element.44), channel_id=1, source_target_pairs={{0,7},{1,2},{2,1},{3,4},{4,3},{5,6},{6,5},{7,0},{8,15},{9,10},{10,... | collective-permute-start | bytes 36872 | tf_op jit(solution)/shard_map/ppermute | solution.py:409
  64.4 5.4 %collective-permute-start.24 = (f32[3,512]{1,0:T(4,128)S(1)}, f32[3,512]{1,0:T(4,128)S(1)}, u32[]{:S(2)}, u32[]{:S(2)}) collective-permute-start(f32[3,512]{1,0:T(4,128)S(1)} %get-tuple-element.43), channel_id=1, source_target_pairs={{0,8},{8,16},{16,24},{24,0},{1,9},{9,17},{17,25},{25,1},{2,10},{10... | collective-permute-start | bytes 18440 | tf_op jit(solution)/shard_map/ppermute | solution.py:407
  65.1 6.1 %collective-permute-start.27 = (f32[2,8,1024]{2,1,0:T(8,128)S(1)}, f32[2,8,1024]{2,1,0:T(8,128)S(1)}, u32[]{:S(2)}, u32[]{:S(2)}) collective-permute-start(f32[2,8,1024]{2,1,0:T(8,128)S(1)} %pad_maximum_fusion.2), channel_id=1, source_target_pairs={{0,6},{1,7},{2,4},{3,5},{4,2},{5,3},{6,0},{7,1},{8,14},{9,15},{10,... | collective-permute-start | bytes 196616 | tf_op jit(solution)/shard_map/ppermute | solution.py:414
  69.9 1.4 %collective-permute-start.26 = (f32[2,8,1024]{2,1,0:T(8,128)S(1)}, f32[2,8,1024]{2,1,0:T(8,128)S(1)}, u32[]{:S(2)}, u32[]{:S(2)}) collective-permute-start(f32[2,8,1024]{2,1,0:T(8,128)S(1)} %collective-permute-done.23.refs_2_), channel_id=1, source_target_pairs={{0,1},{1,0},{2,3},{3,2},{4,5},{5,4},{6,7},{7,6},{8,9},{9,8},{10,11... | collective-permute-start | bytes 196616 | tf_op jit(solution)/shard_map/ppermute | solution.py:417
  69.9 1.3 %collective-permute-start.28 = (f32[3,1024]{1,0:T(4,128)S(1)}, f32[3,1024]{1,0:T(4,128)S(1)}, u32[]{:S(2)}, u32[]{:S(2)}) collective-permute-start(f32[3,1024]{1,0:T(4,128)S(1)} %get-tuple-element.44), channel_id=1, source_target_pairs={{0,1},{1,0},{2,3},{3,2},{4,5},{5,4},{6,7},{7,6},{8,9},{9,8},{10,11... | collective-permute-start | bytes 36872 | tf_op jit(solution)/shard_map/ppermute | solution.py:408
  (8 other events, 15.1 us)

commit v4 on v3

--- a/solution.py
+++ b/solution.py
@@ -61,16 +61,25 @@
     return jnp.concatenate(parts, axis=0)
 
 
-def down(row, depth):
+def down(row):
     width = row.shape[1]
     order = lax.broadcasted_iota(jnp.int32, (width, DEPTH), 1).astype(F32).astype(BF16)
-    one, none = jnp.ones((), BF16), jnp.zeros((), BF16)
     column = jnp.broadcast_to(row, (8, width)).T[:, 0:1]
+    wanted = jnp.broadcast_to(column, (width, DEPTH)).astype(BF16)
+    return jnp.where(order == wanted, jnp.ones((), BF16), jnp.zeros((), BF16))
+
+
+def spread_out(values, group, groups):
+    width = group.shape[1]
+    shape = (groups // 16, 16, width)
+    order = lax.broadcasted_iota(jnp.int32, shape, 0) * 16 + lax.broadcasted_iota(jnp.int32, shape, 1)
+    order = order.astype(F32).astype(BF16)
+    hit = order == jnp.broadcast_to(group.astype(F32), (16, width)).astype(BF16)[None]
     parts = []
-    for k in range(depth // DEPTH):
-        wanted = jnp.broadcast_to(column - float(DEPTH * k), (width, DEPTH)).astype(BF16)
-        parts.append(jnp.where(order == wanted, one, none))
-    return jnp.concatenate(parts, axis=1)
+    for value in values:
+        value = jnp.broadcast_to(value, (16, width)).astype(BF16)[None]
+        parts.append(jnp.where(hit, value, jnp.zeros((), BF16)).reshape(groups, width))
+    return jnp.concatenate(parts, axis=0)
 
 
 def split_rows(rows):
@@ -88,7 +97,18 @@
     return near * (1.0 - fz) + far * fz
 
 
-def tables_kernel(down_ref, up_ref, scale_ref, metric_ref, matrix_ref, answer_ref, scal_ref):
+def tables_kernel(
+    down_ref, up_ref, scale_ref, metric_ref, count_ref, matrix_ref, answer_ref, scal_ref, live_ref
+):
+    slot = lax.broadcasted_iota(jnp.int32, live_ref.shape, 1)
+    remain = slot - RESIDENT
+    heading = remain // CAP
+    limit = jnp.where(
+        heading <= 0,
+        count_ref[0, 0, 0],
+        jnp.where(heading == 1, count_ref[0, 0, 1], count_ref[0, 0, 2]),
+    )
+    live_ref[...] = jnp.where((remain < 0) | (remain % CAP < limit), 1.0, 0.0)
     sections, rows = down_ref.shape
     lane = lax.broadcasted_iota(jnp.int32, (1, 128), 1)
     at = lambda place: jnp.where(lane == place, 1.0, 0.0)
@@ -141,16 +161,16 @@
     first = number == 0
     refs = list(refs)
     take = lambda count: [refs.pop(0) for _ in range(count)]
-    count_ref, u_ref, ym_ref, near_x_ref, far_x_ref, yp_ref, near_ef_ref, far_ef_ref = take(8)
-    cell_ref, off_ref, tau_ref, v_ref, near_ref, matrix_ref, answer_ref, scal_ref = take(8)
+    u_ref, ym_ref, near_x_ref, far_x_ref, yp_ref, near_ef_ref, far_ef_ref = take(7)
+    cell_ref, off_ref, tau_ref, live_ref, v_ref, near_ref, matrix_ref, answer_ref, scal_ref = take(9)
     w_ref, pq_ref, v_out_ref = take(3)
-    if last:
-        leaving_x_ref, leaving_y_ref = take(2)
+    leaving_ref = refs.pop(0) if last else None
     table_ref, spread_ref, chosen_ref = refs
 
     cells_z = u_ref.shape[1]
     rows = u_ref.shape[0] // COMPS
     count = COMPS * rows
+    groups = rows * (cells_z // DEPTH)
     position = lax.axis_index("gy")
     top = jnp.where(position == lax.axis_size("gy") - 1, 0.0, 1.0).astype(F32)
     bottom = jnp.where(position == 0, 0.0, 1.0).astype(F32)
@@ -189,25 +209,17 @@
     for t in range(cell_ref.shape[1] // TILE):
         here = slice(t * TILE, (t + 1) * TILE)
         cell = cell_ref[:, here]
-        row, column = cell // cells_z, (cell % cells_z).astype(F32)
+        row, place = cell // cells_z, cell % cells_z
+        column = place.astype(F32)
         fx, fy, fz = (off_ref[d : d + 1, here] for d in range(3))
         found = jnp.dot(table_ref[...], across(column, cells_z), preferred_element_type=F32)
-        chosen_ref[here, :] = down(column, cells_z)
+        chosen_ref[here, :] = down((place % DEPTH).astype(F32))
         blended = blend_z(found, fz)
-        at_row = order == row
-        weight = jnp.where(at_row, 1.0 - fy, jnp.where(order == row + 1, fy, 0.0)) * fx
+        weight = jnp.where(order == row, 1.0 - fy, jnp.where(order == row + 1, fy, 0.0)) * fx
         edge = jnp.where(row == rows - 1, fy, 0.0)
-        slot = t * TILE + lax.broadcasted_iota(jnp.int32, (1, TILE), 1)
-        remain = slot - RESIDENT
-        heading = remain // CAP
-        limit = jnp.where(
-            heading <= 0,
-            count_ref[0, 0, 0],
-            jnp.where(heading == 1, count_ref[0, 0, 1], count_ref[0, 0, 2]),
-        )
-        live = jnp.where((remain < 0) | (remain % CAP < limit), 1.0, 0.0)
+        live = live_ref[:, here]
         tau = tau_ref[:, here]
-        spread = []
+        pushes = []
         for c in range(COMPS):
             part = jnp.sum(blended[rows * c : rows * (c + 1)] * weight, axis=0, keepdims=True)
             side = blended[count + c : count + c + 1] * (1.0 - fx)
@@ -217,10 +229,10 @@
             drag = tau * (fluid - v)
             v = v + step * drag
             v_out_ref[c : c + 1, here] = v * live if last else v
-            spread.append(jnp.where(at_row, drag * live * (-COUPLING), 0.0))
-        spread = jnp.concatenate(spread, axis=0)
-        high = spread.astype(BF16).astype(F32)
-        spread_ref[:, here] = jnp.concatenate([high, spread - high], axis=0).astype(BF16)
+            pushes.append(drag * live * (-COUPLING))
+        high = [push.astype(BF16).astype(F32) for push in pushes]
+        low = [push - part for push, part in zip(pushes, high)]
+        spread_ref[:, here] = spread_out(high + low, place // DEPTH * rows + row, groups)
     pushed = jnp.dot(spread_ref[...], chosen_ref[...], preferred_element_type=F32)
 
     u = u_ref[...]
@@ -237,7 +249,11 @@
         convection = -(
             u[:rows] * slope_x[own] + u[rows : 2 * rows] * slope_y + u[2 * rows :] * slope_z[own]
         )
-        force = pushed[own] + pushed[count + rows * c : count + rows * (c + 1)]
+        pieces = []
+        for k in range(cells_z // DEPTH):
+            high, low = (groups * (c + COMPS * i) + rows * k for i in range(2))
+            pieces.append(pushed[high : high + rows] + pushed[low : low + rows])
+        force = jnp.concatenate(pieces, axis=1)
         rhs.append(field + step * (convection + force))
     solved = jnp.dot(
         matrix_ref[number, :, 0:count],
@@ -249,11 +265,19 @@
     pq_ref[0:COMPS, :] = solved[count : count + COMPS]
     for c in range(COMPS):
         pq_ref[COMPS + c : COMPS + c + 1, :] = solved[rows * c : rows * c + 1]
-    pq_ref[6:8, :] = jnp.zeros((2, cells_z), F32)
-    pq_ref[6:8, 0:128] = scal_ref[number]
+    pq_ref[6:, :] = jnp.zeros((pq_ref.shape[0] - 6, cells_z), F32)
+    if first:
+        for k in range(scal_ref.shape[0]):
+            pq_ref[6:8, 128 * k : 128 * (k + 1)] = scal_ref[k]
     if last:
-        leaving_y_ref[...] = v_out_ref[:, RESIDENT + CAP : RESIDENT + 3 * CAP]
-        leaving_x_ref[...] = v_out_ref[:, RESIDENT : RESIDENT + CAP]
+        leaving_ref[...] = v_out_ref[:, RESIDENT : RESIDENT + CAP]
+        lower = v_out_ref[:, RESIDENT + CAP : RESIDENT + 2 * CAP]
+        upper = v_out_ref[:, RESIDENT + 2 * CAP :]
+        even = position % 2 == 0
+        for place, part in ((6, jnp.where(even, lower, upper)), (8, jnp.where(even, upper, lower))):
+            pq_ref[place : place + 1, 0:CAP] = part[0:1]
+            pq_ref[place : place + 1, CAP : 2 * CAP] = part[1:2]
+            pq_ref[place + 1 : place + 2, 0:CAP] = part[2:3]
 
 
 def join_kernel(number, last, blocks, direct, *refs):
@@ -265,16 +289,20 @@
     else:
         (all_ref,) = take(1)
     w_ref, answer_ref = take(2)
+    if number > 0:
+        (known_ref,) = take(1)
     if last:
-        v_ref, from_x_ref, chip_ref, beside_ref, u_ref, moved_ref = take(6)
+        v_ref, from_x_ref, u_ref, moved_ref = take(4)
     else:
         u_ref, ef_ref, ym_ref = take(3)
+        if number == 0:
+            (known_ref,) = take(1)
     if direct:
         (all_ref,) = refs
         own_ref, partner_ref, side_ref, other_ref, far_ref = sources
         odd = here % 2 == 1
-        all_ref[here] = own_ref[...]
-        all_ref[here ^ 1] = partner_ref[...]
+        all_ref[here] = own_ref[0:8, :]
+        all_ref[here ^ 1] = partner_ref[0:8, :]
         near = here ^ jnp.where(odd, 4, 2)
         all_ref[near] = side_ref[0]
         all_ref[near ^ 1] = side_ref[1]
@@ -284,16 +312,19 @@
         all_ref[here ^ 6] = far_ref[0]
         all_ref[here ^ 7] = far_ref[1]
     rows = w_ref.shape[0] // COMPS
-
-    def scal(k, which, row=7):
-        return all_ref[k, row : row + 1, which : which + 1]
+    if number == 0:
+        known_ref[...] = all_ref[:, 6:8, 0 : known_ref.shape[2]]
+
+    def scal(k, which, row=1):
+        place = 128 * number + which
+        return known_ref[k, row : row + 1, place : place + 1]
 
     zero = jnp.zeros((COMPS, w_ref.shape[1]), F32)
     entering, own_in, at = zero, zero, []
     for k in range(blocks):
         at.append(entering)
         own_in = jnp.where(here == k, entering, own_in)
-        entering = all_ref[k, 0:COMPS, :] + scal(k, ENTER, 6) * entering
+        entering = all_ref[k, 0:COMPS, :] + scal(k, ENTER, 0) * entering
     leaving, own_out = zero, zero
     for k in reversed(range(blocks)):
         own_out = jnp.where(here == k, leaving, own_out)
@@ -310,13 +341,21 @@
         even = here % 2 == 0
         keep_above = jnp.where(here == blocks - 1, 0.0, 1.0).astype(F32)
         keep_below = jnp.where(here == 0, 0.0, 1.0).astype(F32)
-        chip, beside = chip_ref[...], beside_ref[...]
+        across_chips = jnp.where(even, below, jnp.minimum(here + 1, blocks - 1))
         moved_ref[:, :RESIDENT] = v_ref[:, :RESIDENT]
         moved_ref[:, RESIDENT : RESIDENT + CAP] = from_x_ref[...]
-        moved_ref[:, RESIDENT + CAP : RESIDENT + 2 * CAP] = (
-            jnp.where(even, chip, beside)[:, :CAP] * keep_above
-        )
-        moved_ref[:, RESIDENT + 2 * CAP :] = jnp.where(even, beside, chip)[:, CAP:] * keep_below
+        for c in range(COMPS):
+            row, lanes = c // 2, slice(CAP * (c % 2), CAP * (c % 2) + CAP)
+            beside = all_ref[across_chips, 6 + row : 7 + row, lanes]
+            if direct:
+                chip = partner_ref[8 + row : 9 + row, lanes]
+            else:
+                chip = all_ref[here ^ 1, 8 + row : 9 + row, lanes]
+            own = slice(c, c + 1)
+            moved_ref[own, RESIDENT + CAP : RESIDENT + 2 * CAP] = (
+                jnp.where(even, chip, beside) * keep_above
+            )
+            moved_ref[own, RESIDENT + 2 * CAP :] = jnp.where(even, beside, chip) * keep_below
     else:
         ef_ref[0:COMPS, :] = own_in
         ef_ref[COMPS : 2 * COMPS, :] = own_out
@@ -346,7 +385,11 @@
     size_x, size_y = lax.axis_size("gx"), lax.axis_size("gy")
     assert size_x % 2 == 0 and size_y % 2 == 0
     ring_x = [(i, (i + 1) % size_x) for i in range(size_x)]
-    next_to = [(i, (i + (1 if i % 2 else -1)) % size_y) for i in range(size_y)]
+    diagonal = [
+        ((x + 1) % size_x * size_y + (y + 1) % size_y, x * size_y + y)
+        for x in range(size_x)
+        for y in range(size_y)
+    ]
     same_pair = [(i, i ^ 1) for i in range(size_x)]
     next_pair = [(i, (i + (1 if i % 2 else -1)) % size_x) for i in range(size_x)]
 
@@ -366,17 +409,19 @@
     planes = both_sides(u)
     yp = lax.ppermute(first, "gy", back_y)
     ym = lax.ppermute(final, "gy", ring_y)
-    edges = both_sides(yp)
+    corner = lax.ppermute(first, ("gx", "gy"), diagonal)
+    edges = (corner, corner)
 
     cell = particle_cell.reshape(1, slots)
     tau = inverse_tau.reshape(1, slots)
     like = lambda *shape: jax.ShapeDtypeStruct(shape, F32)
-    matrix, answer, scal = call(
+    matrix, answer, scal, live = call(
         tables_kernel,
-        (like(SECTIONS, 56, 128), like(SECTIONS, cells_y, 128), like(SECTIONS, 2, 128)),
-        scalars(4),
+        (like(SECTIONS, 56, 128), like(SECTIONS, cells_y, 128), like(SECTIONS, 2, 128),
+         like(1, slots)),
+        scalars(5),
         "tables",
-    )(forward_rate, backward_rate, pivot_inv, y_metric)
+    )(forward_rate, backward_rate, pivot_inv, y_metric, outgoing_count)
     v = particle_vel
     rows = COMPS * cells_y
     field_like, slots_like = like(rows, cells_z), like(COMPS, slots)
@@ -392,39 +437,41 @@
         sides = (u, ym, *planes, yp, *edges)
         out = call(
             functools.partial(section_kernel, k, TIME_STEP * SECTION_WEIGHTS[k], last),
-            (field_like, like(8, cells_z), slots_like)
-            + ((like(COMPS, CAP), like(COMPS, 2 * CAP)) if last else ()),
-            scalars(1) + whole_in_vmem(len(sides) + 8),
+            (field_like, like(16 if last else 8, cells_z), slots_like)
+            + ((like(COMPS, CAP),) if last else ()),
+            whole_in_vmem(len(sides) + 9),
             "section",
             [
                 pltpu.VMEM((4 * (rows + 8), cells_z), BF16),
-                pltpu.VMEM((2 * rows, slots), BF16),
-                pltpu.VMEM((slots, cells_z), BF16),
+                pltpu.VMEM((2 * rows * (cells_z // DEPTH), slots), BF16),
+                pltpu.VMEM((slots, DEPTH), BF16),
             ],
-        )(outgoing_count, *sides, cell, particle_offset, tau, v, near, matrix, answer, scal)
+        )(*sides, cell, particle_offset, tau, live, v, near, matrix, answer, scal)
         w, pq, v = out[:3]
         if last:
             from_x = lax.ppermute(out[3], "gx", ring_x)
-            chip = lax.ppermute(out[4], "gy", flip(1))
-            beside = lax.ppermute(out[4], "gy", next_to)
         if direct:
             partner = lax.ppermute(pq, "gy", flip(1))
-            pair = jnp.stack([pq, partner])
+            pair = jnp.stack([pq[:8], partner[:8]])
             side = lax.ppermute(pair, "gy", mixed)
             far = lax.ppermute(pair, "gy", flip(6))
             if last:
-                side, from_x, beside = lax.optimization_barrier((side, from_x, beside))
+                side, from_x = lax.optimization_barrier((side, from_x))
             other = lax.ppermute(side, "gy", flip(1))
             gathered = (pq, partner, side, other, far)
-            scratch = [pltpu.VMEM((size_y,) + pq.shape, F32)]
+            scratch = [pltpu.VMEM((size_y, 8, cells_z), F32)]
         else:
             gathered = (lax.all_gather(pq, "gy", axis=0),)
             scratch = []
         if last:
-            more, shapes = (v, from_x, chip, beside), (field_like, slots_like)
+            more, shapes = (v, from_x), (field_like, slots_like)
         else:
             planes = both_sides(w)
             more, shapes = (), (field_like, like(8, cells_z), like(COMPS, cells_z))
+        if k == 0:
+            shapes = shapes + (like(size_y, 2, 128 * SECTIONS),)
+        else:
+            more = (known,) + more
         joined = call(
             functools.partial(join_kernel, k, last, size_y, direct),
             shapes,
@@ -433,7 +480,9 @@
             scratch,
         )(*gathered, w, answer, *more)
         if not last:
-            u, yp, ym = joined
+            u, yp, ym = joined[:3]
+            if k == 0:
+                known = joined[3]
             edges = both_sides(yp)
     u, moved = joined
     return (u.reshape(velocity.shape), moved)

time: 72.3 us -> 68.1 us (0.942)
  Pallas kernels: 20.6 us -> 17.9 us
    pallas_call x3, Pallas kernels: 13.1 us -> 10.3 us  [on_device(): call(functools.partial(section_kernel, k, TIME_STEP * SECTION_WEIGHTS[k],...]
    ppermute x2 -> x1, starting transfers between devices: 1.45 us -> 2.95 us  [on_device(): corner = lax.ppermute(first, ('gx', 'gy'), diagonal)]
    ppermute x1, starting transfers between devices: 1.66 us -> 0.17 us  [on_device(): yp = lax.ppermute(first, 'gy', back_y)]
    ppermute x1, waiting for transfers between devices: 1.43 us -> 0.01 us  [on_device(): yp = lax.ppermute(first, 'gy', back_y)]
    ppermute x3, waiting for transfers between devices: 3.53 us -> 4.47 us  [on_device(): side = lax.ppermute(pair, 'gy', mixed)]
    ppermute x2 -> x1, waiting for transfers between devices: 0.84 us -> 1.77 us  [on_device(): corner = lax.ppermute(first, ('gx', 'gy'), diagonal)]
    ppermute x3, starting transfers between devices: 0.23 us -> 1.05 us  [on_device(): partner = lax.ppermute(pq, 'gy', flip(1))]
    ppermute x3, waiting for transfers between devices: 0.01 us -> 0.78 us  [on_device(): other = lax.ppermute(side, 'gy', flip(1))]
  transfers between devices with their start and end apart: 29 -> 26, of which waited for: 12 -> 13; matrix products, arithmetic and copies ran while one was open for 1% -> 2% of each run, Pallas kernels for 9% -> 10%
where the time goes in v4:
time: 68.1 us; the launch traced here: 67.9 us
  starting transfers between devices  29.1 us (43%)
  waiting for transfers between devices  18 us (26%)
  Pallas kernels  17.9 us (26%)
  local copies, waits for them, and re-layouts  1.99 us (3%)
  between operations  0.93 us (1%)
    ppermute x5, starting transfers between devices, both_sides(): far = lax.ppermute(block, 'gx', next_pair)  13.4 us
    pallas_call x3, Pallas kernels, on_device(): call(functools.partial(section_kernel, k, TIME_STEP * SECTION_WEIGHTS[k],...  10.3 us
    pallas_call x3, Pallas kernels, on_device(): call(own_plane_kernel, slots_like, whole_in_vmem(3), 'own_plane', [pltpu....  5.27 us
    ppermute x3, starting transfers between devices, on_device(): far = lax.ppermute(pair, 'gy', flip(6))  4.47 us
    ppermute x3, waiting for transfers between devices, on_device(): side = lax.ppermute(pair, 'gy', mixed)  4.47 us
    ppermute x3, waiting for transfers between devices, on_device(): far = lax.ppermute(pair, 'gy', flip(6))  3.43 us
    ppermute x3, starting transfers between devices, on_device(): side = lax.ppermute(pair, 'gy', mixed)  3.42 us
    ppermute x1, waiting for transfers between devices, on_device(): from_x = lax.ppermute(out[3], 'gx', ring_x)  3.11 us
  transfers between devices with their start and end apart: 26, of which 13 were waited for; matrix products, arithmetic and copies ran while one was open for 2% of the time, Pallas kernels for 10%

profile of v4, /device:TPU:0, one launch (start us, length us, event | category | flops | bytes accessed | tf_op | source)
XLA Modules:
  0.0 67.9 jit_solution(5344891323073404164)
XLA Ops:
  0.6 5.1 %collective-permute-start.2 = (f32[48,1024]{1,0:T(8,128)}, f32[48,1024]{1,0:T(8,128)S(1)}, u32[]{:S(2)}, u32[]{:S(2)}) collective-permute-start(f32[48,1024]{1,0:T(8,128)} %bitcast.18), channel_id=1, source_target_pairs={{0,24},{8,16},{16,8},{24,0},{1,25},{9,17},{17,9},{25,1},{2,26},{10... | collective-permute-start | bytes 589832 | tf_op jit(solution)/shard_map/ppermute | solution.py:397
  5.7 1.0 %fusion = (f32[3,1,1,1024]{3,2,1,0:T(1,128)S(1)}, f32[3,1,1,1024]{3,2,1,0:T(1,128)S(1)}) fusion(f32[3,1,16,1024]{3,2,1,0:T(8,128)} %param.10), kind=kLoop, calls=%fused_computation.7 | loop fusion | bytes 49152 | tf_op jit(solution)/shard_map/slice | solution.py:407
  6.9 3.0 %collective-permute-start.4 = (f32[3,1024]{1,0:T(4,128)S(1)}, f32[3,1024]{1,0:T(4,128)S(1)}, u32[]{:S(2)}, u32[]{:S(2)}) collective-permute-start(f32[3,1024]{1,0:T(4,128)S(1)} %bitcast.27), channel_id=1, source_target_pairs={{9,0},{10,1},{11,2},{12,3},{13,4},{14,5},{15,6},{8,7},{17,8},{18,9... | collective-permute-start | bytes 36872 | tf_op jit(solution)/shard_map/ppermute | solution.py:412
  10.0 0.9 %copy-done.1 = f32[3,1,16,1024]{3,2,1,0:T(8,128)S(1)} copy-done((f32[3,1,16,1024]{3,2,1,0:T(8,128)S(1)}, f32[3,1,16,1024]{3,2,1,0:T(8,128)}, u32[]{:S(2)}) %copy-start.1) | copy-done | bytes 196632
  11.0 1.7 %own_plane.3.refs_12_ = f32[3,3584]{1,0:T(4,128)S(1)} custom-call(f32[48,1024]{1,0:T(8,128)S(1)} %bitcast.20, s32[1,3584]{1,0:T(1,128)S(1)} %reshape.17.cell_ref.refs_7_, f32[3,3584]{1,0:T(4,128)S(1)} %copy-done), custom_call_target="tpu_custom_call" | custom-call | tf_op jit(solution)/shard_map/own_plane/pallas_call | solution.py:430
  13.7 1.8 %collective-permute-done.4.refs_5_.refs_6_ = f32[3,1024]{1,0:T(4,128)S(1)} collective-permute-done((f32[3,1024]{1,0:T(4,128)S(1)}, f32[3,1024]{1,0:T(4,128)S(1)}, u32[]{:S(2)}, u32[]{:S(2)}) %collective-permute-start.4) | collective-permute-done | bytes 12320 | tf_op jit(solution)/shard_map/ppermute | solution.py:412
  15.5 3.4 %section.3 = (f32[48,1024]{1,0:T(8,128)S(1)}, f32[8,1024]{1,0:T(8,128)S(1)}, f32[3,3584]{1,0:T(4,128)S(1)}) custom-call(f32[48,1024]{1,0:T(8,128)S(1)} %bitcast.21, f32[3,1024]{1,0:T(4,128)S(1)} %collective-permute-done.refs_1_, f32[48,1024]{1,0:T(8,128)S(1)} %collective-permute-done.1.refs_2_, f32[48,1024]{1,0:T(8,128)S(1)} %collective-permute-done.2.refs_3_, ...), custom_call_target="tpu_custom_call" | custom-call | tf_op jit(solution)/shard_map/section/pallas_call | solution.py:438
  18.8 0.9 %collective-permute-start.5 = (f32[8,1024]{1,0:T(8,128)S(1)}, f32[8,1024]{1,0:T(8,128)S(1)}, u32[]{:S(2)}, u32[]{:S(2)}) collective-permute-start(f32[8,1024]{1,0:T(8,128)S(1)} %get-tuple-element.31.refs_0_), channel_id=1, source_target_pairs={{0,1},{1,0},{2,3},{3,2},{4,5},{5,4},{6,7},{7,6},{8,9},{9,8},{10,11... | collective-permute-start | bytes 98312 | tf_op jit(solution)/shard_map/ppermute | solution.py:454
  19.8 3.5 %collective-permute-start.10 = (f32[48,1024]{1,0:T(8,128)S(1)}, f32[48,1024]{1,0:T(8,128)S(1)}, u32[]{:S(2)}, u32[]{:S(2)}) collective-permute-start(f32[48,1024]{1,0:T(8,128)S(1)} %get-tuple-element.32.refs_5_), channel_id=1, source_target_pairs={{0,24},{8,16},{16,8},{24,0},{1,25},{9,17},{17,9},{25,1},{2,26},{10... | collective-permute-start | bytes 589832 | tf_op jit(solution)/shard_map/ppermute | solution.py:397
  23.3 1.6 %collective-permute-start.6 = (f32[2,8,1024]{2,1,0:T(8,128)S(1)}, f32[2,8,1024]{2,1,0:T(8,128)S(1)}, u32[]{:S(2)}, u32[]{:S(2)}) collective-permute-start(f32[2,8,1024]{2,1,0:T(8,128)S(1)} %pad_maximum_fusion), channel_id=1, source_target_pairs={{0,2},{1,5},{2,0},{3,7},{4,6},{5,1},{6,4},{7,3},{8,10},{9,13},{10,... | collective-permute-start | bytes 196616 | tf_op jit(solution)/shard_map/ppermute | solution.py:456
  24.8 1.5 %collective-permute-start.8 = (f32[2,8,1024]{2,1,0:T(8,128)S(1)}, f32[2,8,1024]{2,1,0:T(8,128)S(1)}, u32[]{:S(2)}, u32[]{:S(2)}) collective-permute-start(f32[2,8,1024]{2,1,0:T(8,128)S(1)} %pad_maximum_fusion), channel_id=1, source_target_pairs={{0,6},{1,7},{2,4},{3,5},{4,2},{5,3},{6,0},{7,1},{8,14},{9,15},{10,... | collective-permute-start | bytes 196616 | tf_op jit(solution)/shard_map/ppermute | solution.py:457
  26.3 2.0 %collective-permute-done.6.refs_2_ = f32[2,8,1024]{2,1,0:T(8,128)S(1)} collective-permute-done((f32[2,8,1024]{2,1,0:T(8,128)S(1)}, f32[2,8,1024]{2,1,0:T(8,128)S(1)}, u32[]{:S(2)}, u32[]{:S(2)}) %collective-permute-start.6) | collective-permute-done | bytes 65568 | tf_op jit(solution)/shard_map/ppermute | solution.py:456
  28.3 1.7 %collective-permute-done.8.refs_4_ = f32[2,8,1024]{2,1,0:T(8,128)S(1)} collective-permute-done((f32[2,8,1024]{2,1,0:T(8,128)S(1)}, f32[2,8,1024]{2,1,0:T(8,128)S(1)}, u32[]{:S(2)}, u32[]{:S(2)}) %collective-permute-start.8) | collective-permute-done | bytes 65568 | tf_op jit(solution)/shard_map/ppermute | solution.py:457
  31.1 1.3 %collective-permute-start.11 = (f32[8,1024]{1,0:T(8,128)S(1)}, f32[8,1024]{1,0:T(8,128)S(1)}, u32[]{:S(2)}, u32[]{:S(2)}) collective-permute-start(f32[8,1024]{1,0:T(8,128)S(1)} %get-tuple-element.35.refs_4_), channel_id=1, source_target_pairs={{0,8},{8,0},{16,24},{24,16},{1,9},{9,1},{17,25},{25,17},{2,10},{10... | collective-permute-start | bytes 98312 | tf_op jit(solution)/shard_map/ppermute | solution.py:398
  32.4 1.7 %own_plane.4.refs_12_ = f32[3,3584]{1,0:T(4,128)S(1)} custom-call(f32[48,1024]{1,0:T(8,128)S(1)} %get-tuple-element.33.u_ref.refs_0_, s32[1,3584]{1,0:T(1,128)S(1)} %reshape.17.cell_ref.refs_7_, f32[3,3584]{1,0:T(4,128)S(1)} %copy-done), custom_call_target="tpu_custom_call" | custom-call | tf_op jit(solution)/shard_map/own_plane/pallas_call | solution.py:430
  34.1 1.9 %collective-permute-done.12.refs_6_ = f32[8,1024]{1,0:T(8,128)S(1)} collective-permute-done((f32[8,1024]{1,0:T(8,128)S(1)}, f32[8,1024]{1,0:T(8,128)S(1)}, u32[]{:S(2)}, u32[]{:S(2)}) %collective-permute-start.12) | collective-permute-done | bytes 32800 | tf_op jit(solution)/shard_map/ppermute | solution.py:397
  36.1 3.5 %section.4 = (f32[48,1024]{1,0:T(8,128)S(1)}, f32[8,1024]{1,0:T(8,128)S(1)}, f32[3,3584]{1,0:T(4,128)S(1)}) custom-call(f32[48,1024]{1,0:T(8,128)S(1)} %get-tuple-element.33.u_ref.refs_0_, f32[3,1024]{1,0:T(4,128)S(1)} %get-tuple-element.34.refs_1_, f32[48,1024]{1,0:T(8,128)S(1)} %collective-permute-done.9.refs_2_, ...), custom_call_target="tpu_custom_call" | custom-call | tf_op jit(solution)/shard_map/section/pallas_call | solution.py:438
  39.6 2.1 %collective-permute-start.18 = (f32[48,1024]{1,0:T(8,128)S(1)}, f32[48,1024]{1,0:T(8,128)S(1)}, u32[]{:S(2)}, u32[]{:S(2)}) collective-permute-start(f32[48,1024]{1,0:T(8,128)S(1)} %get-tuple-element.38.refs_5_), channel_id=1, source_target_pairs={{0,24},{8,16},{16,8},{24,0},{1,25},{9,17},{17,9},{25,1},{2,26},{10... | collective-permute-start | bytes 589832 | tf_op jit(solution)/shard_map/ppermute | solution.py:397
  41.9 0.9 %collective-permute-start.14 = (f32[2,8,1024]{2,1,0:T(8,128)S(1)}, f32[2,8,1024]{2,1,0:T(8,128)S(1)}, u32[]{:S(2)}, u32[]{:S(2)}) collective-permute-start(f32[2,8,1024]{2,1,0:T(8,128)S(1)} %pad_maximum_fusion.1), channel_id=1, source_target_pairs={{0,2},{1,5},{2,0},{3,7},{4,6},{5,1},{6,4},{7,3},{8,10},{9,13},{10,... | collective-permute-start | bytes 196616 | tf_op jit(solution)/shard_map/ppermute | solution.py:456
  42.8 1.5 %collective-permute-start.16 = (f32[2,8,1024]{2,1,0:T(8,128)S(1)}, f32[2,8,1024]{2,1,0:T(8,128)S(1)}, u32[]{:S(2)}, u32[]{:S(2)}) collective-permute-start(f32[2,8,1024]{2,1,0:T(8,128)S(1)} %pad_maximum_fusion.1), channel_id=1, source_target_pairs={{0,6},{1,7},{2,4},{3,5},{4,2},{5,3},{6,0},{7,1},{8,14},{9,15},{10,... | collective-permute-start | bytes 196616 | tf_op jit(solution)/shard_map/ppermute | solution.py:457
  44.3 2.5 %collective-permute-done.14.refs_2_ = f32[2,8,1024]{2,1,0:T(8,128)S(1)} collective-permute-done((f32[2,8,1024]{2,1,0:T(8,128)S(1)}, f32[2,8,1024]{2,1,0:T(8,128)S(1)}, u32[]{:S(2)}, u32[]{:S(2)}) %collective-permute-start.14) | collective-permute-done | bytes 65568 | tf_op jit(solution)/shard_map/ppermute | solution.py:456
  46.8 1.2 %collective-permute-done.16.refs_4_ = f32[2,8,1024]{2,1,0:T(8,128)S(1)} collective-permute-done((f32[2,8,1024]{2,1,0:T(8,128)S(1)}, f32[2,8,1024]{2,1,0:T(8,128)S(1)}, u32[]{:S(2)}, u32[]{:S(2)}) %collective-permute-start.16) | collective-permute-done | bytes 65568 | tf_op jit(solution)/shard_map/ppermute | solution.py:457
  48.3 1.9 %collective-permute-start.20 = (f32[8,1024]{1,0:T(8,128)S(1)}, f32[8,1024]{1,0:T(8,128)S(1)}, u32[]{:S(2)}, u32[]{:S(2)}) collective-permute-start(f32[8,1024]{1,0:T(8,128)S(1)} %get-tuple-element.42.refs_4_), channel_id=1, source_target_pairs={{0,24},{8,16},{16,8},{24,0},{1,25},{9,17},{17,9},{25,1},{2,26},{10... | collective-permute-start | bytes 98312 | tf_op jit(solution)/shard_map/ppermute | solution.py:397
  50.2 1.1 %collective-permute-start.19 = (f32[8,1024]{1,0:T(8,128)S(1)}, f32[8,1024]{1,0:T(8,128)S(1)}, u32[]{:S(2)}, u32[]{:S(2)}) collective-permute-start(f32[8,1024]{1,0:T(8,128)S(1)} %get-tuple-element.42.refs_4_), channel_id=1, source_target_pairs={{0,8},{8,0},{16,24},{24,16},{1,9},{9,1},{17,25},{25,17},{2,10},{10... | collective-permute-start | bytes 98312 | tf_op jit(solution)/shard_map/ppermute | solution.py:398
  51.3 1.9 %own_plane.5.refs_12_ = f32[3,3584]{1,0:T(4,128)S(1)} custom-call(f32[48,1024]{1,0:T(8,128)S(1)} %get-tuple-element.40.u_ref.refs_0_, s32[1,3584]{1,0:T(1,128)S(1)} %reshape.17.cell_ref.refs_7_, f32[3,3584]{1,0:T(4,128)S(1)} %copy-done), custom_call_target="tpu_custom_call" | custom-call | tf_op jit(solution)/shard_map/own_plane/pallas_call | solution.py:430
  53.2 1.1 %collective-permute-done.20.refs_6_ = f32[8,1024]{1,0:T(8,128)S(1)} collective-permute-done((f32[8,1024]{1,0:T(8,128)S(1)}, f32[8,1024]{1,0:T(8,128)S(1)}, u32[]{:S(2)}, u32[]{:S(2)}) %collective-permute-start.20) | collective-permute-done | bytes 32800 | tf_op jit(solution)/shard_map/ppermute | solution.py:397
  54.5 3.5 %section.5 = (f32[48,1024]{1,0:T(8,128)S(1)}, f32[16,1024]{1,0:T(8,128)S(1)}, f32[3,3584]{1,0:T(4,128)S(1)}, f32[3,512]{1,0:T(4,128)S(1)}) custom-call(f32[48,1024]{1,0:T(8,128)S(1)} %get-tuple-element.40.u_ref.refs_0_, f32[3,1024]{1,0:T(4,128)S(1)} %get-tuple-element.41.refs_1_, f32[48,1024]{1,0:T(8,128)S(1)} %collective-permute-done.17.refs_2_, ...), custom_call_target="tpu_custom_call" | custom-call | tf_op jit(solution)/shard_map/section/pallas_call | solution.py:438
  58.0 1.2 %collective-permute-done.21.refs_1_ = f32[16,1024]{1,0:T(8,128)S(1)} collective-permute-done((f32[16,1024]{1,0:T(8,128)S(1)}, f32[16,1024]{1,0:T(8,128)S(1)}, u32[]{:S(2)}, u32[]{:S(2)}) %collective-permute-start.21) | collective-permute-done | bytes 65568 | tf_op jit(solution)/shard_map/ppermute | solution.py:454
  59.3 1.0 %collective-permute-start.22 = (f32[2,8,1024]{2,1,0:T(8,128)S(1)}, f32[2,8,1024]{2,1,0:T(8,128)S(1)}, u32[]{:S(2)}, u32[]{:S(2)}) collective-permute-start(f32[2,8,1024]{2,1,0:T(8,128)S(1)} %pad_maximum_fusion.2), channel_id=1, source_target_pairs={{0,2},{1,5},{2,0},{3,7},{4,6},{5,1},{6,4},{7,3},{8,10},{9,13},{10,... | collective-permute-start | bytes 196616 | tf_op jit(solution)/shard_map/ppermute | solution.py:456
  61.1 1.5 %collective-permute-start.25 = (f32[2,8,1024]{2,1,0:T(8,128)S(1)}, f32[2,8,1024]{2,1,0:T(8,128)S(1)}, u32[]{:S(2)}, u32[]{:S(2)}) collective-permute-start(f32[2,8,1024]{2,1,0:T(8,128)S(1)} %pad_maximum_fusion.2), channel_id=1, source_target_pairs={{0,6},{1,7},{2,4},{3,5},{4,2},{5,3},{6,0},{7,1},{8,14},{9,15},{10,... | collective-permute-start | bytes 196616 | tf_op jit(solution)/shard_map/ppermute | solution.py:457
  62.6 3.1 %collective-permute-done.23.refs_9_ = f32[3,512]{1,0:T(4,128)S(1)} collective-permute-done((f32[3,512]{1,0:T(4,128)S(1)}, f32[3,512]{1,0:T(4,128)S(1)}, u32[]{:S(2)}, u32[]{:S(2)}) %collective-permute-start.23) | collective-permute-done | bytes 6176 | tf_op jit(solution)/shard_map/ppermute | solution.py:452
  67.0 0.9 %join.5 = (f32[48,1024]{1,0:T(8,128)}, f32[3,3584]{1,0:T(4,128)}) custom-call(f32[16,1024]{1,0:T(8,128)S(1)} %get-tuple-element.44.refs_0_, f32[16,1024]{1,0:T(8,128)S(1)} %collective-permute-done.21.refs_1_, f32[2,8,1024]{2,1,0:T(8,128)S(1)} %collective-permute-done.22.refs_2_, f32[2,8,1024]{2,1,0:T(8,128)S(1)} %collective-permute-done.24.refs_3_, ...), custom_call_target="tpu_custom_call" | custom-call | tf_op jit(solution)/shard_map/join/pallas_call | solution.py:475
  (62 shorter events, 5.3 us)
Async XLA Ops:
  0.6 14.8 %collective-permute-start.2 = (f32[48,1024]{1,0:T(8,128)}, f32[48,1024]{1,0:T(8,128)S(1)}, u32[]{:S(2)}, u32[]{:S(2)}) collective-permute-start(f32[48,1024]{1,0:T(8,128)} %bitcast.18), channel_id=1, source_target_pairs={{0,24},{8,16},{16,8},{24,0},{1,25},{9,17},{17,9},{25,1},{2,26},{10... | collective-permute-start | bytes 589832 | tf_op jit(solution)/shard_map/ppermute | solution.py:397
  5.7 9.7 %collective-permute-start.1 = (f32[48,1024]{1,0:T(8,128)}, f32[48,1024]{1,0:T(8,128)S(1)}, u32[]{:S(2)}, u32[]{:S(2)}) collective-permute-start(f32[48,1024]{1,0:T(8,128)} %bitcast.19), channel_id=1, source_target_pairs={{0,8},{8,0},{16,24},{24,16},{1,9},{9,1},{17,25},{25,17},{2,10},{10... | collective-permute-start | bytes 589832 | tf_op jit(solution)/shard_map/ppermute | solution.py:398
  6.7 3.3 %copy-start.9 = (s32[3584]{0:T(1024)S(1)}, s32[3584]{0:T(1024)}, u32[]{:S(2)}) copy-start(s32[3584]{0:T(1024)} %param.16) | copy-start | bytes 43012
  6.7 3.3 %copy-start = (f32[3,3584]{1,0:T(4,128)S(1)}, f32[3,3584]{1,0:T(4,128)}, u32[]{:S(2)}) copy-start(f32[3,3584]{1,0:T(4,128)} %refs_8_.5) | copy-start | bytes 129028
  6.8 6.9 %collective-permute-start = (f32[3,1024]{1,0:T(4,128)S(1)}, f32[3,1024]{1,0:T(4,128)S(1)}, u32[]{:S(2)}, u32[]{:S(2)}) collective-permute-start(f32[3,1024]{1,0:T(4,128)S(1)} %bitcast.26), channel_id=1, source_target_pairs={{0,1},{1,2},{2,3},{3,4},{4,5},{5,6},{6,7},{7,0},{8,9},{9,10},{10,1... | collective-permute-start | bytes 36872 | tf_op jit(solution)/shard_map/ppermute | solution.py:411
  6.8 3.2 %copy-start.10 = (f32[3584]{0:T(1024)S(1)}, f32[3584]{0:T(1024)}, u32[]{:S(2)}) copy-start(f32[3584]{0:T(1024)} %param.18) | copy-start | bytes 43012
  6.9 8.6 %collective-permute-start.4 = (f32[3,1024]{1,0:T(4,128)S(1)}, f32[3,1024]{1,0:T(4,128)S(1)}, u32[]{:S(2)}, u32[]{:S(2)}) collective-permute-start(f32[3,1024]{1,0:T(4,128)S(1)} %bitcast.27), channel_id=1, source_target_pairs={{9,0},{10,1},{11,2},{12,3},{13,4},{14,5},{15,6},{8,7},{17,8},{18,9... | collective-permute-start | bytes 36872 | tf_op jit(solution)/shard_map/ppermute | solution.py:412
  9.8 5.6 %collective-permute-start.3 = (f32[3,1024]{1,0:T(4,128)S(1)}, f32[3,1024]{1,0:T(4,128)S(1)}, u32[]{:S(2)}, u32[]{:S(2)}) collective-permute-start(f32[3,1024]{1,0:T(4,128)S(1)} %bitcast.28), channel_id=1, source_target_pairs={{1,0},{2,1},{3,2},{4,3},{5,4},{6,5},{7,6},{0,7},{9,8},{10,9},{11,1... | collective-permute-start | bytes 36872 | tf_op jit(solution)/shard_map/ppermute | solution.py:410
  11.0 1.8 %copy-start.8 = (s32[1,1,3]{2,1,0:T(1,128)S(1)}, s32[1,1,3]{2,1,0:T(1,128)}, u32[]{:S(2)}) copy-start(s32[1,1,3]{2,1,0:T(1,128)} %count_ref.1) | copy-start | bytes 40
  11.0 4.5 %copy-start.2 = (f32[3,1,16,1024]{3,2,1,0:T(8,128)S(1)}, f32[3,1,16,1024]{3,2,1,0:T(8,128)}, u32[]{:S(2)}) copy-start(f32[3,1,16,1024]{3,2,1,0:T(8,128)} %param.10) | copy-start | bytes 589828
  11.0 4.5 %copy-start.3 = (f32[3,3584]{1,0:T(4,128)S(1)}, f32[3,3584]{1,0:T(4,128)}, u32[]{:S(2)}) copy-start(f32[3,3584]{1,0:T(4,128)} %refs_11_.1) | copy-start | bytes 129028
  18.8 4.4 %collective-permute-start.5 = (f32[8,1024]{1,0:T(8,128)S(1)}, f32[8,1024]{1,0:T(8,128)S(1)}, u32[]{:S(2)}, u32[]{:S(2)}) collective-permute-start(f32[8,1024]{1,0:T(8,128)S(1)} %get-tuple-element.31.refs_0_), channel_id=1, source_target_pairs={{0,1},{1,0},{2,3},{3,2},{4,5},{5,4},{6,7},{7,6},{8,9},{9,8},{10,11... | collective-permute-start | bytes 98312 | tf_op jit(solution)/shard_map/ppermute | solution.py:454
  19.8 16.3 %collective-permute-start.10 = (f32[48,1024]{1,0:T(8,128)S(1)}, f32[48,1024]{1,0:T(8,128)S(1)}, u32[]{:S(2)}, u32[]{:S(2)}) collective-permute-start(f32[48,1024]{1,0:T(8,128)S(1)} %get-tuple-element.32.refs_5_), channel_id=1, source_target_pairs={{0,24},{8,16},{16,8},{24,0},{1,25},{9,17},{17,9},{25,1},{2,26},{10... | collective-permute-start | bytes 589832 | tf_op jit(solution)/shard_map/ppermute | solution.py:397
  23.2 12.8 %collective-permute-start.9 = (f32[48,1024]{1,0:T(8,128)S(1)}, f32[48,1024]{1,0:T(8,128)S(1)}, u32[]{:S(2)}, u32[]{:S(2)}) collective-permute-start(f32[48,1024]{1,0:T(8,128)S(1)} %get-tuple-element.32.refs_5_), channel_id=1, source_target_pairs={{0,8},{8,0},{16,24},{24,16},{1,9},{9,1},{17,25},{25,17},{2,10},{10... | collective-permute-start | bytes 589832 | tf_op jit(solution)/shard_map/ppermute | solution.py:398
  23.3 5.0 %collective-permute-start.6 = (f32[2,8,1024]{2,1,0:T(8,128)S(1)}, f32[2,8,1024]{2,1,0:T(8,128)S(1)}, u32[]{:S(2)}, u32[]{:S(2)}) collective-permute-start(f32[2,8,1024]{2,1,0:T(8,128)S(1)} %pad_maximum_fusion), channel_id=1, source_target_pairs={{0,2},{1,5},{2,0},{3,7},{4,6},{5,1},{6,4},{7,3},{8,10},{9,13},{10,... | collective-permute-start | bytes 196616 | tf_op jit(solution)/shard_map/ppermute | solution.py:456
  24.8 5.2 %collective-permute-start.8 = (f32[2,8,1024]{2,1,0:T(8,128)S(1)}, f32[2,8,1024]{2,1,0:T(8,128)S(1)}, u32[]{:S(2)}, u32[]{:S(2)}) collective-permute-start(f32[2,8,1024]{2,1,0:T(8,128)S(1)} %pad_maximum_fusion), channel_id=1, source_target_pairs={{0,6},{1,7},{2,4},{3,5},{4,2},{5,3},{6,0},{7,1},{8,14},{9,15},{10,... | collective-permute-start | bytes 196616 | tf_op jit(solution)/shard_map/ppermute | solution.py:457
  28.3 1.7 %collective-permute-start.7 = (f32[2,8,1024]{2,1,0:T(8,128)S(1)}, f32[2,8,1024]{2,1,0:T(8,128)S(1)}, u32[]{:S(2)}, u32[]{:S(2)}) collective-permute-start(f32[2,8,1024]{2,1,0:T(8,128)S(1)} %collective-permute-done.6.refs_2_), channel_id=1, source_target_pairs={{0,1},{1,0},{2,3},{3,2},{4,5},{5,4},{6,7},{7,6},{8,9},{9,8},{10,11... | collective-permute-start | bytes 196616 | tf_op jit(solution)/shard_map/ppermute | solution.py:460
  30.2 5.8 %collective-permute-start.12 = (f32[8,1024]{1,0:T(8,128)S(1)}, f32[8,1024]{1,0:T(8,128)S(1)}, u32[]{:S(2)}, u32[]{:S(2)}) collective-permute-start(f32[8,1024]{1,0:T(8,128)S(1)} %get-tuple-element.35.refs_4_), channel_id=1, source_target_pairs={{0,24},{8,16},{16,8},{24,0},{1,25},{9,17},{17,9},{25,1},{2,26},{10... | collective-permute-start | bytes 98312 | tf_op jit(solution)/shard_map/ppermute | solution.py:397
  31.1 4.9 %collective-permute-start.11 = (f32[8,1024]{1,0:T(8,128)S(1)}, f32[8,1024]{1,0:T(8,128)S(1)}, u32[]{:S(2)}, u32[]{:S(2)}) collective-permute-start(f32[8,1024]{1,0:T(8,128)S(1)} %get-tuple-element.35.refs_4_), channel_id=1, source_target_pairs={{0,8},{8,0},{16,24},{24,16},{1,9},{9,1},{17,25},{25,17},{2,10},{10... | collective-permute-start | bytes 98312 | tf_op jit(solution)/shard_map/ppermute | solution.py:398
  39.5 2.4 %collective-permute-start.13 = (f32[8,1024]{1,0:T(8,128)S(1)}, f32[8,1024]{1,0:T(8,128)S(1)}, u32[]{:S(2)}, u32[]{:S(2)}) collective-permute-start(f32[8,1024]{1,0:T(8,128)S(1)} %get-tuple-element.37.refs_0_), channel_id=1, source_target_pairs={{0,1},{1,0},{2,3},{3,2},{4,5},{5,4},{6,7},{7,6},{8,9},{9,8},{10,11... | collective-permute-start | bytes 98312 | tf_op jit(solution)/shard_map/ppermute | solution.py:454
  39.6 14.8 %collective-permute-start.18 = (f32[48,1024]{1,0:T(8,128)S(1)}, f32[48,1024]{1,0:T(8,128)S(1)}, u32[]{:S(2)}, u32[]{:S(2)}) collective-permute-start(f32[48,1024]{1,0:T(8,128)S(1)} %get-tuple-element.38.refs_5_), channel_id=1, source_target_pairs={{0,24},{8,16},{16,8},{24,0},{1,25},{9,17},{17,9},{25,1},{2,26},{10... | collective-permute-start | bytes 589832 | tf_op jit(solution)/shard_map/ppermute | solution.py:397
  41.7 12.8 %collective-permute-start.17 = (f32[48,1024]{1,0:T(8,128)S(1)}, f32[48,1024]{1,0:T(8,128)S(1)}, u32[]{:S(2)}, u32[]{:S(2)}) collective-permute-start(f32[48,1024]{1,0:T(8,128)S(1)} %get-tuple-element.38.refs_5_), channel_id=1, source_target_pairs={{0,8},{8,0},{16,24},{24,16},{1,9},{9,1},{17,25},{25,17},{2,10},{10... | collective-permute-start | bytes 589832 | tf_op jit(solution)/shard_map/ppermute | solution.py:398
  41.9 4.9 %collective-permute-start.14 = (f32[2,8,1024]{2,1,0:T(8,128)S(1)}, f32[2,8,1024]{2,1,0:T(8,128)S(1)}, u32[]{:S(2)}, u32[]{:S(2)}) collective-permute-start(f32[2,8,1024]{2,1,0:T(8,128)S(1)} %pad_maximum_fusion.1), channel_id=1, source_target_pairs={{0,2},{1,5},{2,0},{3,7},{4,6},{5,1},{6,4},{7,3},{8,10},{9,13},{10,... | collective-permute-start | bytes 196616 | tf_op jit(solution)/shard_map/ppermute | solution.py:456
  42.8 5.2 %collective-permute-start.16 = (f32[2,8,1024]{2,1,0:T(8,128)S(1)}, f32[2,8,1024]{2,1,0:T(8,128)S(1)}, u32[]{:S(2)}, u32[]{:S(2)}) collective-permute-start(f32[2,8,1024]{2,1,0:T(8,128)S(1)} %pad_maximum_fusion.1), channel_id=1, source_target_pairs={{0,6},{1,7},{2,4},{3,5},{4,2},{5,3},{6,0},{7,1},{8,14},{9,15},{10,... | collective-permute-start | bytes 196616 | tf_op jit(solution)/shard_map/ppermute | solution.py:457
  46.8 1.3 %collective-permute-start.15 = (f32[2,8,1024]{2,1,0:T(8,128)S(1)}, f32[2,8,1024]{2,1,0:T(8,128)S(1)}, u32[]{:S(2)}, u32[]{:S(2)}) collective-permute-start(f32[2,8,1024]{2,1,0:T(8,128)S(1)} %collective-permute-done.14.refs_2_), channel_id=1, source_target_pairs={{0,1},{1,0},{2,3},{3,2},{4,5},{5,4},{6,7},{7,6},{8,9},{9,8},{10,11... | collective-permute-start | bytes 196616 | tf_op jit(solution)/shard_map/ppermute | solution.py:460
  48.3 6.0 %collective-permute-start.20 = (f32[8,1024]{1,0:T(8,128)S(1)}, f32[8,1024]{1,0:T(8,128)S(1)}, u32[]{:S(2)}, u32[]{:S(2)}) collective-permute-start(f32[8,1024]{1,0:T(8,128)S(1)} %get-tuple-element.42.refs_4_), channel_id=1, source_target_pairs={{0,24},{8,16},{16,8},{24,0},{1,25},{9,17},{17,9},{25,1},{2,26},{10... | collective-permute-start | bytes 98312 | tf_op jit(solution)/shard_map/ppermute | solution.py:397
  50.2 4.2 %collective-permute-start.19 = (f32[8,1024]{1,0:T(8,128)S(1)}, f32[8,1024]{1,0:T(8,128)S(1)}, u32[]{:S(2)}, u32[]{:S(2)}) collective-permute-start(f32[8,1024]{1,0:T(8,128)S(1)} %get-tuple-element.42.refs_4_), channel_id=1, source_target_pairs={{0,8},{8,0},{16,24},{24,16},{1,9},{9,1},{17,25},{25,17},{2,10},{10... | collective-permute-start | bytes 98312 | tf_op jit(solution)/shard_map/ppermute | solution.py:398
  57.9 1.3 %collective-permute-start.21 = (f32[16,1024]{1,0:T(8,128)S(1)}, f32[16,1024]{1,0:T(8,128)S(1)}, u32[]{:S(2)}, u32[]{:S(2)}) collective-permute-start(f32[16,1024]{1,0:T(8,128)S(1)} %get-tuple-element.44.refs_0_), channel_id=1, source_target_pairs={{0,1},{1,0},{2,3},{3,2},{4,5},{5,4},{6,7},{7,6},{8,9},{9,8},{10,11... | collective-permute-start | bytes 196616 | tf_op jit(solution)/shard_map/ppermute | solution.py:454
  59.3 6.4 %collective-permute-start.22 = (f32[2,8,1024]{2,1,0:T(8,128)S(1)}, f32[2,8,1024]{2,1,0:T(8,128)S(1)}, u32[]{:S(2)}, u32[]{:S(2)}) collective-permute-start(f32[2,8,1024]{2,1,0:T(8,128)S(1)} %pad_maximum_fusion.2), channel_id=1, source_target_pairs={{0,2},{1,5},{2,0},{3,7},{4,6},{5,1},{6,4},{7,3},{8,10},{9,13},{10,... | collective-permute-start | bytes 196616 | tf_op jit(solution)/shard_map/ppermute | solution.py:456
  60.2 5.4 %collective-permute-start.23 = (f32[3,512]{1,0:T(4,128)S(1)}, f32[3,512]{1,0:T(4,128)S(1)}, u32[]{:S(2)}, u32[]{:S(2)}) collective-permute-start(f32[3,512]{1,0:T(4,128)S(1)} %get-tuple-element.45), channel_id=1, source_target_pairs={{0,8},{8,16},{16,24},{24,0},{1,9},{9,17},{17,25},{25,1},{2,10},{10... | collective-permute-start | bytes 18440 | tf_op jit(solution)/shard_map/ppermute | solution.py:452
  61.1 5.2 %collective-permute-start.25 = (f32[2,8,1024]{2,1,0:T(8,128)S(1)}, f32[2,8,1024]{2,1,0:T(8,128)S(1)}, u32[]{:S(2)}, u32[]{:S(2)}) collective-permute-start(f32[2,8,1024]{2,1,0:T(8,128)S(1)} %pad_maximum_fusion.2), channel_id=1, source_target_pairs={{0,6},{1,7},{2,4},{3,5},{4,2},{5,3},{6,0},{7,1},{8,14},{9,15},{10,... | collective-permute-start | bytes 196616 | tf_op jit(solution)/shard_map/ppermute | solution.py:457
  65.7 1.3 %collective-permute-start.24 = (f32[2,8,1024]{2,1,0:T(8,128)S(1)}, f32[2,8,1024]{2,1,0:T(8,128)S(1)}, u32[]{:S(2)}, u32[]{:S(2)}) collective-permute-start(f32[2,8,1024]{2,1,0:T(8,128)S(1)} %collective-permute-done.22.refs_2_), channel_id=1, source_target_pairs={{0,1},{1,0},{2,3},{3,2},{4,5},{5,4},{6,7},{7,6},{8,9},{9,8},{10,11... | collective-permute-start | bytes 196616 | tf_op jit(solution)/shard_map/ppermute | solution.py:460
  (5 other events, 8.0 us)

commit v5 on v4

--- a/solution.py
+++ b/solution.py
@@ -21,6 +21,7 @@
 DEPTH = 256
 VMEM_LIMIT = 32 * 1024 * 1024
 ENTER, LEAVE, PIVOT, UPWARD, METRIC = range(16, 21)
+ROW, COLUMN, INNER, GROUP, LIVE, EDGE = range(6)
 
 F32 = jnp.float32
 BF16 = jnp.bfloat16
@@ -74,7 +75,7 @@
     shape = (groups // 16, 16, width)
     order = lax.broadcasted_iota(jnp.int32, shape, 0) * 16 + lax.broadcasted_iota(jnp.int32, shape, 1)
     order = order.astype(F32).astype(BF16)
-    hit = order == jnp.broadcast_to(group.astype(F32), (16, width)).astype(BF16)[None]
+    hit = order == jnp.broadcast_to(group, (16, width)).astype(BF16)[None]
     parts = []
     for value in values:
         value = jnp.broadcast_to(value, (16, width)).astype(BF16)[None]
@@ -98,9 +99,20 @@
 
 
 def tables_kernel(
-    down_ref, up_ref, scale_ref, metric_ref, count_ref, matrix_ref, answer_ref, scal_ref, live_ref
+    cells_z,
+    down_ref,
+    up_ref,
+    scale_ref,
+    metric_ref,
+    count_ref,
+    cell_ref,
+    off_ref,
+    matrix_ref,
+    answer_ref,
+    scal_ref,
+    slots_ref,
 ):
-    slot = lax.broadcasted_iota(jnp.int32, live_ref.shape, 1)
+    slot = lax.broadcasted_iota(jnp.int32, cell_ref.shape, 1)
     remain = slot - RESIDENT
     heading = remain // CAP
     limit = jnp.where(
@@ -108,8 +120,15 @@
         count_ref[0, 0, 0],
         jnp.where(heading == 1, count_ref[0, 0, 1], count_ref[0, 0, 2]),
     )
-    live_ref[...] = jnp.where((remain < 0) | (remain % CAP < limit), 1.0, 0.0)
     sections, rows = down_ref.shape
+    cell = cell_ref[...]
+    row, place = cell // cells_z, cell % cells_z
+    slots_ref[ROW : ROW + 1, :] = row.astype(F32)
+    slots_ref[COLUMN : COLUMN + 1, :] = place.astype(F32)
+    slots_ref[INNER : INNER + 1, :] = (place % DEPTH).astype(F32)
+    slots_ref[GROUP : GROUP + 1, :] = (place // DEPTH * rows + row).astype(F32)
+    slots_ref[LIVE : LIVE + 1, :] = jnp.where((remain < 0) | (remain % CAP < limit), 1.0, 0.0)
+    slots_ref[EDGE : EDGE + 1, :] = jnp.where(row == rows - 1, off_ref[1:2, :], 0.0)
     lane = lax.broadcasted_iota(jnp.int32, (1, 128), 1)
     at = lambda place: jnp.where(lane == place, 1.0, 0.0)
     matrix_ref[...] = jnp.zeros_like(matrix_ref)
@@ -138,19 +157,87 @@
         )
 
 
-def own_plane_kernel(u_ref, cell_ref, off_ref, out_ref, table_ref):
+def two_sides(one_ref, other_ref):
+    even = lax.axis_index("gx") % 2 == 0
+    one, other = one_ref[...], other_ref[...]
+    return jnp.where(even, one, other), jnp.where(even, other, one)
+
+
+def joined_plane(plane, ef, answer):
+    enter, leave = answer[:, ENTER : ENTER + 1], answer[:, LEAVE : LEAVE + 1]
+    rows = enter.shape[0]
+    return jnp.concatenate(
+        [
+            plane[rows * c : rows * (c + 1)]
+            + enter * ef[c : c + 1]
+            + leave * ef[COMPS + c : COMPS + c + 1]
+            for c in range(COMPS)
+        ],
+        axis=0,
+    )
+
+
+def pack(ef_ref, parts):
+    for i, part in enumerate(parts):
+        ef_ref[6 + i // 2 : 7 + i // 2, CAP * (i % 2) : CAP * (i % 2) + CAP] = part
+
+
+def unpack(ef):
+    return [ef[6 + i // 2 : 7 + i // 2, CAP * (i % 2) : CAP * (i % 2) + CAP] for i in range(4)]
+
+
+def visitors_kernel(
+    number,
+    step,
+    u_ref,
+    ef_ref,
+    near_x_ref,
+    far_x_ref,
+    near_ef_ref,
+    far_ef_ref,
+    near_old_ref,
+    far_old_ref,
+    answer_ref,
+    out_ref,
+):
+    cells_z = u_ref.shape[1]
+    rows = u_ref.shape[0] // COMPS
+    count = COMPS * rows
+    _, ef = two_sides(near_ef_ref, far_ef_ref)
+    _, old = two_sides(near_old_ref, far_old_ref)
+    _, plane = two_sides(near_x_ref, far_x_ref)
+    plane = joined_plane(plane, ef, answer_ref[number - 1])
+    pad = jnp.zeros((8 - COMPS, cells_z), F32)
+    cell, fx, fy, fz = unpack(old)
+    *v, tau = unpack(ef)
+    row = jnp.floor(cell * (1.0 / cells_z))
+    chosen = across(cell - row * cells_z, cells_z)
+    behind = split_rows(jnp.concatenate([plane, ef[COMPS : 2 * COMPS], pad], axis=0))
+    here = split_rows(jnp.concatenate([u_ref[...], ef_ref[COMPS : 2 * COMPS, :], pad], axis=0))
+    blended = blend_z(jnp.dot(behind, chosen, preferred_element_type=F32), fz) * (1.0 - fx)
+    blended = blended + blend_z(jnp.dot(here, chosen, preferred_element_type=F32), fz) * fx
+    order = lax.broadcasted_iota(jnp.int32, (rows, CAP), 0).astype(F32)
+    weight = jnp.where(order == row, 1.0 - fy, jnp.where(order == row + 1.0, fy, 0.0))
+    edge = jnp.where(row == rows - 1.0, fy, 0.0)
+    for c in range(COMPS):
+        part = jnp.sum(blended[rows * c : rows * (c + 1)] * weight, axis=0, keepdims=True)
+        fluid = part + blended[count + c : count + c + 1] * edge
+        moved = v[c] + step * (tau * (fluid - v[c]))
+        out_ref[c : c + 1, :] = jnp.where(cell >= 0.0, moved, 0.0)
+
+
+def own_plane_kernel(u_ref, slots_ref, off_ref, out_ref, table_ref):
     cells_z = u_ref.shape[1]
     rows = u_ref.shape[0] // COMPS
     table_ref[...] = split_rows(u_ref[...])
-    order = lax.broadcasted_iota(jnp.int32, (rows, TILE), 0)
-    for t in range(cell_ref.shape[1] // TILE):
+    order = lax.broadcasted_iota(jnp.int32, (rows, TILE), 0).astype(F32)
+    for t in range(slots_ref.shape[1] // TILE):
         here = slice(t * TILE, (t + 1) * TILE)
-        cell = cell_ref[:, here]
-        row = cell // cells_z
+        row, column = (slots_ref[d : d + 1, here] for d in (ROW, COLUMN))
         fx, fy, fz = (off_ref[d : d + 1, here] for d in range(3))
-        chosen = across((cell % cells_z).astype(F32), cells_z)
+        chosen = across(column, cells_z)
         blended = blend_z(jnp.dot(table_ref[...], chosen, preferred_element_type=F32), fz)
-        weight = jnp.where(order == row, 1.0 - fy, jnp.where(order == row + 1, fy, 0.0))
+        weight = jnp.where(order == row, 1.0 - fy, jnp.where(order == row + 1.0, fy, 0.0))
         weight = weight * (1.0 - fx)
         for c in range(COMPS):
             part = blended[rows * c : rows * (c + 1)] * weight
@@ -162,9 +249,8 @@
     refs = list(refs)
     take = lambda count: [refs.pop(0) for _ in range(count)]
     u_ref, ym_ref, near_x_ref, far_x_ref, yp_ref, near_ef_ref, far_ef_ref = take(7)
-    cell_ref, off_ref, tau_ref, live_ref, v_ref, near_ref, matrix_ref, answer_ref, scal_ref = take(9)
+    slots_ref, off_ref, tau_ref, v_ref, near_ref, matrix_ref, answer_ref, scal_ref = take(8)
     w_ref, pq_ref, v_out_ref = take(3)
-    leaving_ref = refs.pop(0) if last else None
     table_ref, spread_ref, chosen_ref = refs
 
     cells_z = u_ref.shape[1]
@@ -174,65 +260,49 @@
     position = lax.axis_index("gy")
     top = jnp.where(position == lax.axis_size("gy") - 1, 0.0, 1.0).astype(F32)
     bottom = jnp.where(position == 0, 0.0, 1.0).astype(F32)
-    y_minus = ym_ref[...] * bottom
-    even = lax.axis_index("gx") % 2 == 0
-
-    def sides(one, other):
-        return jnp.where(even, one, other), jnp.where(even, other, one)
-
-    x_plus, x_minus = sides(near_x_ref[...], far_x_ref[...])
-    ahead, behind = sides(near_ef_ref[...], far_ef_ref[...])
+    x_plus, x_minus = two_sides(near_x_ref, far_x_ref)
+    ahead, behind = two_sides(near_ef_ref, far_ef_ref)
     if first:
-        y_plus = yp_ref[...] * top
+        chip, beside = yp_ref[...], ym_ref[...]
+        below = position % 2 == 1
+        y_plus = jnp.where(below, beside, chip)[:COMPS] * top
+        y_minus = jnp.where(below, chip, beside)[COMPS:] * bottom
         corner = ahead * top
     else:
+        y_minus = ym_ref[...] * bottom
         y_plus = yp_ref[COMPS : 2 * COMPS, :]
         corner = ahead[COMPS : 2 * COMPS]
-        enter = answer_ref[number - 1, :, ENTER : ENTER + 1]
-        leave = answer_ref[number - 1, :, LEAVE : LEAVE + 1]
-
-        def joined(plane, ef):
-            return jnp.concatenate(
-                [
-                    plane[rows * c : rows * (c + 1)]
-                    + enter * ef[c : c + 1]
-                    + leave * ef[COMPS + c : COMPS + c + 1]
-                    for c in range(COMPS)
-                ],
-                axis=0,
-            )
-
-        x_plus, x_minus = joined(x_plus, ahead), joined(x_minus, behind)
+        x_plus, x_minus = (
+            joined_plane(plane, ef, answer_ref[number - 1])
+            for plane, ef in ((x_plus, ahead), (x_minus, behind))
+        )
     pad = jnp.zeros((2, cells_z), F32)
     table_ref[...] = split_rows(jnp.concatenate([x_plus, y_plus, corner, pad], axis=0))
-    order = lax.broadcasted_iota(jnp.int32, (rows, TILE), 0)
-    for t in range(cell_ref.shape[1] // TILE):
+    order = lax.broadcasted_iota(jnp.int32, (rows, TILE), 0).astype(F32)
+    for t in range(slots_ref.shape[1] // TILE):
         here = slice(t * TILE, (t + 1) * TILE)
-        cell = cell_ref[:, here]
-        row, place = cell // cells_z, cell % cells_z
-        column = place.astype(F32)
+        row, column, inner, group, live, edge = (slots_ref[d : d + 1, here] for d in range(6))
         fx, fy, fz = (off_ref[d : d + 1, here] for d in range(3))
         found = jnp.dot(table_ref[...], across(column, cells_z), preferred_element_type=F32)
-        chosen_ref[here, :] = down((place % DEPTH).astype(F32))
+        chosen_ref[here, :] = down(inner)
         blended = blend_z(found, fz)
-        weight = jnp.where(order == row, 1.0 - fy, jnp.where(order == row + 1, fy, 0.0)) * fx
-        edge = jnp.where(row == rows - 1, fy, 0.0)
-        live = live_ref[:, here]
-        tau = tau_ref[:, here]
-        pushes = []
-        for c in range(COMPS):
-            part = jnp.sum(blended[rows * c : rows * (c + 1)] * weight, axis=0, keepdims=True)
-            side = blended[count + c : count + c + 1] * (1.0 - fx)
-            side = side + blended[count + COMPS + c : count + COMPS + c + 1] * fx
-            fluid = near_ref[c : c + 1, here] + part + side * edge
-            v = v_ref[c : c + 1, here]
-            drag = tau * (fluid - v)
-            v = v + step * drag
-            v_out_ref[c : c + 1, here] = v * live if last else v
-            pushes.append(drag * live * (-COUPLING))
-        high = [push.astype(BF16).astype(F32) for push in pushes]
-        low = [push - part for push, part in zip(pushes, high)]
-        spread_ref[:, here] = spread_out(high + low, place // DEPTH * rows + row, groups)
+        weight = jnp.where(order == row, 1.0 - fy, jnp.where(order == row + 1.0, fy, 0.0)) * fx
+        parts = [
+            jnp.sum(blended[rows * c : rows * (c + 1)] * weight, axis=0, keepdims=True)
+            for c in range(COMPS)
+        ]
+        side = blended[count : count + COMPS] * (1.0 - fx)
+        side = side + blended[count + COMPS : count + 2 * COMPS] * fx
+        fluid = near_ref[:, here] + jnp.concatenate(parts, axis=0) + side * edge
+        v = v_ref[:, here]
+        drag = tau_ref[:, here] * (fluid - v)
+        v = v + step * drag
+        v_out_ref[:, here] = v * live if last else v
+        push = drag * live * (-COUPLING)
+        high = push.astype(BF16).astype(F32)
+        low = push - high
+        pushes = [part[c : c + 1] for part in (high, low) for c in range(COMPS)]
+        spread_ref[:, here] = spread_out(pushes, group, groups)
     pushed = jnp.dot(spread_ref[...], chosen_ref[...], preferred_element_type=F32)
 
     u = u_ref[...]
@@ -270,7 +340,6 @@
         for k in range(scal_ref.shape[0]):
             pq_ref[6:8, 128 * k : 128 * (k + 1)] = scal_ref[k]
     if last:
-        leaving_ref[...] = v_out_ref[:, RESIDENT : RESIDENT + CAP]
         lower = v_out_ref[:, RESIDENT + CAP : RESIDENT + 2 * CAP]
         upper = v_out_ref[:, RESIDENT + 2 * CAP :]
         even = position % 2 == 0
@@ -294,6 +363,7 @@
     if last:
         v_ref, from_x_ref, u_ref, moved_ref = take(4)
     else:
+        slots_ref, off_ref, tau_ref, v_ref = take(4)
         u_ref, ef_ref, ym_ref = take(3)
         if number == 0:
             (known_ref,) = take(1)
@@ -359,7 +429,14 @@
     else:
         ef_ref[0:COMPS, :] = own_in
         ef_ref[COMPS : 2 * COMPS, :] = own_out
-        ef_ref[2 * COMPS :, :] = jnp.zeros((2, w_ref.shape[1]), F32)
+        leaving = slice(RESIDENT, RESIDENT + CAP)
+        if number == 0:
+            cell = slots_ref[ROW : ROW + 1, leaving] * float(w_ref.shape[1])
+            cell = cell + slots_ref[COLUMN : COLUMN + 1, leaving]
+            cell = jnp.where(slots_ref[LIVE : LIVE + 1, leaving] > 0.0, cell, -1.0)
+            pack(ef_ref, [cell] + [off_ref[d : d + 1, leaving] for d in range(3)])
+        else:
+            pack(ef_ref, [v_ref[c : c + 1, leaving] for c in range(COMPS)] + [tau_ref[:, leaving]])
         for c in range(COMPS):
             ym_ref[c : c + 1, :] = (
                 scal(below, PIVOT) * own_in[c : c + 1]
@@ -381,10 +458,10 @@
 ):
     comps, cells_x, cells_y, cells_z = velocity.shape
     assert (comps, cells_x, cells_y) == (COMPS, 1, 16)
+    assert cells_z == 2 * CAP and SECTIONS == 3
     slots = particle_vel.shape[1]
     size_x, size_y = lax.axis_size("gx"), lax.axis_size("gy")
     assert size_x % 2 == 0 and size_y % 2 == 0
-    ring_x = [(i, (i + 1) % size_x) for i in range(size_x)]
     diagonal = [
         ((x + 1) % size_x * size_y + (y + 1) % size_y, x * size_y + y)
         for x in range(size_x)
@@ -397,8 +474,7 @@
         far = lax.ppermute(block, "gx", next_pair)
         return lax.ppermute(block, "gx", same_pair), far
 
-    ring_y = [(i, (i + 1) % size_y) for i in range(size_y)]
-    back_y = [(b, a) for a, b in ring_y]
+    next_to = [(i, (i + (1 if i % 2 else -1)) % size_y) for i in range(size_y)]
     flip = lambda bits: [(i, i ^ bits) for i in range(size_y)]
     mixed = [(i, i ^ (4 if i % 2 else 2)) for i in range(size_y)]
     direct = size_y == 8
@@ -407,21 +483,22 @@
     first = velocity[:, 0, 0, :]
     final = velocity[:, 0, cells_y - 1, :]
     planes = both_sides(u)
-    yp = lax.ppermute(first, "gy", back_y)
-    ym = lax.ppermute(final, "gy", ring_y)
     corner = lax.ppermute(first, ("gx", "gy"), diagonal)
+    both = jnp.concatenate([first, final], axis=0)
+    ym = lax.ppermute(both, "gy", next_to)
+    yp = lax.ppermute(both, "gy", flip(1))
     edges = (corner, corner)
 
     cell = particle_cell.reshape(1, slots)
     tau = inverse_tau.reshape(1, slots)
     like = lambda *shape: jax.ShapeDtypeStruct(shape, F32)
-    matrix, answer, scal, live = call(
-        tables_kernel,
+    matrix, answer, scal, places = call(
+        functools.partial(tables_kernel, cells_z),
         (like(SECTIONS, 56, 128), like(SECTIONS, cells_y, 128), like(SECTIONS, 2, 128),
-         like(1, slots)),
-        scalars(5),
+         like(8, slots)),
+        scalars(5) + whole_in_vmem(2),
         "tables",
-    )(forward_rate, backward_rate, pivot_inv, y_metric, outgoing_count)
+    )(forward_rate, backward_rate, pivot_inv, y_metric, outgoing_count, cell, particle_offset)
     v = particle_vel
     rows = COMPS * cells_y
     field_like, slots_like = like(rows, cells_z), like(COMPS, slots)
@@ -433,30 +510,34 @@
             whole_in_vmem(3),
             "own_plane",
             [pltpu.VMEM((4 * rows, cells_z), BF16)],
-        )(u, cell, particle_offset)
+        )(u, places, particle_offset)
         sides = (u, ym, *planes, yp, *edges)
         out = call(
             functools.partial(section_kernel, k, TIME_STEP * SECTION_WEIGHTS[k], last),
-            (field_like, like(16 if last else 8, cells_z), slots_like)
-            + ((like(COMPS, CAP),) if last else ()),
-            whole_in_vmem(len(sides) + 9),
+            (field_like, like(16 if last else 8, cells_z), slots_like),
+            whole_in_vmem(len(sides) + 8),
             "section",
             [
                 pltpu.VMEM((4 * (rows + 8), cells_z), BF16),
                 pltpu.VMEM((2 * rows * (cells_z // DEPTH), slots), BF16),
                 pltpu.VMEM((slots, DEPTH), BF16),
             ],
-        )(*sides, cell, particle_offset, tau, live, v, near, matrix, answer, scal)
+        )(*sides, places, particle_offset, tau, v, near, matrix, answer, scal)
         w, pq, v = out[:3]
         if last:
-            from_x = lax.ppermute(out[3], "gx", ring_x)
+            from_x = call(
+                functools.partial(visitors_kernel, k, TIME_STEP * SECTION_WEIGHTS[k]),
+                like(COMPS, CAP),
+                whole_in_vmem(9),
+                "visitors",
+            )(u, yp, *planes, *edges, *old_edges, answer)
         if direct:
             partner = lax.ppermute(pq, "gy", flip(1))
+            if last:
+                partner, from_x = lax.optimization_barrier((partner, from_x))
             pair = jnp.stack([pq[:8], partner[:8]])
             side = lax.ppermute(pair, "gy", mixed)
             far = lax.ppermute(pair, "gy", flip(6))
-            if last:
-                side, from_x = lax.optimization_barrier((side, from_x))
             other = lax.ppermute(side, "gy", flip(1))
             gathered = (pq, partner, side, other, far)
             scratch = [pltpu.VMEM((size_y, 8, cells_z), F32)]
@@ -467,7 +548,8 @@
             more, shapes = (v, from_x), (field_like, slots_like)
         else:
             planes = both_sides(w)
-            more, shapes = (), (field_like, like(8, cells_z), like(COMPS, cells_z))
+            more = (places, particle_offset, tau, v)
+            shapes = (field_like, like(8, cells_z), like(COMPS, cells_z))
         if k == 0:
             shapes = shapes + (like(size_y, 2, 128 * SECTIONS),)
         else:
@@ -483,7 +565,7 @@
             u, yp, ym = joined[:3]
             if k == 0:
                 known = joined[3]
-            edges = both_sides(yp)
+            old_edges, edges = edges, both_sides(yp)
     u, moved = joined
     return (u.reshape(velocity.shape), moved)
 

time: 68.1 us -> 66.5 us (0.977)
  waiting for transfers between devices: 18 us -> 15.9 us
  starting transfers between devices: 29.1 us -> 28.2 us
  Pallas kernels: 17.9 us -> 18.6 us
    ppermute x3 -> x2, waiting for transfers between devices: 3.12 us -> 0.01 us  [the longest x1 0.01 us: on_device(): yp = lax.ppermute(both, 'gy', flip(1))]
    ppermute x1, starting transfers between devices: 2.95 us -> 0.5 us  [on_device(): corner = lax.ppermute(first, ('gx', 'gy'), diagonal)]
    ppermute x3, waiting for transfers between devices: 4.47 us -> 6.75 us  [on_device(): side = lax.ppermute(pair, 'gy', mixed)]
    ppermute x3 -> x2, starting transfers between devices: 1.08 us -> 2.62 us  [the longest x1 2.55 us: on_device(): ym = lax.ppermute(both, 'gy', next_to)]
    pallas_call x1 -> x2, Pallas kernels: 0.88 us -> 1.75 us  [the longest x1 0.91 us: on_device(): call(functools.partial(tables_kernel, cells_z), (like(SECTIONS, 56, 128),...]
    ppermute x3, waiting for transfers between devices: 1.23 us -> 0.38 us  [on_device(): partner = lax.ppermute(pq, 'gy', flip(1))]
    ppermute x3, waiting for transfers between devices: 3.43 us -> 4.26 us  [on_device(): far = lax.ppermute(pair, 'gy', flip(6))]
    ppermute x3, waiting for transfers between devices: 0.78 us -> 0.09 us  [on_device(): other = lax.ppermute(side, 'gy', flip(1))]
  transfers between devices with their start and end apart: 26 -> 25, of which waited for: 13 -> 12; matrix products, arithmetic and copies ran while one was open for 2% -> 2% of each run, Pallas kernels for 10% -> 11%
where the time goes in v5:
time: 66.5 us; the launch traced here: 66.3 us
  starting transfers between devices  28.2 us (42%)
  Pallas kernels  18.6 us (28%)
  waiting for transfers between devices  15.9 us (24%)
  local copies, waits for them, and re-layouts  2.61 us (4%)
  between operations  0.91 us (1%)
    ppermute x5, starting transfers between devices, both_sides(): far = lax.ppermute(block, 'gx', next_pair)  13.4 us
    pallas_call x3, Pallas kernels, on_device(): call(functools.partial(section_kernel, k, TIME_STEP * SECTION_WEIGHTS[k],...  10.3 us
    ppermute x3, waiting for transfers between devices, on_device(): side = lax.ppermute(pair, 'gy', mixed)  6.75 us
    pallas_call x3, Pallas kernels, on_device(): call(own_plane_kernel, slots_like, whole_in_vmem(3), 'own_plane', [pltpu....  5.18 us
    ppermute x3, starting transfers between devices, on_device(): far = lax.ppermute(pair, 'gy', flip(6))  4.47 us
    ppermute x3, waiting for transfers between devices, on_device(): far = lax.ppermute(pair, 'gy', flip(6))  4.26 us
    ppermute x3, starting transfers between devices, on_device(): side = lax.ppermute(pair, 'gy', mixed)  3.41 us
    ppermute x5, waiting for transfers between devices, both_sides(): far = lax.ppermute(block, 'gx', next_pair)  3.06 us
  transfers between devices with their start and end apart: 25, of which 12 were waited for; matrix products, arithmetic and copies ran while one was open for 2% of the time, Pallas kernels for 11%

profile of v5, /device:TPU:0, one launch (start us, length us, event | category | flops | bytes accessed | tf_op | source)
XLA Modules:
  0.0 66.3 jit_solution(17281328199688528643)
XLA Ops:
  0.6 5.1 %collective-permute-start.2 = (f32[48,1024]{1,0:T(8,128)}, f32[48,1024]{1,0:T(8,128)S(1)}, u32[]{:S(2)}, u32[]{:S(2)}) collective-permute-start(f32[48,1024]{1,0:T(8,128)} %bitcast.18), channel_id=1, source_target_pairs={{0,24},{8,16},{16,8},{24,0},{1,25},{9,17},{17,9},{25,1},{2,26},{10... | collective-permute-start | bytes 589832 | tf_op jit(solution)/shard_map/ppermute | solution.py:474
  5.7 1.0 %fusion = (f32[3,1,1,1024]{3,2,1,0:T(1,128)S(1)}, f32[3,1,1,1024]{3,2,1,0:T(1,128)S(1)}) fusion(f32[3,1,16,1024]{3,2,1,0:T(8,128)} %param.10), kind=kLoop, calls=%fused_computation.8 | loop fusion | bytes 49152 | tf_op jit(solution)/shard_map/slice | solution.py:483
  6.9 2.5 %collective-permute-start = (f32[6,1024]{1,0:T(8,128)S(1)}, f32[6,1024]{1,0:T(8,128)S(1)}, u32[]{:S(2)}, u32[]{:S(2)}) collective-permute-start(f32[6,1024]{1,0:T(8,128)S(1)} %pad_maximum_fusion.3), channel_id=1, source_target_pairs={{0,7},{1,2},{2,1},{3,4},{4,3},{5,6},{6,5},{7,0},{8,15},{9,10},{10,... | collective-permute-start | bytes 73736 | tf_op jit(solution)/shard_map/ppermute | solution.py:488
  10.7 0.9 %tables.1 = (f32[3,56,128]{2,1,0:T(8,128)S(1)}, f32[3,16,128]{2,1,0:T(8,128)S(1)}, f32[3,2,128]{2,1,0:T(2,128)S(1)}, f32[8,3584]{1,0:T(8,128)S(1)}) custom-call(f32[3,16]{1,0:T(4,128)S(1)} %copy-done.3, f32[3,16]{1,0:T(4,128)S(1)} %copy-done.4, f32[3,16]{1,0:T(4,128)S(1)} %copy-done.5, f32[16]{0:T(128)S(1)} %copy-done.6, s32[1,1,3]{2,1,0:T(1,128)S(1)} %copy-done.7, ...), custom_call_target="tpu_custom_call" | custom-call | tf_op jit(solution)/shard_map/tables/pallas_call | solution.py:495
  11.6 0.9 %copy-done.1 = f32[3,1,16,1024]{3,2,1,0:T(8,128)S(1)} copy-done((f32[3,1,16,1024]{3,2,1,0:T(8,128)S(1)}, f32[3,1,16,1024]{3,2,1,0:T(8,128)}, u32[]{:S(2)}) %copy-start.1) | copy-done | bytes 196632
  12.5 1.7 %own_plane.3.refs_11_ = f32[3,3584]{1,0:T(4,128)S(1)} custom-call(f32[48,1024]{1,0:T(8,128)S(1)} %bitcast.20, f32[8,3584]{1,0:T(8,128)S(1)} %get-tuple-element.26.slots_ref.refs_7_.refs_8_, f32[3,3584]{1,0:T(4,128)S(1)} %copy-done), custom_call_target="tpu_custom_call" | custom-call | tf_op jit(solution)/shard_map/own_plane/pallas_call | solution.py:507
  14.2 1.2 %collective-permute-done.4.refs_5_.refs_6_ = f32[3,1024]{1,0:T(4,128)S(1)} collective-permute-done((f32[3,1024]{1,0:T(4,128)S(1)}, f32[3,1024]{1,0:T(4,128)S(1)}, u32[]{:S(2)}, u32[]{:S(2)}) %collective-permute-start.4) | collective-permute-done | bytes 12320 | tf_op jit(solution)/shard_map/ppermute | solution.py:486
  15.5 3.4 %section.3 = (f32[48,1024]{1,0:T(8,128)S(1)}, f32[8,1024]{1,0:T(8,128)S(1)}, f32[3,3584]{1,0:T(4,128)S(1)}) custom-call(f32[48,1024]{1,0:T(8,128)S(1)} %bitcast.21, f32[6,1024]{1,0:T(8,128)S(1)} %collective-permute-done.refs_1_, f32[48,1024]{1,0:T(8,128)S(1)} %collective-permute-done.1.refs_2_, f32[48,1024]{1,0:T(8,128)S(1)} %collective-permute-done.2.refs_3_, ...), custom_call_target="tpu_custom_call" | custom-call | tf_op jit(solution)/shard_map/section/pallas_call | solution.py:515
  18.9 0.9 %collective-permute-start.5 = (f32[8,1024]{1,0:T(8,128)S(1)}, f32[8,1024]{1,0:T(8,128)S(1)}, u32[]{:S(2)}, u32[]{:S(2)}) collective-permute-start(f32[8,1024]{1,0:T(8,128)S(1)} %get-tuple-element.30.refs_0_), channel_id=1, source_target_pairs={{0,1},{1,0},{2,3},{3,2},{4,5},{5,4},{6,7},{7,6},{8,9},{9,8},{10,11... | collective-permute-start | bytes 98312 | tf_op jit(solution)/shard_map/ppermute | solution.py:535
  19.8 3.5 %collective-permute-start.10 = (f32[48,1024]{1,0:T(8,128)S(1)}, f32[48,1024]{1,0:T(8,128)S(1)}, u32[]{:S(2)}, u32[]{:S(2)}) collective-permute-start(f32[48,1024]{1,0:T(8,128)S(1)} %get-tuple-element.31.refs_5_), channel_id=1, source_target_pairs={{0,24},{8,16},{16,8},{24,0},{1,25},{9,17},{17,9},{25,1},{2,26},{10... | collective-permute-start | bytes 589832 | tf_op jit(solution)/shard_map/ppermute | solution.py:474
  23.3 1.6 %collective-permute-start.6 = (f32[2,8,1024]{2,1,0:T(8,128)S(1)}, f32[2,8,1024]{2,1,0:T(8,128)S(1)}, u32[]{:S(2)}, u32[]{:S(2)}) collective-permute-start(f32[2,8,1024]{2,1,0:T(8,128)S(1)} %pad_maximum_fusion), channel_id=1, source_target_pairs={{0,2},{1,5},{2,0},{3,7},{4,6},{5,1},{6,4},{7,3},{8,10},{9,13},{10,... | collective-permute-start | bytes 196616 | tf_op jit(solution)/shard_map/ppermute | solution.py:539
  24.8 1.5 %collective-permute-start.8 = (f32[2,8,1024]{2,1,0:T(8,128)S(1)}, f32[2,8,1024]{2,1,0:T(8,128)S(1)}, u32[]{:S(2)}, u32[]{:S(2)}) collective-permute-start(f32[2,8,1024]{2,1,0:T(8,128)S(1)} %pad_maximum_fusion), channel_id=1, source_target_pairs={{0,6},{1,7},{2,4},{3,5},{4,2},{5,3},{6,0},{7,1},{8,14},{9,15},{10,... | collective-permute-start | bytes 196616 | tf_op jit(solution)/shard_map/ppermute | solution.py:540
  26.3 2.0 %collective-permute-done.6.refs_2_ = f32[2,8,1024]{2,1,0:T(8,128)S(1)} collective-permute-done((f32[2,8,1024]{2,1,0:T(8,128)S(1)}, f32[2,8,1024]{2,1,0:T(8,128)S(1)}, u32[]{:S(2)}, u32[]{:S(2)}) %collective-permute-start.6) | collective-permute-done | bytes 65568 | tf_op jit(solution)/shard_map/ppermute | solution.py:539
  28.3 1.7 %collective-permute-done.8.refs_4_ = f32[2,8,1024]{2,1,0:T(8,128)S(1)} collective-permute-done((f32[2,8,1024]{2,1,0:T(8,128)S(1)}, f32[2,8,1024]{2,1,0:T(8,128)S(1)}, u32[]{:S(2)}, u32[]{:S(2)}) %collective-permute-start.8) | collective-permute-done | bytes 65568 | tf_op jit(solution)/shard_map/ppermute | solution.py:540
  31.1 1.3 %collective-permute-start.11 = (f32[8,1024]{1,0:T(8,128)S(1)}, f32[8,1024]{1,0:T(8,128)S(1)}, u32[]{:S(2)}, u32[]{:S(2)}) collective-permute-start(f32[8,1024]{1,0:T(8,128)S(1)} %get-tuple-element.35.refs_4_), channel_id=1, source_target_pairs={{0,8},{8,0},{16,24},{24,16},{1,9},{9,1},{17,25},{25,17},{2,10},{10... | collective-permute-start | bytes 98312 | tf_op jit(solution)/shard_map/ppermute | solution.py:475
  32.4 1.7 %own_plane.4.refs_11_ = f32[3,3584]{1,0:T(4,128)S(1)} custom-call(f32[48,1024]{1,0:T(8,128)S(1)} %get-tuple-element.33.u_ref.refs_0_, f32[8,3584]{1,0:T(8,128)S(1)} %get-tuple-element.26.slots_ref.refs_7_.refs_8_, f32[3,3584]{1,0:T(4,128)S(1)} %copy-done), custom_call_target="tpu_custom_call" | custom-call | tf_op jit(solution)/shard_map/own_plane/pallas_call | solution.py:507
  34.1 2.0 %collective-permute-done.12.refs_6_.far_old_ref = f32[8,1024]{1,0:T(8,128)S(1)} collective-permute-done((f32[8,1024]{1,0:T(8,128)S(1)}, f32[8,1024]{1,0:T(8,128)S(1)}, u32[]{:S(2)}, u32[]{:S(2)}) %collective-permute-start.12) | collective-permute-done | bytes 32800 | tf_op jit(solution)/shard_map/ppermute | solution.py:474
  36.1 3.5 %section.4 = (f32[48,1024]{1,0:T(8,128)S(1)}, f32[8,1024]{1,0:T(8,128)S(1)}, f32[3,3584]{1,0:T(4,128)S(1)}) custom-call(f32[48,1024]{1,0:T(8,128)S(1)} %get-tuple-element.33.u_ref.refs_0_, f32[3,1024]{1,0:T(4,128)S(1)} %get-tuple-element.34.refs_1_, f32[48,1024]{1,0:T(8,128)S(1)} %collective-permute-done.9.refs_2_, ...), custom_call_target="tpu_custom_call" | custom-call | tf_op jit(solution)/shard_map/section/pallas_call | solution.py:515
  39.6 2.1 %collective-permute-start.18 = (f32[48,1024]{1,0:T(8,128)S(1)}, f32[48,1024]{1,0:T(8,128)S(1)}, u32[]{:S(2)}, u32[]{:S(2)}) collective-permute-start(f32[48,1024]{1,0:T(8,128)S(1)} %get-tuple-element.37.refs_5_), channel_id=1, source_target_pairs={{0,24},{8,16},{16,8},{24,0},{1,25},{9,17},{17,9},{25,1},{2,26},{10... | collective-permute-start | bytes 589832 | tf_op jit(solution)/shard_map/ppermute | solution.py:474
  42.8 1.5 %collective-permute-start.16 = (f32[2,8,1024]{2,1,0:T(8,128)S(1)}, f32[2,8,1024]{2,1,0:T(8,128)S(1)}, u32[]{:S(2)}, u32[]{:S(2)}) collective-permute-start(f32[2,8,1024]{2,1,0:T(8,128)S(1)} %pad_maximum_fusion.1), channel_id=1, source_target_pairs={{0,6},{1,7},{2,4},{3,5},{4,2},{5,3},{6,0},{7,1},{8,14},{9,15},{10,... | collective-permute-start | bytes 196616 | tf_op jit(solution)/shard_map/ppermute | solution.py:540
  44.3 2.5 %collective-permute-done.14.refs_2_ = f32[2,8,1024]{2,1,0:T(8,128)S(1)} collective-permute-done((f32[2,8,1024]{2,1,0:T(8,128)S(1)}, f32[2,8,1024]{2,1,0:T(8,128)S(1)}, u32[]{:S(2)}, u32[]{:S(2)}) %collective-permute-start.14) | collective-permute-done | bytes 65568 | tf_op jit(solution)/shard_map/ppermute | solution.py:539
  46.8 1.2 %collective-permute-done.16.refs_4_ = f32[2,8,1024]{2,1,0:T(8,128)S(1)} collective-permute-done((f32[2,8,1024]{2,1,0:T(8,128)S(1)}, f32[2,8,1024]{2,1,0:T(8,128)S(1)}, u32[]{:S(2)}, u32[]{:S(2)}) %collective-permute-start.16) | collective-permute-done | bytes 65568 | tf_op jit(solution)/shard_map/ppermute | solution.py:540
  48.3 1.9 %collective-permute-start.20 = (f32[8,1024]{1,0:T(8,128)S(1)}, f32[8,1024]{1,0:T(8,128)S(1)}, u32[]{:S(2)}, u32[]{:S(2)}) collective-permute-start(f32[8,1024]{1,0:T(8,128)S(1)} %get-tuple-element.42.refs_4_.ef_ref), channel_id=1, source_target_pairs={{0,24},{8,16},{16,8},{24,0},{1,25},{9,17},{17,9},{25,1},{2,26},{10... | collective-permute-start | bytes 98312 | tf_op jit(solution)/shard_map/ppermute | solution.py:474
  50.2 1.1 %collective-permute-start.19 = (f32[8,1024]{1,0:T(8,128)S(1)}, f32[8,1024]{1,0:T(8,128)S(1)}, u32[]{:S(2)}, u32[]{:S(2)}) collective-permute-start(f32[8,1024]{1,0:T(8,128)S(1)} %get-tuple-element.42.refs_4_.ef_ref), channel_id=1, source_target_pairs={{0,8},{8,0},{16,24},{24,16},{1,9},{9,1},{17,25},{25,17},{2,10},{10... | collective-permute-start | bytes 98312 | tf_op jit(solution)/shard_map/ppermute | solution.py:475
  51.3 1.9 %own_plane.5.refs_11_ = f32[3,3584]{1,0:T(4,128)S(1)} custom-call(f32[48,1024]{1,0:T(8,128)S(1)} %get-tuple-element.40.u_ref.refs_0_, f32[8,3584]{1,0:T(8,128)S(1)} %get-tuple-element.26.slots_ref.refs_7_.refs_8_, f32[3,3584]{1,0:T(4,128)S(1)} %copy-done), custom_call_target="tpu_custom_call" | custom-call | tf_op jit(solution)/shard_map/own_plane/pallas_call | solution.py:507
  53.2 1.1 %collective-permute-done.20.refs_6_.far_ef_ref = f32[8,1024]{1,0:T(8,128)S(1)} collective-permute-done((f32[8,1024]{1,0:T(8,128)S(1)}, f32[8,1024]{1,0:T(8,128)S(1)}, u32[]{:S(2)}, u32[]{:S(2)}) %collective-permute-start.20) | collective-permute-done | bytes 32800 | tf_op jit(solution)/shard_map/ppermute | solution.py:474
  54.5 3.4 %section.5 = (f32[48,1024]{1,0:T(8,128)S(1)}, f32[16,1024]{1,0:T(8,128)S(1)}, f32[3,3584]{1,0:T(4,128)S(1)}) custom-call(f32[48,1024]{1,0:T(8,128)S(1)} %get-tuple-element.40.u_ref.refs_0_, f32[3,1024]{1,0:T(4,128)S(1)} %get-tuple-element.41.refs_1_, f32[48,1024]{1,0:T(8,128)S(1)} %collective-permute-done.17.refs_2_.near_x_ref, ...), custom_call_target="tpu_custom_call" | custom-call | tf_op jit(solution)/shard_map/section/pallas_call | solution.py:515
  59.2 1.0 %collective-permute-start.22 = (f32[2,8,1024]{2,1,0:T(8,128)S(1)}, f32[2,8,1024]{2,1,0:T(8,128)S(1)}, u32[]{:S(2)}, u32[]{:S(2)}) collective-permute-start(f32[2,8,1024]{2,1,0:T(8,128)S(1)} %pad_maximum_fusion.2), channel_id=1, source_target_pairs={{0,2},{1,5},{2,0},{3,7},{4,6},{5,1},{6,4},{7,3},{8,10},{9,13},{10,... | collective-permute-start | bytes 196616 | tf_op jit(solution)/shard_map/ppermute | solution.py:539
  60.2 1.5 %collective-permute-start.24 = (f32[2,8,1024]{2,1,0:T(8,128)S(1)}, f32[2,8,1024]{2,1,0:T(8,128)S(1)}, u32[]{:S(2)}, u32[]{:S(2)}) collective-permute-start(f32[2,8,1024]{2,1,0:T(8,128)S(1)} %pad_maximum_fusion.2), channel_id=1, source_target_pairs={{0,6},{1,7},{2,4},{3,5},{4,2},{5,3},{6,0},{7,1},{8,14},{9,15},{10,... | collective-permute-start | bytes 196616 | tf_op jit(solution)/shard_map/ppermute | solution.py:540
  61.7 2.3 %collective-permute-done.22.refs_2_ = f32[2,8,1024]{2,1,0:T(8,128)S(1)} collective-permute-done((f32[2,8,1024]{2,1,0:T(8,128)S(1)}, f32[2,8,1024]{2,1,0:T(8,128)S(1)}, u32[]{:S(2)}, u32[]{:S(2)}) %collective-permute-start.22) | collective-permute-done | bytes 65568 | tf_op jit(solution)/shard_map/ppermute | solution.py:539
  64.0 1.4 %collective-permute-done.24.refs_4_ = f32[2,8,1024]{2,1,0:T(8,128)S(1)} collective-permute-done((f32[2,8,1024]{2,1,0:T(8,128)S(1)}, f32[2,8,1024]{2,1,0:T(8,128)S(1)}, u32[]{:S(2)}, u32[]{:S(2)}) %collective-permute-start.24) | collective-permute-done | bytes 65568 | tf_op jit(solution)/shard_map/ppermute | solution.py:540
  65.4 0.9 %join.5 = (f32[48,1024]{1,0:T(8,128)}, f32[3,3584]{1,0:T(4,128)}) custom-call(f32[16,1024]{1,0:T(8,128)S(1)} %get-tuple-element.43.refs_0_, f32[16,1024]{1,0:T(8,128)S(1)} %collective-permute-done.21.refs_1_, f32[2,8,1024]{2,1,0:T(8,128)S(1)} %collective-permute-done.22.refs_2_, f32[2,8,1024]{2,1,0:T(8,128)S(1)} %collective-permute-done.23.refs_3_, ...), custom_call_target="tpu_custom_call" | custom-call | tf_op jit(solution)/shard_map/join/pallas_call | solution.py:557
  (60 shorter events, 5.4 us)
Async XLA Ops:
  0.6 14.8 %collective-permute-start.2 = (f32[48,1024]{1,0:T(8,128)}, f32[48,1024]{1,0:T(8,128)S(1)}, u32[]{:S(2)}, u32[]{:S(2)}) collective-permute-start(f32[48,1024]{1,0:T(8,128)} %bitcast.18), channel_id=1, source_target_pairs={{0,24},{8,16},{16,8},{24,0},{1,25},{9,17},{17,9},{25,1},{2,26},{10... | collective-permute-start | bytes 589832 | tf_op jit(solution)/shard_map/ppermute | solution.py:474
  5.7 9.7 %collective-permute-start.1 = (f32[48,1024]{1,0:T(8,128)}, f32[48,1024]{1,0:T(8,128)S(1)}, u32[]{:S(2)}, u32[]{:S(2)}) collective-permute-start(f32[48,1024]{1,0:T(8,128)} %bitcast.19), channel_id=1, source_target_pairs={{0,8},{8,0},{16,24},{24,16},{1,9},{9,1},{17,25},{25,17},{2,10},{10... | collective-permute-start | bytes 589832 | tf_op jit(solution)/shard_map/ppermute | solution.py:475
  6.8 3.2 %copy-start.8 = (f32[3584]{0:T(1024)S(1)}, f32[3584]{0:T(1024)}, u32[]{:S(2)}) copy-start(f32[3584]{0:T(1024)} %param.18) | copy-start | bytes 43012
  6.8 3.3 %copy-start = (f32[3,3584]{1,0:T(4,128)S(1)}, f32[3,3584]{1,0:T(4,128)}, u32[]{:S(2)}) copy-start(f32[3,3584]{1,0:T(4,128)} %refs_8_.7) | copy-start | bytes 129028
  6.8 3.2 %copy-start.9 = (s32[3584]{0:T(1024)S(1)}, s32[3584]{0:T(1024)}, u32[]{:S(2)}) copy-start(s32[3584]{0:T(1024)} %param.16) | copy-start | bytes 43012
  6.8 8.6 %collective-permute-start.3 = (f32[6,1024]{1,0:T(8,128)S(1)}, f32[6,1024]{1,0:T(8,128)S(1)}, u32[]{:S(2)}, u32[]{:S(2)}) collective-permute-start(f32[6,1024]{1,0:T(8,128)S(1)} %pad_maximum_fusion.3), channel_id=1, source_target_pairs={{0,1},{1,0},{2,3},{3,2},{4,5},{5,4},{6,7},{7,6},{8,9},{9,8},{10,11... | collective-permute-start | bytes 73736 | tf_op jit(solution)/shard_map/ppermute | solution.py:489
  6.9 8.5 %collective-permute-start = (f32[6,1024]{1,0:T(8,128)S(1)}, f32[6,1024]{1,0:T(8,128)S(1)}, u32[]{:S(2)}, u32[]{:S(2)}) collective-permute-start(f32[6,1024]{1,0:T(8,128)S(1)} %pad_maximum_fusion.3), channel_id=1, source_target_pairs={{0,7},{1,2},{2,1},{3,4},{4,3},{5,6},{6,5},{7,0},{8,15},{9,10},{10,... | collective-permute-start | bytes 73736 | tf_op jit(solution)/shard_map/ppermute | solution.py:488
  9.4 6.0 %collective-permute-start.4 = (f32[3,1024]{1,0:T(4,128)S(1)}, f32[3,1024]{1,0:T(4,128)S(1)}, u32[]{:S(2)}, u32[]{:S(2)}) collective-permute-start(f32[3,1024]{1,0:T(4,128)S(1)} %bitcast.27), channel_id=1, source_target_pairs={{9,0},{10,1},{11,2},{12,3},{13,4},{14,5},{15,6},{8,7},{17,8},{18,9... | collective-permute-start | bytes 36872 | tf_op jit(solution)/shard_map/ppermute | solution.py:486
  10.0 0.7 %copy-start.4 = (f32[3,16]{1,0:T(4,128)S(1)}, f32[3,16]{1,0:T(4,128)}, u32[]{:S(2)}) copy-start(f32[3,16]{1,0:T(4,128)} %up_ref.1) | copy-start | bytes 580
  10.0 0.7 %copy-start.5 = (f32[3,16]{1,0:T(4,128)S(1)}, f32[3,16]{1,0:T(4,128)}, u32[]{:S(2)}) copy-start(f32[3,16]{1,0:T(4,128)} %scale_ref.1) | copy-start | bytes 580
  11.6 0.9 %copy-start.1 = (f32[3,1,16,1024]{3,2,1,0:T(8,128)S(1)}, f32[3,1,16,1024]{3,2,1,0:T(8,128)}, u32[]{:S(2)}) copy-start(f32[3,1,16,1024]{3,2,1,0:T(8,128)} %param.10) | copy-start | bytes 589828
  12.5 2.9 %copy-start.2 = (f32[3,3584]{1,0:T(4,128)S(1)}, f32[3,3584]{1,0:T(4,128)}, u32[]{:S(2)}) copy-start(f32[3,3584]{1,0:T(4,128)} %refs_10_.1) | copy-start | bytes 129028
  18.9 4.4 %collective-permute-start.5 = (f32[8,1024]{1,0:T(8,128)S(1)}, f32[8,1024]{1,0:T(8,128)S(1)}, u32[]{:S(2)}, u32[]{:S(2)}) collective-permute-start(f32[8,1024]{1,0:T(8,128)S(1)} %get-tuple-element.30.refs_0_), channel_id=1, source_target_pairs={{0,1},{1,0},{2,3},{3,2},{4,5},{5,4},{6,7},{7,6},{8,9},{9,8},{10,11... | collective-permute-start | bytes 98312 | tf_op jit(solution)/shard_map/ppermute | solution.py:535
  19.8 16.3 %collective-permute-start.10 = (f32[48,1024]{1,0:T(8,128)S(1)}, f32[48,1024]{1,0:T(8,128)S(1)}, u32[]{:S(2)}, u32[]{:S(2)}) collective-permute-start(f32[48,1024]{1,0:T(8,128)S(1)} %get-tuple-element.31.refs_5_), channel_id=1, source_target_pairs={{0,24},{8,16},{16,8},{24,0},{1,25},{9,17},{17,9},{25,1},{2,26},{10... | collective-permute-start | bytes 589832 | tf_op jit(solution)/shard_map/ppermute | solution.py:474
  23.3 12.8 %collective-permute-start.9 = (f32[48,1024]{1,0:T(8,128)S(1)}, f32[48,1024]{1,0:T(8,128)S(1)}, u32[]{:S(2)}, u32[]{:S(2)}) collective-permute-start(f32[48,1024]{1,0:T(8,128)S(1)} %get-tuple-element.31.refs_5_), channel_id=1, source_target_pairs={{0,8},{8,0},{16,24},{24,16},{1,9},{9,1},{17,25},{25,17},{2,10},{10... | collective-permute-start | bytes 589832 | tf_op jit(solution)/shard_map/ppermute | solution.py:475
  23.3 5.0 %collective-permute-start.6 = (f32[2,8,1024]{2,1,0:T(8,128)S(1)}, f32[2,8,1024]{2,1,0:T(8,128)S(1)}, u32[]{:S(2)}, u32[]{:S(2)}) collective-permute-start(f32[2,8,1024]{2,1,0:T(8,128)S(1)} %pad_maximum_fusion), channel_id=1, source_target_pairs={{0,2},{1,5},{2,0},{3,7},{4,6},{5,1},{6,4},{7,3},{8,10},{9,13},{10,... | collective-permute-start | bytes 196616 | tf_op jit(solution)/shard_map/ppermute | solution.py:539
  24.8 5.2 %collective-permute-start.8 = (f32[2,8,1024]{2,1,0:T(8,128)S(1)}, f32[2,8,1024]{2,1,0:T(8,128)S(1)}, u32[]{:S(2)}, u32[]{:S(2)}) collective-permute-start(f32[2,8,1024]{2,1,0:T(8,128)S(1)} %pad_maximum_fusion), channel_id=1, source_target_pairs={{0,6},{1,7},{2,4},{3,5},{4,2},{5,3},{6,0},{7,1},{8,14},{9,15},{10,... | collective-permute-start | bytes 196616 | tf_op jit(solution)/shard_map/ppermute | solution.py:540
  28.3 1.7 %collective-permute-start.7 = (f32[2,8,1024]{2,1,0:T(8,128)S(1)}, f32[2,8,1024]{2,1,0:T(8,128)S(1)}, u32[]{:S(2)}, u32[]{:S(2)}) collective-permute-start(f32[2,8,1024]{2,1,0:T(8,128)S(1)} %collective-permute-done.6.refs_2_), channel_id=1, source_target_pairs={{0,1},{1,0},{2,3},{3,2},{4,5},{5,4},{6,7},{7,6},{8,9},{9,8},{10,11... | collective-permute-start | bytes 196616 | tf_op jit(solution)/shard_map/ppermute | solution.py:541
  30.3 5.8 %collective-permute-start.12 = (f32[8,1024]{1,0:T(8,128)S(1)}, f32[8,1024]{1,0:T(8,128)S(1)}, u32[]{:S(2)}, u32[]{:S(2)}) collective-permute-start(f32[8,1024]{1,0:T(8,128)S(1)} %get-tuple-element.35.refs_4_), channel_id=1, source_target_pairs={{0,24},{8,16},{16,8},{24,0},{1,25},{9,17},{17,9},{25,1},{2,26},{10... | collective-permute-start | bytes 98312 | tf_op jit(solution)/shard_map/ppermute | solution.py:474
  31.1 4.9 %collective-permute-start.11 = (f32[8,1024]{1,0:T(8,128)S(1)}, f32[8,1024]{1,0:T(8,128)S(1)}, u32[]{:S(2)}, u32[]{:S(2)}) collective-permute-start(f32[8,1024]{1,0:T(8,128)S(1)} %get-tuple-element.35.refs_4_), channel_id=1, source_target_pairs={{0,8},{8,0},{16,24},{24,16},{1,9},{9,1},{17,25},{25,17},{2,10},{10... | collective-permute-start | bytes 98312 | tf_op jit(solution)/shard_map/ppermute | solution.py:475
  39.5 2.4 %collective-permute-start.13 = (f32[8,1024]{1,0:T(8,128)S(1)}, f32[8,1024]{1,0:T(8,128)S(1)}, u32[]{:S(2)}, u32[]{:S(2)}) collective-permute-start(f32[8,1024]{1,0:T(8,128)S(1)} %get-tuple-element.36.refs_0_), channel_id=1, source_target_pairs={{0,1},{1,0},{2,3},{3,2},{4,5},{5,4},{6,7},{7,6},{8,9},{9,8},{10,11... | collective-permute-start | bytes 98312 | tf_op jit(solution)/shard_map/ppermute | solution.py:535
  39.6 14.8 %collective-permute-start.18 = (f32[48,1024]{1,0:T(8,128)S(1)}, f32[48,1024]{1,0:T(8,128)S(1)}, u32[]{:S(2)}, u32[]{:S(2)}) collective-permute-start(f32[48,1024]{1,0:T(8,128)S(1)} %get-tuple-element.37.refs_5_), channel_id=1, source_target_pairs={{0,24},{8,16},{16,8},{24,0},{1,25},{9,17},{17,9},{25,1},{2,26},{10... | collective-permute-start | bytes 589832 | tf_op jit(solution)/shard_map/ppermute | solution.py:474
  41.7 12.8 %collective-permute-start.17 = (f32[48,1024]{1,0:T(8,128)S(1)}, f32[48,1024]{1,0:T(8,128)S(1)}, u32[]{:S(2)}, u32[]{:S(2)}) collective-permute-start(f32[48,1024]{1,0:T(8,128)S(1)} %get-tuple-element.37.refs_5_), channel_id=1, source_target_pairs={{0,8},{8,0},{16,24},{24,16},{1,9},{9,1},{17,25},{25,17},{2,10},{10... | collective-permute-start | bytes 589832 | tf_op jit(solution)/shard_map/ppermute | solution.py:475
  41.9 4.9 %collective-permute-start.14 = (f32[2,8,1024]{2,1,0:T(8,128)S(1)}, f32[2,8,1024]{2,1,0:T(8,128)S(1)}, u32[]{:S(2)}, u32[]{:S(2)}) collective-permute-start(f32[2,8,1024]{2,1,0:T(8,128)S(1)} %pad_maximum_fusion.1), channel_id=1, source_target_pairs={{0,2},{1,5},{2,0},{3,7},{4,6},{5,1},{6,4},{7,3},{8,10},{9,13},{10,... | collective-permute-start | bytes 196616 | tf_op jit(solution)/shard_map/ppermute | solution.py:539
  42.8 5.2 %collective-permute-start.16 = (f32[2,8,1024]{2,1,0:T(8,128)S(1)}, f32[2,8,1024]{2,1,0:T(8,128)S(1)}, u32[]{:S(2)}, u32[]{:S(2)}) collective-permute-start(f32[2,8,1024]{2,1,0:T(8,128)S(1)} %pad_maximum_fusion.1), channel_id=1, source_target_pairs={{0,6},{1,7},{2,4},{3,5},{4,2},{5,3},{6,0},{7,1},{8,14},{9,15},{10,... | collective-permute-start | bytes 196616 | tf_op jit(solution)/shard_map/ppermute | solution.py:540
  46.8 1.3 %collective-permute-start.15 = (f32[2,8,1024]{2,1,0:T(8,128)S(1)}, f32[2,8,1024]{2,1,0:T(8,128)S(1)}, u32[]{:S(2)}, u32[]{:S(2)}) collective-permute-start(f32[2,8,1024]{2,1,0:T(8,128)S(1)} %collective-permute-done.14.refs_2_), channel_id=1, source_target_pairs={{0,1},{1,0},{2,3},{3,2},{4,5},{5,4},{6,7},{7,6},{8,9},{9,8},{10,11... | collective-permute-start | bytes 196616 | tf_op jit(solution)/shard_map/ppermute | solution.py:541
  48.3 6.0 %collective-permute-start.20 = (f32[8,1024]{1,0:T(8,128)S(1)}, f32[8,1024]{1,0:T(8,128)S(1)}, u32[]{:S(2)}, u32[]{:S(2)}) collective-permute-start(f32[8,1024]{1,0:T(8,128)S(1)} %get-tuple-element.42.refs_4_.ef_ref), channel_id=1, source_target_pairs={{0,24},{8,16},{16,8},{24,0},{1,25},{9,17},{17,9},{25,1},{2,26},{10... | collective-permute-start | bytes 98312 | tf_op jit(solution)/shard_map/ppermute | solution.py:474
  50.2 4.2 %collective-permute-start.19 = (f32[8,1024]{1,0:T(8,128)S(1)}, f32[8,1024]{1,0:T(8,128)S(1)}, u32[]{:S(2)}, u32[]{:S(2)}) collective-permute-start(f32[8,1024]{1,0:T(8,128)S(1)} %get-tuple-element.42.refs_4_.ef_ref), channel_id=1, source_target_pairs={{0,8},{8,0},{16,24},{24,16},{1,9},{9,1},{17,25},{25,17},{2,10},{10... | collective-permute-start | bytes 98312 | tf_op jit(solution)/shard_map/ppermute | solution.py:475
  57.9 1.3 %collective-permute-start.21 = (f32[16,1024]{1,0:T(8,128)S(1)}, f32[16,1024]{1,0:T(8,128)S(1)}, u32[]{:S(2)}, u32[]{:S(2)}) collective-permute-start(f32[16,1024]{1,0:T(8,128)S(1)} %get-tuple-element.43.refs_0_), channel_id=1, source_target_pairs={{0,1},{1,0},{2,3},{3,2},{4,5},{5,4},{6,7},{7,6},{8,9},{9,8},{10,11... | collective-permute-start | bytes 196616 | tf_op jit(solution)/shard_map/ppermute | solution.py:535
  59.2 4.7 %collective-permute-start.22 = (f32[2,8,1024]{2,1,0:T(8,128)S(1)}, f32[2,8,1024]{2,1,0:T(8,128)S(1)}, u32[]{:S(2)}, u32[]{:S(2)}) collective-permute-start(f32[2,8,1024]{2,1,0:T(8,128)S(1)} %pad_maximum_fusion.2), channel_id=1, source_target_pairs={{0,2},{1,5},{2,0},{3,7},{4,6},{5,1},{6,4},{7,3},{8,10},{9,13},{10,... | collective-permute-start | bytes 196616 | tf_op jit(solution)/shard_map/ppermute | solution.py:539
  60.2 5.2 %collective-permute-start.24 = (f32[2,8,1024]{2,1,0:T(8,128)S(1)}, f32[2,8,1024]{2,1,0:T(8,128)S(1)}, u32[]{:S(2)}, u32[]{:S(2)}) collective-permute-start(f32[2,8,1024]{2,1,0:T(8,128)S(1)} %pad_maximum_fusion.2), channel_id=1, source_target_pairs={{0,6},{1,7},{2,4},{3,5},{4,2},{5,3},{6,0},{7,1},{8,14},{9,15},{10,... | collective-permute-start | bytes 196616 | tf_op jit(solution)/shard_map/ppermute | solution.py:540
  64.0 1.4 %collective-permute-start.23 = (f32[2,8,1024]{2,1,0:T(8,128)S(1)}, f32[2,8,1024]{2,1,0:T(8,128)S(1)}, u32[]{:S(2)}, u32[]{:S(2)}) collective-permute-start(f32[2,8,1024]{2,1,0:T(8,128)S(1)} %collective-permute-done.22.refs_2_), channel_id=1, source_target_pairs={{0,1},{1,0},{2,3},{3,2},{4,5},{5,4},{6,7},{7,6},{8,9},{9,8},{10,11... | collective-permute-start | bytes 196616 | tf_op jit(solution)/shard_map/ppermute | solution.py:541
  (3 other events, 2.0 us)

commit v6 on v5

--- a/solution.py
+++ b/solution.py
@@ -21,7 +21,7 @@
 DEPTH = 256
 VMEM_LIMIT = 32 * 1024 * 1024
 ENTER, LEAVE, PIVOT, UPWARD, METRIC = range(16, 21)
-ROW, COLUMN, INNER, GROUP, LIVE, EDGE = range(6)
+ROW, COLUMN, INNER, GROUP, LIVE, EDGE, SHARES = range(7)
 
 F32 = jnp.float32
 BF16 = jnp.bfloat16
@@ -123,6 +123,7 @@
     sections, rows = down_ref.shape
     cell = cell_ref[...]
     row, place = cell // cells_z, cell % cells_z
+    slots_ref[...] = jnp.zeros_like(slots_ref)
     slots_ref[ROW : ROW + 1, :] = row.astype(F32)
     slots_ref[COLUMN : COLUMN + 1, :] = place.astype(F32)
     slots_ref[INNER : INNER + 1, :] = (place % DEPTH).astype(F32)
@@ -133,6 +134,10 @@
     at = lambda place: jnp.where(lane == place, 1.0, 0.0)
     matrix_ref[...] = jnp.zeros_like(matrix_ref)
     scal_ref[...] = jnp.zeros_like(scal_ref)
+    order = lax.broadcasted_iota(jnp.int32, (rows, 1), 0)
+    fy = off_ref[1:2, :]
+    weight = jnp.where(order == row, 1.0 - fy, jnp.where(order == row + 1, fy, 0.0))
+    edge = slots_ref[EDGE : EDGE + 1, :]
     for k in range(sections):
         lower = []
         row = at(ENTER)
@@ -152,6 +157,13 @@
                 place = rows * c + i
                 matrix_ref[k, place : place + 1, :] = inner if c == 0 else pltpu.roll(inner, rows * c, 1)
             answer_ref[k, i : i + 1, :] = row + metric_ref[i] * at(METRIC)
+        if k < sections - 1:
+            for i, which, more in ((0, ENTER, 0.0), (1, LEAVE, edge)):
+                share = jnp.sum(
+                    weight * answer_ref[k, :, which : which + 1], axis=0, keepdims=True
+                )
+                place = SHARES + 2 * k + i
+                slots_ref[place : place + 1, :] = share + more
         scal_ref[k, 1:2, :] = (
             row + scale_ref[k, rows - 1] * at(PIVOT) + up_ref[k, rows - 1] * at(UPWARD)
         )
@@ -244,6 +256,25 @@
             out_ref[c : c + 1, here] = jnp.sum(part, axis=0, keepdims=True)
 
 
+def ahead_plane_kernel(near_x_ref, far_x_ref, slots_ref, off_ref, own_ref, out_ref, table_ref):
+    plane, _ = two_sides(near_x_ref, far_x_ref)
+    cells_z = plane.shape[1]
+    rows = plane.shape[0] // COMPS
+    table_ref[...] = split_rows(plane)
+    order = lax.broadcasted_iota(jnp.int32, (rows, TILE), 0).astype(F32)
+    for t in range(slots_ref.shape[1] // TILE):
+        here = slice(t * TILE, (t + 1) * TILE)
+        row, column = (slots_ref[d : d + 1, here] for d in (ROW, COLUMN))
+        fx, fy, fz = (off_ref[d : d + 1, here] for d in range(3))
+        chosen = across(column, cells_z)
+        blended = blend_z(jnp.dot(table_ref[...], chosen, preferred_element_type=F32), fz)
+        weight = jnp.where(order == row, 1.0 - fy, jnp.where(order == row + 1.0, fy, 0.0)) * fx
+        for c in range(COMPS):
+            part = blended[rows * c : rows * (c + 1)] * weight
+            part = jnp.sum(part, axis=0, keepdims=True)
+            out_ref[c : c + 1, here] = own_ref[c : c + 1, here] + part
+
+
 def section_kernel(number, step, last, *refs):
     first = number == 0
     refs = list(refs)
@@ -276,24 +307,42 @@
             joined_plane(plane, ef, answer_ref[number - 1])
             for plane, ef in ((x_plus, ahead), (x_minus, behind))
         )
-    pad = jnp.zeros((2, cells_z), F32)
-    table_ref[...] = split_rows(jnp.concatenate([x_plus, y_plus, corner, pad], axis=0))
-    order = lax.broadcasted_iota(jnp.int32, (rows, TILE), 0).astype(F32)
+    if first:
+        edge_rows = [
+            jnp.concatenate(
+                [jnp.zeros((COMPS, cells_z), F32), row, jnp.zeros((2, cells_z), F32)], axis=0
+            )
+            for row in (y_plus, corner)
+        ]
+    else:
+        edge_rows = [yp_ref[...], ahead]
+    table = split_rows(jnp.concatenate(edge_rows, axis=0))
+    tall = table.shape[0]
+    for k in range(cells_z // DEPTH):
+        table_ref[tall * k : tall * (k + 1), :] = table[:, DEPTH * k : DEPTH * (k + 1)]
+    upper_half = lax.broadcasted_iota(jnp.int32, (8, TILE), 0) >= COMPS
     for t in range(slots_ref.shape[1] // TILE):
         here = slice(t * TILE, (t + 1) * TILE)
-        row, column, inner, group, live, edge = (slots_ref[d : d + 1, here] for d in range(6))
-        fx, fy, fz = (off_ref[d : d + 1, here] for d in range(3))
-        found = jnp.dot(table_ref[...], across(column, cells_z), preferred_element_type=F32)
+        column, inner, group, live, edge = (
+            slots_ref[d : d + 1, here] for d in (COLUMN, INNER, GROUP, LIVE, EDGE)
+        )
+        fx, fz = off_ref[0:1, here], off_ref[2:3, here]
         chosen_ref[here, :] = down(inner)
-        blended = blend_z(found, fz)
-        weight = jnp.where(order == row, 1.0 - fy, jnp.where(order == row + 1.0, fy, 0.0)) * fx
-        parts = [
-            jnp.sum(blended[rows * c : rows * (c + 1)] * weight, axis=0, keepdims=True)
-            for c in range(COMPS)
-        ]
-        side = blended[count : count + COMPS] * (1.0 - fx)
-        side = side + blended[count + COMPS : count + 2 * COMPS] * fx
-        fluid = near_ref[:, here] + jnp.concatenate(parts, axis=0) + side * edge
+        found = jnp.dot(table_ref[...], across(inner, DEPTH), preferred_element_type=F32)
+        picked = found[:tall]
+        for k in range(1, cells_z // DEPTH):
+            picked = jnp.where(column >= float(DEPTH * k), found[tall * k : tall * (k + 1)], picked)
+        blended = blend_z(picked, fz)
+        if first:
+            enters, leaves = 0.0, edge
+        else:
+            enters, leaves = (
+                slots_ref[d : d + 1, here]
+                for d in (SHARES + 2 * (number - 1), SHARES + 2 * (number - 1) + 1)
+            )
+        more = blended[:8] * (1.0 - fx) + blended[8:] * fx
+        more = more * jnp.where(upper_half, leaves, enters)
+        fluid = near_ref[:, here] + more[:COMPS] + more[COMPS : 2 * COMPS]
         v = v_ref[:, here]
         drag = tau_ref[:, here] * (fluid - v)
         v = v + step * drag
@@ -495,22 +544,33 @@
     matrix, answer, scal, places = call(
         functools.partial(tables_kernel, cells_z),
         (like(SECTIONS, 56, 128), like(SECTIONS, cells_y, 128), like(SECTIONS, 2, 128),
-         like(8, slots)),
+         like(16, slots)),
         scalars(5) + whole_in_vmem(2),
         "tables",
     )(forward_rate, backward_rate, pivot_inv, y_metric, outgoing_count, cell, particle_offset)
     v = particle_vel
     rows = COMPS * cells_y
     field_like, slots_like = like(rows, cells_z), like(COMPS, slots)
-    for k in range(SECTIONS):
-        last = k == SECTIONS - 1
-        near = call(
+
+    def own_plane(plane):
+        return call(
             own_plane_kernel,
             slots_like,
             whole_in_vmem(3),
             "own_plane",
             [pltpu.VMEM((4 * rows, cells_z), BF16)],
-        )(u, places, particle_offset)
+        )(plane, places, particle_offset)
+
+    own_near = own_plane(u)
+    for k in range(SECTIONS):
+        last = k == SECTIONS - 1
+        near = call(
+            ahead_plane_kernel,
+            slots_like,
+            whole_in_vmem(5),
+            "ahead_plane",
+            [pltpu.VMEM((4 * rows, cells_z), BF16)],
+        )(*planes, places, particle_offset, own_near)
         sides = (u, ym, *planes, yp, *edges)
         out = call(
             functools.partial(section_kernel, k, TIME_STEP * SECTION_WEIGHTS[k], last),
@@ -518,7 +578,7 @@
             whole_in_vmem(len(sides) + 8),
             "section",
             [
-                pltpu.VMEM((4 * (rows + 8), cells_z), BF16),
+                pltpu.VMEM((4 * 16 * cells_z // DEPTH, DEPTH), BF16),
                 pltpu.VMEM((2 * rows * (cells_z // DEPTH), slots), BF16),
                 pltpu.VMEM((slots, DEPTH), BF16),
             ],
@@ -548,6 +608,7 @@
             more, shapes = (v, from_x), (field_like, slots_like)
         else:
             planes = both_sides(w)
+            own_near = own_plane(w)
             more = (places, particle_offset, tau, v)
             shapes = (field_like, like(8, cells_z), like(COMPS, cells_z))
         if k == 0:

time: 66.5 us -> 64.8 us (0.974)
  waiting for transfers between devices: 15.9 us -> 12.8 us
  Pallas kernels: 18.6 us -> 21 us
  starting transfers between devices: 28.2 us -> 27.2 us
    pallas_call x3 -> x6, Pallas kernels: 5.18 us -> 10 us  [the longest x3 5 us: own_plane(): call(own_plane_kernel, slots_like, whole_in_vmem(3), 'own_plane', [pltpu....]
    ppermute x5, waiting for transfers between devices: 3.06 us -> 0.15 us  [both_sides(): far = lax.ppermute(block, 'gx', next_pair)]
    pallas_call x3, Pallas kernels: 10.3 us -> 7.68 us  [on_device(): call(functools.partial(section_kernel, k, TIME_STEP * SECTION_WEIGHTS[k],...]
    ppermute x5, starting transfers between devices: 2.67 us -> 0.81 us  [both_sides(): return (lax.ppermute(block, 'gx', same_pair), far)]
    ppermute x5, starting transfers between devices: 13.4 us -> 14.9 us  [both_sides(): far = lax.ppermute(block, 'gx', next_pair)]
    ppermute x1, waiting for transfers between devices: 1.23 us -> 0.01 us  [on_device(): corner = lax.ppermute(first, ('gx', 'gy'), diagonal)]
    ppermute x5, waiting for transfers between devices: 0.16 us -> 1.26 us  [both_sides(): return (lax.ppermute(block, 'gx', same_pair), far)]
    ppermute x3, starting transfers between devices: 1.05 us -> 0.21 us  [on_device(): partner = lax.ppermute(pq, 'gy', flip(1))]
  transfers between devices with their start and end apart: 25 -> 25, of which waited for: 12 -> 10; matrix products, arithmetic and copies ran while one was open for 2% -> 2% of each run, Pallas kernels for 11% -> 19%
where the time goes in v6:
time: 64.8 us; the launch traced here: 64.6 us
  starting transfers between devices  27.2 us (42%)
  Pallas kernels  21 us (32%)
  waiting for transfers between devices  12.8 us (20%)
  local copies, waits for them, and re-layouts  2.62 us (4%)
  between operations  1.01 us (2%)
    ppermute x5, starting transfers between devices, both_sides(): far = lax.ppermute(block, 'gx', next_pair)  14.9 us
    pallas_call x3, Pallas kernels, on_device(): call(functools.partial(section_kernel, k, TIME_STEP * SECTION_WEIGHTS[k],...  7.68 us
    ppermute x3, waiting for transfers between devices, on_device(): side = lax.ppermute(pair, 'gy', mixed)  6.38 us
    pallas_call x3, Pallas kernels, own_plane(): call(own_plane_kernel, slots_like, whole_in_vmem(3), 'own_plane', [pltpu....  5 us
    pallas_call x3, Pallas kernels, on_device(): call(ahead_plane_kernel, slots_like, whole_in_vmem(5), 'ahead_plane', [pl...  5 us
    ppermute x3, waiting for transfers between devices, on_device(): far = lax.ppermute(pair, 'gy', flip(6))  4.6 us
    ppermute x3, starting transfers between devices, on_device(): far = lax.ppermute(pair, 'gy', flip(6))  4.51 us
    ppermute x3, starting transfers between devices, on_device(): side = lax.ppermute(pair, 'gy', mixed)  3.63 us
  transfers between devices with their start and end apart: 25, of which 10 were waited for; matrix products, arithmetic and copies ran while one was open for 2% of the time, Pallas kernels for 19%

profile of v6, /device:TPU:0, one launch (start us, length us, event | category | flops | bytes accessed | tf_op | source)
XLA Modules:
  0.0 64.6 jit_solution(1020321547830884261)
XLA Ops:
  0.6 5.1 %collective-permute-start.2 = (f32[48,1024]{1,0:T(8,128)}, f32[48,1024]{1,0:T(8,128)S(1)}, u32[]{:S(2)}, u32[]{:S(2)}) collective-permute-start(f32[48,1024]{1,0:T(8,128)} %bitcast.18), channel_id=1, source_target_pairs={{0,24},{8,16},{16,8},{24,0},{1,25},{9,17},{17,9},{25,1},{2,26},{10... | collective-permute-start | bytes 589832 | tf_op jit(solution)/shard_map/ppermute | solution.py:523
  5.7 1.0 %fusion = (f32[3,1,1,1024]{3,2,1,0:T(1,128)S(1)}, f32[3,1,1,1024]{3,2,1,0:T(1,128)S(1)}) fusion(f32[3,1,16,1024]{3,2,1,0:T(8,128)} %param.10), kind=kLoop, calls=%fused_computation.8 | loop fusion | bytes 49152 | tf_op jit(solution)/shard_map/slice | solution.py:532
  6.9 2.5 %collective-permute-start = (f32[6,1024]{1,0:T(8,128)S(1)}, f32[6,1024]{1,0:T(8,128)S(1)}, u32[]{:S(2)}, u32[]{:S(2)}) collective-permute-start(f32[6,1024]{1,0:T(8,128)S(1)} %pad_maximum_fusion.3), channel_id=1, source_target_pairs={{0,7},{1,2},{2,1},{3,4},{4,3},{5,6},{6,5},{7,0},{8,15},{9,10},{10,... | collective-permute-start | bytes 73736 | tf_op jit(solution)/shard_map/ppermute | solution.py:537
  10.7 1.1 %tables.1 = (f32[3,56,128]{2,1,0:T(8,128)S(1)}, f32[3,16,128]{2,1,0:T(8,128)S(1)}, f32[3,2,128]{2,1,0:T(2,128)S(1)}, f32[16,3584]{1,0:T(8,128)S(1)}) custom-call(f32[3,16]{1,0:T(4,128)S(1)} %copy-done.4, f32[3,16]{1,0:T(4,128)S(1)} %copy-done.5, f32[3,16]{1,0:T(4,128)S(1)} %copy-done.6, f32[16]{0:T(128)S(1)} %copy-done.7, s32[1,1,3]{2,1,0:T(1,128)S(1)} %copy-done.8, ...), custom_call_target="tpu_custom_call" | custom-call | tf_op jit(solution)/shard_map/tables/pallas_call | solution.py:544
  11.8 0.9 %copy-done.1 = f32[3,1,16,1024]{3,2,1,0:T(8,128)S(1)} copy-done((f32[3,1,16,1024]{3,2,1,0:T(8,128)S(1)}, f32[3,1,16,1024]{3,2,1,0:T(8,128)}, u32[]{:S(2)}) %copy-start.1) | copy-done | bytes 196632
  12.7 1.7 %own_plane.3.own_ref = f32[3,3584]{1,0:T(4,128)S(1)} custom-call(f32[48,1024]{1,0:T(8,128)S(1)} %bitcast.20, f32[16,3584]{1,0:T(8,128)S(1)} %get-tuple-element.26.slots_ref.refs_7_.refs_8_, f32[3,3584]{1,0:T(4,128)S(1)} %copy-done), custom_call_target="tpu_custom_call" | custom-call | tf_op jit(solution)/shard_map/own_plane/pallas_call | solution.py:556
  14.4 0.9 %collective-permute-done.1.near_x_ref.refs_2_ = f32[48,1024]{1,0:T(8,128)S(1)} collective-permute-done((f32[48,1024]{1,0:T(8,128)}, f32[48,1024]{1,0:T(8,128)S(1)}, u32[]{:S(2)}, u32[]{:S(2)}) %collective-permute-start.1) | collective-permute-done | bytes 196640 | tf_op jit(solution)/shard_map/ppermute | solution.py:524
  15.3 1.7 %ahead_plane.3.refs_11_ = f32[3,3584]{1,0:T(4,128)S(1)} custom-call(f32[48,1024]{1,0:T(8,128)S(1)} %collective-permute-done.1.near_x_ref.refs_2_, f32[48,1024]{1,0:T(8,128)S(1)} %collective-permute-done.2.far_x_ref.refs_3_, f32[16,3584]{1,0:T(8,128)S(1)} %get-tuple-element.26.slots_ref.refs_7_.refs_8_, f32[3,3584]{1,0:T(4,128)S(1)} %copy-done, ...), custom_call_target="tpu_custom_call" | custom-call | tf_op jit(solution)/shard_map/ahead_plane/pallas_call | solution.py:567
  17.0 2.6 %section.3 = (f32[48,1024]{1,0:T(8,128)S(1)}, f32[8,1024]{1,0:T(8,128)S(1)}, f32[3,3584]{1,0:T(4,128)S(1)}) custom-call(f32[48,1024]{1,0:T(8,128)S(1)} %bitcast.21, f32[6,1024]{1,0:T(8,128)S(1)} %collective-permute-done.refs_1_, f32[48,1024]{1,0:T(8,128)S(1)} %collective-permute-done.1.near_x_ref.refs_2_, ...), custom_call_target="tpu_custom_call" | custom-call | tf_op jit(solution)/shard_map/section/pallas_call | solution.py:575
  19.6 2.8 %collective-permute-start.10 = (f32[48,1024]{1,0:T(8,128)S(1)}, f32[48,1024]{1,0:T(8,128)S(1)}, u32[]{:S(2)}, u32[]{:S(2)}) collective-permute-start(f32[48,1024]{1,0:T(8,128)S(1)} %get-tuple-element.31.refs_5_.u_ref), channel_id=1, source_target_pairs={{0,24},{8,16},{16,8},{24,0},{1,25},{9,17},{17,9},{25,1},{2,26},{10... | collective-permute-start | bytes 589832 | tf_op jit(solution)/shard_map/ppermute | solution.py:523
  22.4 1.5 %collective-permute-start.6 = (f32[2,8,1024]{2,1,0:T(8,128)S(1)}, f32[2,8,1024]{2,1,0:T(8,128)S(1)}, u32[]{:S(2)}, u32[]{:S(2)}) collective-permute-start(f32[2,8,1024]{2,1,0:T(8,128)S(1)} %pad_maximum_fusion), channel_id=1, source_target_pairs={{0,2},{1,5},{2,0},{3,7},{4,6},{5,1},{6,4},{7,3},{8,10},{9,13},{10,... | collective-permute-start | bytes 196616 | tf_op jit(solution)/shard_map/ppermute | solution.py:599
  24.0 1.5 %collective-permute-start.8 = (f32[2,8,1024]{2,1,0:T(8,128)S(1)}, f32[2,8,1024]{2,1,0:T(8,128)S(1)}, u32[]{:S(2)}, u32[]{:S(2)}) collective-permute-start(f32[2,8,1024]{2,1,0:T(8,128)S(1)} %pad_maximum_fusion), channel_id=1, source_target_pairs={{0,6},{1,7},{2,4},{3,5},{4,2},{5,3},{6,0},{7,1},{8,14},{9,15},{10,... | collective-permute-start | bytes 196616 | tf_op jit(solution)/shard_map/ppermute | solution.py:600
  25.5 2.0 %collective-permute-done.6.refs_2_ = f32[2,8,1024]{2,1,0:T(8,128)S(1)} collective-permute-done((f32[2,8,1024]{2,1,0:T(8,128)S(1)}, f32[2,8,1024]{2,1,0:T(8,128)S(1)}, u32[]{:S(2)}, u32[]{:S(2)}) %collective-permute-start.6) | collective-permute-done | bytes 65568 | tf_op jit(solution)/shard_map/ppermute | solution.py:599
  27.5 1.7 %collective-permute-done.8.refs_4_ = f32[2,8,1024]{2,1,0:T(8,128)S(1)} collective-permute-done((f32[2,8,1024]{2,1,0:T(8,128)S(1)}, f32[2,8,1024]{2,1,0:T(8,128)S(1)}, u32[]{:S(2)}, u32[]{:S(2)}) %collective-permute-start.8) | collective-permute-done | bytes 65568 | tf_op jit(solution)/shard_map/ppermute | solution.py:600
  29.4 2.0 %collective-permute-start.12 = (f32[8,1024]{1,0:T(8,128)S(1)}, f32[8,1024]{1,0:T(8,128)S(1)}, u32[]{:S(2)}, u32[]{:S(2)}) collective-permute-start(f32[8,1024]{1,0:T(8,128)S(1)} %get-tuple-element.35.refs_4_), channel_id=1, source_target_pairs={{0,24},{8,16},{16,8},{24,0},{1,25},{9,17},{17,9},{25,1},{2,26},{10... | collective-permute-start | bytes 98312 | tf_op jit(solution)/shard_map/ppermute | solution.py:523
  31.7 1.7 %own_plane.4.own_ref = f32[3,3584]{1,0:T(4,128)S(1)} custom-call(f32[48,1024]{1,0:T(8,128)S(1)} %get-tuple-element.31.refs_5_.u_ref, f32[16,3584]{1,0:T(8,128)S(1)} %get-tuple-element.26.slots_ref.refs_7_.refs_8_, f32[3,3584]{1,0:T(4,128)S(1)} %copy-done), custom_call_target="tpu_custom_call" | custom-call | tf_op jit(solution)/shard_map/own_plane/pallas_call | solution.py:556
  33.4 1.7 %ahead_plane.4.refs_11_ = f32[3,3584]{1,0:T(4,128)S(1)} custom-call(f32[48,1024]{1,0:T(8,128)S(1)} %collective-permute-done.9.near_x_ref.refs_2_, f32[48,1024]{1,0:T(8,128)S(1)} %collective-permute-done.10.far_x_ref.refs_3_, f32[16,3584]{1,0:T(8,128)S(1)} %get-tuple-element.26.slots_ref.refs_7_.refs_8_, f32[3,3584]{1,0:T(4,128)S(1)} %copy-done, ...), custom_call_target="tpu_custom_call" | custom-call | tf_op jit(solution)/shard_map/ahead_plane/pallas_call | solution.py:567
  35.6 2.6 %section.4 = (f32[48,1024]{1,0:T(8,128)S(1)}, f32[8,1024]{1,0:T(8,128)S(1)}, f32[3,3584]{1,0:T(4,128)S(1)}) custom-call(f32[48,1024]{1,0:T(8,128)S(1)} %get-tuple-element.33.refs_0_, f32[3,1024]{1,0:T(4,128)S(1)} %get-tuple-element.34.refs_1_, f32[48,1024]{1,0:T(8,128)S(1)} %collective-permute-done.9.near_x_ref.refs_2_, ...), custom_call_target="tpu_custom_call" | custom-call | tf_op jit(solution)/shard_map/section/pallas_call | solution.py:575
  38.2 2.3 %collective-permute-start.18 = (f32[48,1024]{1,0:T(8,128)S(1)}, f32[48,1024]{1,0:T(8,128)S(1)}, u32[]{:S(2)}, u32[]{:S(2)}) collective-permute-start(f32[48,1024]{1,0:T(8,128)S(1)} %get-tuple-element.37.refs_5_.u_ref), channel_id=1, source_target_pairs={{0,24},{8,16},{16,8},{24,0},{1,25},{9,17},{17,9},{25,1},{2,26},{10... | collective-permute-start | bytes 589832 | tf_op jit(solution)/shard_map/ppermute | solution.py:523
  40.6 1.1 %collective-permute-start.14 = (f32[2,8,1024]{2,1,0:T(8,128)S(1)}, f32[2,8,1024]{2,1,0:T(8,128)S(1)}, u32[]{:S(2)}, u32[]{:S(2)}) collective-permute-start(f32[2,8,1024]{2,1,0:T(8,128)S(1)} %pad_maximum_fusion.1), channel_id=1, source_target_pairs={{0,2},{1,5},{2,0},{3,7},{4,6},{5,1},{6,4},{7,3},{8,10},{9,13},{10,... | collective-permute-start | bytes 196616 | tf_op jit(solution)/shard_map/ppermute | solution.py:599
  41.7 1.5 %collective-permute-start.16 = (f32[2,8,1024]{2,1,0:T(8,128)S(1)}, f32[2,8,1024]{2,1,0:T(8,128)S(1)}, u32[]{:S(2)}, u32[]{:S(2)}) collective-permute-start(f32[2,8,1024]{2,1,0:T(8,128)S(1)} %pad_maximum_fusion.1), channel_id=1, source_target_pairs={{0,6},{1,7},{2,4},{3,5},{4,2},{5,3},{6,0},{7,1},{8,14},{9,15},{10,... | collective-permute-start | bytes 196616 | tf_op jit(solution)/shard_map/ppermute | solution.py:600
  43.2 2.1 %collective-permute-done.14.refs_2_ = f32[2,8,1024]{2,1,0:T(8,128)S(1)} collective-permute-done((f32[2,8,1024]{2,1,0:T(8,128)S(1)}, f32[2,8,1024]{2,1,0:T(8,128)S(1)}, u32[]{:S(2)}, u32[]{:S(2)}) %collective-permute-start.14) | collective-permute-done | bytes 65568 | tf_op jit(solution)/shard_map/ppermute | solution.py:599
  45.3 1.5 %collective-permute-done.16.refs_4_ = f32[2,8,1024]{2,1,0:T(8,128)S(1)} collective-permute-done((f32[2,8,1024]{2,1,0:T(8,128)S(1)}, f32[2,8,1024]{2,1,0:T(8,128)S(1)}, u32[]{:S(2)}, u32[]{:S(2)}) %collective-permute-start.16) | collective-permute-done | bytes 65568 | tf_op jit(solution)/shard_map/ppermute | solution.py:600
  47.1 2.6 %collective-permute-start.20 = (f32[8,1024]{1,0:T(8,128)S(1)}, f32[8,1024]{1,0:T(8,128)S(1)}, u32[]{:S(2)}, u32[]{:S(2)}) collective-permute-start(f32[8,1024]{1,0:T(8,128)S(1)} %get-tuple-element.42.refs_4_.ef_ref), channel_id=1, source_target_pairs={{0,24},{8,16},{16,8},{24,0},{1,25},{9,17},{17,9},{25,1},{2,26},{10... | collective-permute-start | bytes 98312 | tf_op jit(solution)/shard_map/ppermute | solution.py:523
  50.2 1.7 %own_plane.5.own_ref = f32[3,3584]{1,0:T(4,128)S(1)} custom-call(f32[48,1024]{1,0:T(8,128)S(1)} %get-tuple-element.37.refs_5_.u_ref, f32[16,3584]{1,0:T(8,128)S(1)} %get-tuple-element.26.slots_ref.refs_7_.refs_8_, f32[3,3584]{1,0:T(4,128)S(1)} %copy-done), custom_call_target="tpu_custom_call" | custom-call | tf_op jit(solution)/shard_map/own_plane/pallas_call | solution.py:556
  51.9 1.7 %ahead_plane.5.refs_11_ = f32[3,3584]{1,0:T(4,128)S(1)} custom-call(f32[48,1024]{1,0:T(8,128)S(1)} %collective-permute-done.17.near_x_ref.refs_2_, f32[48,1024]{1,0:T(8,128)S(1)} %collective-permute-done.18.far_x_ref.refs_3_, f32[16,3584]{1,0:T(8,128)S(1)} %get-tuple-element.26.slots_ref.refs_7_.refs_8_, f32[3,3584]{1,0:T(4,128)S(1)} %copy-done, ...), custom_call_target="tpu_custom_call" | custom-call | tf_op jit(solution)/shard_map/ahead_plane/pallas_call | solution.py:567
  53.7 2.6 %section.5 = (f32[48,1024]{1,0:T(8,128)S(1)}, f32[16,1024]{1,0:T(8,128)S(1)}, f32[3,3584]{1,0:T(4,128)S(1)}) custom-call(f32[48,1024]{1,0:T(8,128)S(1)} %get-tuple-element.40.refs_0_.u_ref, f32[3,1024]{1,0:T(4,128)S(1)} %get-tuple-element.41.refs_1_, f32[48,1024]{1,0:T(8,128)S(1)} %collective-permute-done.17.near_x_ref.refs_2_, ...), custom_call_target="tpu_custom_call" | custom-call | tf_op jit(solution)/shard_map/section/pallas_call | solution.py:575
  57.6 1.0 %collective-permute-start.22 = (f32[2,8,1024]{2,1,0:T(8,128)S(1)}, f32[2,8,1024]{2,1,0:T(8,128)S(1)}, u32[]{:S(2)}, u32[]{:S(2)}) collective-permute-start(f32[2,8,1024]{2,1,0:T(8,128)S(1)} %pad_maximum_fusion.2), channel_id=1, source_target_pairs={{0,2},{1,5},{2,0},{3,7},{4,6},{5,1},{6,4},{7,3},{8,10},{9,13},{10,... | collective-permute-start | bytes 196616 | tf_op jit(solution)/shard_map/ppermute | solution.py:599
  58.6 1.5 %collective-permute-start.24 = (f32[2,8,1024]{2,1,0:T(8,128)S(1)}, f32[2,8,1024]{2,1,0:T(8,128)S(1)}, u32[]{:S(2)}, u32[]{:S(2)}) collective-permute-start(f32[2,8,1024]{2,1,0:T(8,128)S(1)} %pad_maximum_fusion.2), channel_id=1, source_target_pairs={{0,6},{1,7},{2,4},{3,5},{4,2},{5,3},{6,0},{7,1},{8,14},{9,15},{10,... | collective-permute-start | bytes 196616 | tf_op jit(solution)/shard_map/ppermute | solution.py:600
  60.1 2.2 %collective-permute-done.22.refs_2_ = f32[2,8,1024]{2,1,0:T(8,128)S(1)} collective-permute-done((f32[2,8,1024]{2,1,0:T(8,128)S(1)}, f32[2,8,1024]{2,1,0:T(8,128)S(1)}, u32[]{:S(2)}, u32[]{:S(2)}) %collective-permute-start.22) | collective-permute-done | bytes 65568 | tf_op jit(solution)/shard_map/ppermute | solution.py:599
  62.3 1.4 %collective-permute-done.24.refs_4_ = f32[2,8,1024]{2,1,0:T(8,128)S(1)} collective-permute-done((f32[2,8,1024]{2,1,0:T(8,128)S(1)}, f32[2,8,1024]{2,1,0:T(8,128)S(1)}, u32[]{:S(2)}, u32[]{:S(2)}) %collective-permute-start.24) | collective-permute-done | bytes 65568 | tf_op jit(solution)/shard_map/ppermute | solution.py:600
  63.7 0.9 %join.5 = (f32[48,1024]{1,0:T(8,128)}, f32[3,3584]{1,0:T(4,128)}) custom-call(f32[16,1024]{1,0:T(8,128)S(1)} %get-tuple-element.43.refs_0_, f32[16,1024]{1,0:T(8,128)S(1)} %collective-permute-done.21.refs_1_, f32[2,8,1024]{2,1,0:T(8,128)S(1)} %collective-permute-done.22.refs_2_, f32[2,8,1024]{2,1,0:T(8,128)S(1)} %collective-permute-done.23.refs_3_, ...), custom_call_target="tpu_custom_call" | custom-call | tf_op jit(solution)/shard_map/join/pallas_call | solution.py:618
  (65 shorter events, 4.6 us)
Async XLA Ops:
  0.6 13.8 %collective-permute-start.2 = (f32[48,1024]{1,0:T(8,128)}, f32[48,1024]{1,0:T(8,128)S(1)}, u32[]{:S(2)}, u32[]{:S(2)}) collective-permute-start(f32[48,1024]{1,0:T(8,128)} %bitcast.18), channel_id=1, source_target_pairs={{0,24},{8,16},{16,8},{24,0},{1,25},{9,17},{17,9},{25,1},{2,26},{10... | collective-permute-start | bytes 589832 | tf_op jit(solution)/shard_map/ppermute | solution.py:523
  5.7 9.5 %collective-permute-start.1 = (f32[48,1024]{1,0:T(8,128)}, f32[48,1024]{1,0:T(8,128)S(1)}, u32[]{:S(2)}, u32[]{:S(2)}) collective-permute-start(f32[48,1024]{1,0:T(8,128)} %bitcast.19), channel_id=1, source_target_pairs={{0,8},{8,0},{16,24},{24,16},{1,9},{9,1},{17,25},{25,17},{2,10},{10... | collective-permute-start | bytes 589832 | tf_op jit(solution)/shard_map/ppermute | solution.py:524
  6.8 3.2 %copy-start.9 = (f32[3584]{0:T(1024)S(1)}, f32[3584]{0:T(1024)}, u32[]{:S(2)}) copy-start(f32[3584]{0:T(1024)} %param.18) | copy-start | bytes 43012
  6.8 3.3 %copy-start = (f32[3,3584]{1,0:T(4,128)S(1)}, f32[3,3584]{1,0:T(4,128)}, u32[]{:S(2)}) copy-start(f32[3,3584]{1,0:T(4,128)} %refs_8_.7) | copy-start | bytes 129028
  6.8 3.2 %copy-start.10 = (s32[3584]{0:T(1024)S(1)}, s32[3584]{0:T(1024)}, u32[]{:S(2)}) copy-start(s32[3584]{0:T(1024)} %param.16) | copy-start | bytes 43012
  6.8 10.1 %collective-permute-start.3 = (f32[6,1024]{1,0:T(8,128)S(1)}, f32[6,1024]{1,0:T(8,128)S(1)}, u32[]{:S(2)}, u32[]{:S(2)}) collective-permute-start(f32[6,1024]{1,0:T(8,128)S(1)} %pad_maximum_fusion.3), channel_id=1, source_target_pairs={{0,1},{1,0},{2,3},{3,2},{4,5},{5,4},{6,7},{7,6},{8,9},{9,8},{10,11... | collective-permute-start | bytes 73736 | tf_op jit(solution)/shard_map/ppermute | solution.py:538
  6.9 10.1 %collective-permute-start = (f32[6,1024]{1,0:T(8,128)S(1)}, f32[6,1024]{1,0:T(8,128)S(1)}, u32[]{:S(2)}, u32[]{:S(2)}) collective-permute-start(f32[6,1024]{1,0:T(8,128)S(1)} %pad_maximum_fusion.3), channel_id=1, source_target_pairs={{0,7},{1,2},{2,1},{3,4},{4,3},{5,6},{6,5},{7,0},{8,15},{9,10},{10,... | collective-permute-start | bytes 73736 | tf_op jit(solution)/shard_map/ppermute | solution.py:537
  9.4 7.5 %collective-permute-start.4 = (f32[3,1024]{1,0:T(4,128)S(1)}, f32[3,1024]{1,0:T(4,128)S(1)}, u32[]{:S(2)}, u32[]{:S(2)}) collective-permute-start(f32[3,1024]{1,0:T(4,128)S(1)} %bitcast.27), channel_id=1, source_target_pairs={{9,0},{10,1},{11,2},{12,3},{13,4},{14,5},{15,6},{8,7},{17,8},{18,9... | collective-permute-start | bytes 36872 | tf_op jit(solution)/shard_map/ppermute | solution.py:535
  10.0 0.7 %copy-start.6 = (f32[3,16]{1,0:T(4,128)S(1)}, f32[3,16]{1,0:T(4,128)}, u32[]{:S(2)}) copy-start(f32[3,16]{1,0:T(4,128)} %scale_ref.1) | copy-start | bytes 580
  11.8 0.9 %copy-start.1 = (f32[3,1,16,1024]{3,2,1,0:T(8,128)S(1)}, f32[3,1,16,1024]{3,2,1,0:T(8,128)}, u32[]{:S(2)}) copy-start(f32[3,1,16,1024]{3,2,1,0:T(8,128)} %param.10) | copy-start | bytes 589828
  14.4 2.6 %copy-start.2 = (f32[3,1,16,1024]{3,2,1,0:T(8,128)S(1)}, f32[3,1,16,1024]{3,2,1,0:T(8,128)}, u32[]{:S(2)}) copy-start(f32[3,1,16,1024]{3,2,1,0:T(8,128)} %param.10) | copy-start | bytes 589828
  14.4 2.6 %copy-start.3 = (f32[3,3584]{1,0:T(4,128)S(1)}, f32[3,3584]{1,0:T(4,128)}, u32[]{:S(2)}) copy-start(f32[3,3584]{1,0:T(4,128)} %refs_10_.1) | copy-start | bytes 129028
  19.6 2.9 %collective-permute-start.5 = (f32[8,1024]{1,0:T(8,128)S(1)}, f32[8,1024]{1,0:T(8,128)S(1)}, u32[]{:S(2)}, u32[]{:S(2)}) collective-permute-start(f32[8,1024]{1,0:T(8,128)S(1)} %get-tuple-element.30.refs_0_), channel_id=1, source_target_pairs={{0,1},{1,0},{2,3},{3,2},{4,5},{5,4},{6,7},{7,6},{8,9},{9,8},{10,11... | collective-permute-start | bytes 98312 | tf_op jit(solution)/shard_map/ppermute | solution.py:595
  19.6 13.8 %collective-permute-start.10 = (f32[48,1024]{1,0:T(8,128)S(1)}, f32[48,1024]{1,0:T(8,128)S(1)}, u32[]{:S(2)}, u32[]{:S(2)}) collective-permute-start(f32[48,1024]{1,0:T(8,128)S(1)} %get-tuple-element.31.refs_5_.u_ref), channel_id=1, source_target_pairs={{0,24},{8,16},{16,8},{24,0},{1,25},{9,17},{17,9},{25,1},{2,26},{10... | collective-permute-start | bytes 589832 | tf_op jit(solution)/shard_map/ppermute | solution.py:523
  22.4 11.0 %collective-permute-start.9 = (f32[48,1024]{1,0:T(8,128)S(1)}, f32[48,1024]{1,0:T(8,128)S(1)}, u32[]{:S(2)}, u32[]{:S(2)}) collective-permute-start(f32[48,1024]{1,0:T(8,128)S(1)} %get-tuple-element.31.refs_5_.u_ref), channel_id=1, source_target_pairs={{0,8},{8,0},{16,24},{24,16},{1,9},{9,1},{17,25},{25,17},{2,10},{10... | collective-permute-start | bytes 589832 | tf_op jit(solution)/shard_map/ppermute | solution.py:524
  22.4 5.0 %collective-permute-start.6 = (f32[2,8,1024]{2,1,0:T(8,128)S(1)}, f32[2,8,1024]{2,1,0:T(8,128)S(1)}, u32[]{:S(2)}, u32[]{:S(2)}) collective-permute-start(f32[2,8,1024]{2,1,0:T(8,128)S(1)} %pad_maximum_fusion), channel_id=1, source_target_pairs={{0,2},{1,5},{2,0},{3,7},{4,6},{5,1},{6,4},{7,3},{8,10},{9,13},{10,... | collective-permute-start | bytes 196616 | tf_op jit(solution)/shard_map/ppermute | solution.py:599
  24.0 5.2 %collective-permute-start.8 = (f32[2,8,1024]{2,1,0:T(8,128)S(1)}, f32[2,8,1024]{2,1,0:T(8,128)S(1)}, u32[]{:S(2)}, u32[]{:S(2)}) collective-permute-start(f32[2,8,1024]{2,1,0:T(8,128)S(1)} %pad_maximum_fusion), channel_id=1, source_target_pairs={{0,6},{1,7},{2,4},{3,5},{4,2},{5,3},{6,0},{7,1},{8,14},{9,15},{10,... | collective-permute-start | bytes 196616 | tf_op jit(solution)/shard_map/ppermute | solution.py:600
  27.5 1.7 %collective-permute-start.7 = (f32[2,8,1024]{2,1,0:T(8,128)S(1)}, f32[2,8,1024]{2,1,0:T(8,128)S(1)}, u32[]{:S(2)}, u32[]{:S(2)}) collective-permute-start(f32[2,8,1024]{2,1,0:T(8,128)S(1)} %collective-permute-done.6.refs_2_), channel_id=1, source_target_pairs={{0,1},{1,0},{2,3},{3,2},{4,5},{5,4},{6,7},{7,6},{8,9},{9,8},{10,11... | collective-permute-start | bytes 196616 | tf_op jit(solution)/shard_map/ppermute | solution.py:601
  29.4 5.8 %collective-permute-start.12 = (f32[8,1024]{1,0:T(8,128)S(1)}, f32[8,1024]{1,0:T(8,128)S(1)}, u32[]{:S(2)}, u32[]{:S(2)}) collective-permute-start(f32[8,1024]{1,0:T(8,128)S(1)} %get-tuple-element.35.refs_4_), channel_id=1, source_target_pairs={{0,24},{8,16},{16,8},{24,0},{1,25},{9,17},{17,9},{25,1},{2,26},{10... | collective-permute-start | bytes 98312 | tf_op jit(solution)/shard_map/ppermute | solution.py:523
  31.5 4.1 %collective-permute-start.11 = (f32[8,1024]{1,0:T(8,128)S(1)}, f32[8,1024]{1,0:T(8,128)S(1)}, u32[]{:S(2)}, u32[]{:S(2)}) collective-permute-start(f32[8,1024]{1,0:T(8,128)S(1)} %get-tuple-element.35.refs_4_), channel_id=1, source_target_pairs={{0,8},{8,0},{16,24},{24,16},{1,9},{9,1},{17,25},{25,17},{2,10},{10... | collective-permute-start | bytes 98312 | tf_op jit(solution)/shard_map/ppermute | solution.py:524
  38.1 2.4 %collective-permute-start.13 = (f32[8,1024]{1,0:T(8,128)S(1)}, f32[8,1024]{1,0:T(8,128)S(1)}, u32[]{:S(2)}, u32[]{:S(2)}) collective-permute-start(f32[8,1024]{1,0:T(8,128)S(1)} %get-tuple-element.36.refs_0_), channel_id=1, source_target_pairs={{0,1},{1,0},{2,3},{3,2},{4,5},{5,4},{6,7},{7,6},{8,9},{9,8},{10,11... | collective-permute-start | bytes 98312 | tf_op jit(solution)/shard_map/ppermute | solution.py:595
  38.2 13.7 %collective-permute-start.18 = (f32[48,1024]{1,0:T(8,128)S(1)}, f32[48,1024]{1,0:T(8,128)S(1)}, u32[]{:S(2)}, u32[]{:S(2)}) collective-permute-start(f32[48,1024]{1,0:T(8,128)S(1)} %get-tuple-element.37.refs_5_.u_ref), channel_id=1, source_target_pairs={{0,24},{8,16},{16,8},{24,0},{1,25},{9,17},{17,9},{25,1},{2,26},{10... | collective-permute-start | bytes 589832 | tf_op jit(solution)/shard_map/ppermute | solution.py:523
  40.5 11.4 %collective-permute-start.17 = (f32[48,1024]{1,0:T(8,128)S(1)}, f32[48,1024]{1,0:T(8,128)S(1)}, u32[]{:S(2)}, u32[]{:S(2)}) collective-permute-start(f32[48,1024]{1,0:T(8,128)S(1)} %get-tuple-element.37.refs_5_.u_ref), channel_id=1, source_target_pairs={{0,8},{8,0},{16,24},{24,16},{1,9},{9,1},{17,25},{25,17},{2,10},{10... | collective-permute-start | bytes 589832 | tf_op jit(solution)/shard_map/ppermute | solution.py:524
  40.6 4.7 %collective-permute-start.14 = (f32[2,8,1024]{2,1,0:T(8,128)S(1)}, f32[2,8,1024]{2,1,0:T(8,128)S(1)}, u32[]{:S(2)}, u32[]{:S(2)}) collective-permute-start(f32[2,8,1024]{2,1,0:T(8,128)S(1)} %pad_maximum_fusion.1), channel_id=1, source_target_pairs={{0,2},{1,5},{2,0},{3,7},{4,6},{5,1},{6,4},{7,3},{8,10},{9,13},{10,... | collective-permute-start | bytes 196616 | tf_op jit(solution)/shard_map/ppermute | solution.py:599
  41.7 5.2 %collective-permute-start.16 = (f32[2,8,1024]{2,1,0:T(8,128)S(1)}, f32[2,8,1024]{2,1,0:T(8,128)S(1)}, u32[]{:S(2)}, u32[]{:S(2)}) collective-permute-start(f32[2,8,1024]{2,1,0:T(8,128)S(1)} %pad_maximum_fusion.1), channel_id=1, source_target_pairs={{0,6},{1,7},{2,4},{3,5},{4,2},{5,3},{6,0},{7,1},{8,14},{9,15},{10,... | collective-permute-start | bytes 196616 | tf_op jit(solution)/shard_map/ppermute | solution.py:600
  45.3 1.5 %collective-permute-start.15 = (f32[2,8,1024]{2,1,0:T(8,128)S(1)}, f32[2,8,1024]{2,1,0:T(8,128)S(1)}, u32[]{:S(2)}, u32[]{:S(2)}) collective-permute-start(f32[2,8,1024]{2,1,0:T(8,128)S(1)} %collective-permute-done.14.refs_2_), channel_id=1, source_target_pairs={{0,1},{1,0},{2,3},{3,2},{4,5},{5,4},{6,7},{7,6},{8,9},{9,8},{10,11... | collective-permute-start | bytes 196616 | tf_op jit(solution)/shard_map/ppermute | solution.py:601
  47.1 6.5 %collective-permute-start.20 = (f32[8,1024]{1,0:T(8,128)S(1)}, f32[8,1024]{1,0:T(8,128)S(1)}, u32[]{:S(2)}, u32[]{:S(2)}) collective-permute-start(f32[8,1024]{1,0:T(8,128)S(1)} %get-tuple-element.42.refs_4_.ef_ref), channel_id=1, source_target_pairs={{0,24},{8,16},{16,8},{24,0},{1,25},{9,17},{17,9},{25,1},{2,26},{10... | collective-permute-start | bytes 98312 | tf_op jit(solution)/shard_map/ppermute | solution.py:523
  49.7 4.0 %collective-permute-start.19 = (f32[8,1024]{1,0:T(8,128)S(1)}, f32[8,1024]{1,0:T(8,128)S(1)}, u32[]{:S(2)}, u32[]{:S(2)}) collective-permute-start(f32[8,1024]{1,0:T(8,128)S(1)} %get-tuple-element.42.refs_4_.ef_ref), channel_id=1, source_target_pairs={{0,8},{8,0},{16,24},{24,16},{1,9},{9,1},{17,25},{25,17},{2,10},{10... | collective-permute-start | bytes 98312 | tf_op jit(solution)/shard_map/ppermute | solution.py:524
  56.2 1.3 %collective-permute-start.21 = (f32[16,1024]{1,0:T(8,128)S(1)}, f32[16,1024]{1,0:T(8,128)S(1)}, u32[]{:S(2)}, u32[]{:S(2)}) collective-permute-start(f32[16,1024]{1,0:T(8,128)S(1)} %get-tuple-element.43.refs_0_), channel_id=1, source_target_pairs={{0,1},{1,0},{2,3},{3,2},{4,5},{5,4},{6,7},{7,6},{8,9},{9,8},{10,11... | collective-permute-start | bytes 196616 | tf_op jit(solution)/shard_map/ppermute | solution.py:595
  57.6 4.7 %collective-permute-start.22 = (f32[2,8,1024]{2,1,0:T(8,128)S(1)}, f32[2,8,1024]{2,1,0:T(8,128)S(1)}, u32[]{:S(2)}, u32[]{:S(2)}) collective-permute-start(f32[2,8,1024]{2,1,0:T(8,128)S(1)} %pad_maximum_fusion.2), channel_id=1, source_target_pairs={{0,2},{1,5},{2,0},{3,7},{4,6},{5,1},{6,4},{7,3},{8,10},{9,13},{10,... | collective-permute-start | bytes 196616 | tf_op jit(solution)/shard_map/ppermute | solution.py:599
  58.6 5.2 %collective-permute-start.24 = (f32[2,8,1024]{2,1,0:T(8,128)S(1)}, f32[2,8,1024]{2,1,0:T(8,128)S(1)}, u32[]{:S(2)}, u32[]{:S(2)}) collective-permute-start(f32[2,8,1024]{2,1,0:T(8,128)S(1)} %pad_maximum_fusion.2), channel_id=1, source_target_pairs={{0,6},{1,7},{2,4},{3,5},{4,2},{5,3},{6,0},{7,1},{8,14},{9,15},{10,... | collective-permute-start | bytes 196616 | tf_op jit(solution)/shard_map/ppermute | solution.py:600
  62.3 1.4 %collective-permute-start.23 = (f32[2,8,1024]{2,1,0:T(8,128)S(1)}, f32[2,8,1024]{2,1,0:T(8,128)S(1)}, u32[]{:S(2)}, u32[]{:S(2)}) collective-permute-start(f32[2,8,1024]{2,1,0:T(8,128)S(1)} %collective-permute-done.22.refs_2_), channel_id=1, source_target_pairs={{0,1},{1,0},{2,3},{3,2},{4,5},{5,4},{6,7},{7,6},{8,9},{9,8},{10,11... | collective-permute-start | bytes 196616 | tf_op jit(solution)/shard_map/ppermute | solution.py:601
  (4 other events, 2.7 us)

commit v7 on v6

--- a/solution.py
+++ b/solution.py
@@ -96,6 +96,30 @@
     near = values[:rows] + values[rows : 2 * rows]
     far = values[2 * rows : 3 * rows] + values[3 * rows :]
     return near * (1.0 - fz) + far * fz
+
+
+def three_parts(values):
+    high = values.astype(BF16).astype(F32)
+    middle = (values - high).astype(BF16).astype(F32)
+    return high, middle, values - high - middle
+
+
+def three_part_dot(matrix, values):
+    high, middle, low = three_parts(matrix)
+    second = lambda part: pltpu.roll(part, 64, 1)
+    left = jnp.concatenate(
+        [high + second(high), middle + second(high), middle + second(low)], axis=1
+    )
+    a, b, c = three_parts(values)
+    blank = jnp.zeros((64 - values.shape[0], values.shape[1]), F32)
+    right = []
+    for part in (a, b, a, c, b, a):
+        right += [part, blank]
+    return jnp.dot(
+        left.astype(BF16),
+        jnp.concatenate(right, axis=0).astype(BF16),
+        preferred_element_type=F32,
+    )
 
 
 def tables_kernel(
@@ -256,7 +280,8 @@
             out_ref[c : c + 1, here] = jnp.sum(part, axis=0, keepdims=True)
 
 
-def ahead_plane_kernel(near_x_ref, far_x_ref, slots_ref, off_ref, own_ref, out_ref, table_ref):
+def ahead_plane_kernel(first, one_ref, other_ref, slots_ref, off_ref, own_ref, out_ref, table_ref):
+    near_x_ref, far_x_ref = (other_ref, one_ref) if first else (one_ref, other_ref)
     plane, _ = two_sides(near_x_ref, far_x_ref)
     cells_z = plane.shape[1]
     rows = plane.shape[0] // COMPS
@@ -280,6 +305,8 @@
     refs = list(refs)
     take = lambda count: [refs.pop(0) for _ in range(count)]
     u_ref, ym_ref, near_x_ref, far_x_ref, yp_ref, near_ef_ref, far_ef_ref = take(7)
+    if first:
+        near_x_ref, far_x_ref = far_x_ref, near_x_ref
     slots_ref, off_ref, tau_ref, v_ref, near_ref, matrix_ref, answer_ref, scal_ref = take(8)
     w_ref, pq_ref, v_out_ref = take(3)
     table_ref, spread_ref, chosen_ref = refs
@@ -374,12 +401,7 @@
             pieces.append(pushed[high : high + rows] + pushed[low : low + rows])
         force = jnp.concatenate(pieces, axis=1)
         rhs.append(field + step * (convection + force))
-    solved = jnp.dot(
-        matrix_ref[number, :, 0:count],
-        jnp.concatenate(rhs, axis=0),
-        precision=lax.Precision.HIGHEST,
-        preferred_element_type=F32,
-    )
+    solved = three_part_dot(matrix_ref[number], jnp.concatenate(rhs, axis=0))
     w_ref[...] = solved[:count]
     pq_ref[0:COMPS, :] = solved[count : count + COMPS]
     for c in range(COMPS):
@@ -564,14 +586,15 @@
     own_near = own_plane(u)
     for k in range(SECTIONS):
         last = k == SECTIONS - 1
+        given = planes[::-1] if k == 0 else planes
         near = call(
-            ahead_plane_kernel,
+            functools.partial(ahead_plane_kernel, k == 0),
             slots_like,
             whole_in_vmem(5),
             "ahead_plane",
             [pltpu.VMEM((4 * rows, cells_z), BF16)],
-        )(*planes, places, particle_offset, own_near)
-        sides = (u, ym, *planes, yp, *edges)
+        )(*given, places, particle_offset, own_near)
+        sides = (u, ym, *given, yp, *edges)
         out = call(
             functools.partial(section_kernel, k, TIME_STEP * SECTION_WEIGHTS[k], last),
             (field_like, like(16 if last else 8, cells_z), slots_like),

time: 64.8 us -> 63.6 us (0.981)
  waiting for transfers between devices: 12.8 us -> 11.5 us
  Pallas kernels: 21 us -> 20 us
  starting transfers between devices: 27.2 us -> 28.2 us
    ppermute x5, starting transfers between devices: 14.9 us -> 8.64 us  [both_sides(): far = lax.ppermute(block, 'gx', next_pair)]
    ppermute x5, starting transfers between devices: 0.81 us -> 6.78 us  [both_sides(): return (lax.ppermute(block, 'gx', same_pair), far)]
    ppermute x5, waiting for transfers between devices: 1.26 us -> 0.01 us  [both_sides(): return (lax.ppermute(block, 'gx', same_pair), far)]
    pallas_call x3, Pallas kernels: 7.68 us -> 6.44 us  [on_device(): call(functools.partial(section_kernel, k, TIME_STEP * SECTION_WEIGHTS[k],...]
  transfers between devices with their start and end apart: 25 -> 25, of which waited for: 10 -> 8; matrix products, arithmetic and copies ran while one was open for 2% -> 2% of each run, Pallas kernels for 19% -> 20%
where the time goes in v7:
time: 63.6 us; the launch traced here: 63.4 us
  starting transfers between devices  28.2 us (44%)
  Pallas kernels  20 us (31%)
  waiting for transfers between devices  11.5 us (18%)
  local copies, waits for them, and re-layouts  2.63 us (4%)
  between operations  1.02 us (2%)
    ppermute x5, starting transfers between devices, both_sides(): far = lax.ppermute(block, 'gx', next_pair)  8.64 us
    ppermute x5, starting transfers between devices, both_sides(): return (lax.ppermute(block, 'gx', same_pair), far)  6.78 us
    pallas_call x3, Pallas kernels, on_device(): call(functools.partial(section_kernel, k, TIME_STEP * SECTION_WEIGHTS[k],...  6.44 us
    ppermute x3, waiting for transfers between devices, on_device(): side = lax.ppermute(pair, 'gy', mixed)  5.93 us
    pallas_call x3, Pallas kernels, own_plane(): call(own_plane_kernel, slots_like, whole_in_vmem(3), 'own_plane', [pltpu....  5.2 us
    ppermute x3, waiting for transfers between devices, on_device(): far = lax.ppermute(pair, 'gy', flip(6))  5.04 us
    pallas_call x3, Pallas kernels, on_device(): call(functools.partial(ahead_plane_kernel, k == 0), slots_like, whole_in_...  4.99 us
    ppermute x3, starting transfers between devices, on_device(): far = lax.ppermute(pair, 'gy', flip(6))  4.51 us
  transfers between devices with their start and end apart: 25, of which 8 were waited for; matrix products, arithmetic and copies ran while one was open for 2% of the time, Pallas kernels for 20%

profile of v7, /device:TPU:0, one launch (start us, length us, event | category | flops | bytes accessed | tf_op | source)
XLA Modules:
  0.0 63.4 jit_solution(8461945844301582312)
XLA Ops:
  0.6 3.1 %collective-permute-start.2 = (f32[48,1024]{1,0:T(8,128)}, f32[48,1024]{1,0:T(8,128)S(1)}, u32[]{:S(2)}, u32[]{:S(2)}) collective-permute-start(f32[48,1024]{1,0:T(8,128)} %bitcast.18), channel_id=1, source_target_pairs={{0,8},{8,0},{16,24},{24,16},{1,9},{9,1},{17,25},{25,17},{2,10},{10... | collective-permute-start | bytes 589832 | tf_op jit(solution)/shard_map/ppermute | solution.py:546
  3.7 2.5 %collective-permute-start.1 = (f32[48,1024]{1,0:T(8,128)}, f32[48,1024]{1,0:T(8,128)S(1)}, u32[]{:S(2)}, u32[]{:S(2)}) collective-permute-start(f32[48,1024]{1,0:T(8,128)} %bitcast.19), channel_id=1, source_target_pairs={{0,24},{8,16},{16,8},{24,0},{1,25},{9,17},{17,9},{25,1},{2,26},{10... | collective-permute-start | bytes 589832 | tf_op jit(solution)/shard_map/ppermute | solution.py:545
  6.2 1.0 %fusion = (f32[3,1,1,1024]{3,2,1,0:T(1,128)S(1)}, f32[3,1,1,1024]{3,2,1,0:T(1,128)S(1)}) fusion(f32[3,1,16,1024]{3,2,1,0:T(8,128)} %param.10), kind=kLoop, calls=%fused_computation.8 | loop fusion | bytes 49152 | tf_op jit(solution)/shard_map/slice | solution.py:554
  7.3 2.5 %collective-permute-start = (f32[6,1024]{1,0:T(8,128)S(1)}, f32[6,1024]{1,0:T(8,128)S(1)}, u32[]{:S(2)}, u32[]{:S(2)}) collective-permute-start(f32[6,1024]{1,0:T(8,128)S(1)} %pad_maximum_fusion.3), channel_id=1, source_target_pairs={{0,7},{1,2},{2,1},{3,4},{4,3},{5,6},{6,5},{7,0},{8,15},{9,10},{10,... | collective-permute-start | bytes 73736 | tf_op jit(solution)/shard_map/ppermute | solution.py:559
  11.6 1.1 %tables.1 = (f32[3,56,128]{2,1,0:T(8,128)S(1)}, f32[3,16,128]{2,1,0:T(8,128)S(1)}, f32[3,2,128]{2,1,0:T(2,128)S(1)}, f32[16,3584]{1,0:T(8,128)S(1)}) custom-call(f32[3,16]{1,0:T(4,128)S(1)} %copy-done.4, f32[3,16]{1,0:T(4,128)S(1)} %copy-done.5, f32[3,16]{1,0:T(4,128)S(1)} %copy-done.6, f32[16]{0:T(128)S(1)} %copy-done.7, s32[1,1,3]{2,1,0:T(1,128)S(1)} %copy-done.8, ...), custom_call_target="tpu_custom_call" | custom-call | tf_op jit(solution)/shard_map/tables/pallas_call | solution.py:566
  13.6 1.7 %own_plane.3.own_ref = f32[3,3584]{1,0:T(4,128)S(1)} custom-call(f32[48,1024]{1,0:T(8,128)S(1)} %bitcast.20, f32[16,3584]{1,0:T(8,128)S(1)} %get-tuple-element.26.slots_ref.refs_7_.refs_8_, f32[3,3584]{1,0:T(4,128)S(1)} %copy-done), custom_call_target="tpu_custom_call" | custom-call | tf_op jit(solution)/shard_map/own_plane/pallas_call | solution.py:578
  15.5 1.7 %ahead_plane.3.refs_11_ = f32[3,3584]{1,0:T(4,128)S(1)} custom-call(f32[48,1024]{1,0:T(8,128)S(1)} %collective-permute-done.1.one_ref.refs_2_, f32[48,1024]{1,0:T(8,128)S(1)} %collective-permute-done.2.other_ref.refs_3_, f32[16,3584]{1,0:T(8,128)S(1)} %get-tuple-element.26.slots_ref.refs_7_.refs_8_, f32[3,3584]{1,0:T(4,128)S(1)} %copy-done, ...), custom_call_target="tpu_custom_call" | custom-call | tf_op jit(solution)/shard_map/ahead_plane/pallas_call | solution.py:590
  17.2 2.2 %section.3 = (f32[48,1024]{1,0:T(8,128)S(1)}, f32[8,1024]{1,0:T(8,128)S(1)}, f32[3,3584]{1,0:T(4,128)S(1)}) custom-call(f32[48,1024]{1,0:T(8,128)S(1)} %bitcast.21, f32[6,1024]{1,0:T(8,128)S(1)} %collective-permute-done.refs_1_, f32[48,1024]{1,0:T(8,128)S(1)} %collective-permute-done.1.one_ref.refs_2_, ...), custom_call_target="tpu_custom_call" | custom-call | tf_op jit(solution)/shard_map/section/pallas_call | solution.py:598
  19.8 1.4 %collective-permute-start.10 = (f32[48,1024]{1,0:T(8,128)S(1)}, f32[48,1024]{1,0:T(8,128)S(1)}, u32[]{:S(2)}, u32[]{:S(2)}) collective-permute-start(f32[48,1024]{1,0:T(8,128)S(1)} %get-tuple-element.31.refs_5_.u_ref), channel_id=1, source_target_pairs={{0,24},{8,16},{16,8},{24,0},{1,25},{9,17},{17,9},{25,1},{2,26},{10... | collective-permute-start | bytes 589832 | tf_op jit(solution)/shard_map/ppermute | solution.py:545
  22.1 1.6 %collective-permute-start.6 = (f32[2,8,1024]{2,1,0:T(8,128)S(1)}, f32[2,8,1024]{2,1,0:T(8,128)S(1)}, u32[]{:S(2)}, u32[]{:S(2)}) collective-permute-start(f32[2,8,1024]{2,1,0:T(8,128)S(1)} %pad_maximum_fusion), channel_id=1, source_target_pairs={{0,2},{1,5},{2,0},{3,7},{4,6},{5,1},{6,4},{7,3},{8,10},{9,13},{10,... | collective-permute-start | bytes 196616 | tf_op jit(solution)/shard_map/ppermute | solution.py:622
  23.6 1.5 %collective-permute-start.8 = (f32[2,8,1024]{2,1,0:T(8,128)S(1)}, f32[2,8,1024]{2,1,0:T(8,128)S(1)}, u32[]{:S(2)}, u32[]{:S(2)}) collective-permute-start(f32[2,8,1024]{2,1,0:T(8,128)S(1)} %pad_maximum_fusion), channel_id=1, source_target_pairs={{0,6},{1,7},{2,4},{3,5},{4,2},{5,3},{6,0},{7,1},{8,14},{9,15},{10,... | collective-permute-start | bytes 196616 | tf_op jit(solution)/shard_map/ppermute | solution.py:623
  25.1 1.9 %collective-permute-done.6.refs_2_ = f32[2,8,1024]{2,1,0:T(8,128)S(1)} collective-permute-done((f32[2,8,1024]{2,1,0:T(8,128)S(1)}, f32[2,8,1024]{2,1,0:T(8,128)S(1)}, u32[]{:S(2)}, u32[]{:S(2)}) %collective-permute-start.6) | collective-permute-done | bytes 65568 | tf_op jit(solution)/shard_map/ppermute | solution.py:622
  27.0 1.8 %collective-permute-done.8.refs_4_ = f32[2,8,1024]{2,1,0:T(8,128)S(1)} collective-permute-done((f32[2,8,1024]{2,1,0:T(8,128)S(1)}, f32[2,8,1024]{2,1,0:T(8,128)S(1)}, u32[]{:S(2)}, u32[]{:S(2)}) %collective-permute-start.8) | collective-permute-done | bytes 65568 | tf_op jit(solution)/shard_map/ppermute | solution.py:623
  29.1 1.4 %collective-permute-start.12 = (f32[8,1024]{1,0:T(8,128)S(1)}, f32[8,1024]{1,0:T(8,128)S(1)}, u32[]{:S(2)}, u32[]{:S(2)}) collective-permute-start(f32[8,1024]{1,0:T(8,128)S(1)} %get-tuple-element.35.refs_4_), channel_id=1, source_target_pairs={{0,24},{8,16},{16,8},{24,0},{1,25},{9,17},{17,9},{25,1},{2,26},{10... | collective-permute-start | bytes 98312 | tf_op jit(solution)/shard_map/ppermute | solution.py:545
  30.5 1.1 %collective-permute-start.11 = (f32[8,1024]{1,0:T(8,128)S(1)}, f32[8,1024]{1,0:T(8,128)S(1)}, u32[]{:S(2)}, u32[]{:S(2)}) collective-permute-start(f32[8,1024]{1,0:T(8,128)S(1)} %get-tuple-element.35.refs_4_), channel_id=1, source_target_pairs={{0,8},{8,0},{16,24},{24,16},{1,9},{9,1},{17,25},{25,17},{2,10},{10... | collective-permute-start | bytes 98312 | tf_op jit(solution)/shard_map/ppermute | solution.py:546
  31.6 1.7 %own_plane.4.own_ref = f32[3,3584]{1,0:T(4,128)S(1)} custom-call(f32[48,1024]{1,0:T(8,128)S(1)} %get-tuple-element.31.refs_5_.u_ref, f32[16,3584]{1,0:T(8,128)S(1)} %get-tuple-element.26.slots_ref.refs_7_.refs_8_, f32[3,3584]{1,0:T(4,128)S(1)} %copy-done), custom_call_target="tpu_custom_call" | custom-call | tf_op jit(solution)/shard_map/own_plane/pallas_call | solution.py:578
  33.3 1.7 %ahead_plane.4.refs_11_ = f32[3,3584]{1,0:T(4,128)S(1)} custom-call(f32[48,1024]{1,0:T(8,128)S(1)} %collective-permute-done.9.one_ref.refs_2_, f32[48,1024]{1,0:T(8,128)S(1)} %collective-permute-done.10.other_ref.refs_3_, f32[16,3584]{1,0:T(8,128)S(1)} %get-tuple-element.26.slots_ref.refs_7_.refs_8_, f32[3,3584]{1,0:T(4,128)S(1)} %copy-done, ...), custom_call_target="tpu_custom_call" | custom-call | tf_op jit(solution)/shard_map/ahead_plane/pallas_call | solution.py:590
  35.0 2.1 %section.4 = (f32[48,1024]{1,0:T(8,128)S(1)}, f32[8,1024]{1,0:T(8,128)S(1)}, f32[3,3584]{1,0:T(4,128)S(1)}) custom-call(f32[48,1024]{1,0:T(8,128)S(1)} %get-tuple-element.33.refs_0_, f32[3,1024]{1,0:T(4,128)S(1)} %get-tuple-element.34.refs_1_, f32[48,1024]{1,0:T(8,128)S(1)} %collective-permute-done.9.one_ref.refs_2_, ...), custom_call_target="tpu_custom_call" | custom-call | tf_op jit(solution)/shard_map/section/pallas_call | solution.py:598
  37.2 2.0 %collective-permute-start.18 = (f32[48,1024]{1,0:T(8,128)S(1)}, f32[48,1024]{1,0:T(8,128)S(1)}, u32[]{:S(2)}, u32[]{:S(2)}) collective-permute-start(f32[48,1024]{1,0:T(8,128)S(1)} %get-tuple-element.37.refs_5_.u_ref), channel_id=1, source_target_pairs={{0,24},{8,16},{16,8},{24,0},{1,25},{9,17},{17,9},{25,1},{2,26},{10... | collective-permute-start | bytes 589832 | tf_op jit(solution)/shard_map/ppermute | solution.py:545
  39.8 1.5 %collective-permute-start.14 = (f32[2,8,1024]{2,1,0:T(8,128)S(1)}, f32[2,8,1024]{2,1,0:T(8,128)S(1)}, u32[]{:S(2)}, u32[]{:S(2)}) collective-permute-start(f32[2,8,1024]{2,1,0:T(8,128)S(1)} %pad_maximum_fusion.1), channel_id=1, source_target_pairs={{0,2},{1,5},{2,0},{3,7},{4,6},{5,1},{6,4},{7,3},{8,10},{9,13},{10,... | collective-permute-start | bytes 196616 | tf_op jit(solution)/shard_map/ppermute | solution.py:622
  41.3 1.5 %collective-permute-start.16 = (f32[2,8,1024]{2,1,0:T(8,128)S(1)}, f32[2,8,1024]{2,1,0:T(8,128)S(1)}, u32[]{:S(2)}, u32[]{:S(2)}) collective-permute-start(f32[2,8,1024]{2,1,0:T(8,128)S(1)} %pad_maximum_fusion.1), channel_id=1, source_target_pairs={{0,6},{1,7},{2,4},{3,5},{4,2},{5,3},{6,0},{7,1},{8,14},{9,15},{10,... | collective-permute-start | bytes 196616 | tf_op jit(solution)/shard_map/ppermute | solution.py:623
  42.8 1.9 %collective-permute-done.14.refs_2_ = f32[2,8,1024]{2,1,0:T(8,128)S(1)} collective-permute-done((f32[2,8,1024]{2,1,0:T(8,128)S(1)}, f32[2,8,1024]{2,1,0:T(8,128)S(1)}, u32[]{:S(2)}, u32[]{:S(2)}) %collective-permute-start.14) | collective-permute-done | bytes 65568 | tf_op jit(solution)/shard_map/ppermute | solution.py:622
  44.7 1.8 %collective-permute-done.16.refs_4_ = f32[2,8,1024]{2,1,0:T(8,128)S(1)} collective-permute-done((f32[2,8,1024]{2,1,0:T(8,128)S(1)}, f32[2,8,1024]{2,1,0:T(8,128)S(1)}, u32[]{:S(2)}, u32[]{:S(2)}) %collective-permute-start.16) | collective-permute-done | bytes 65568 | tf_op jit(solution)/shard_map/ppermute | solution.py:623
  46.7 1.4 %collective-permute-start.20 = (f32[8,1024]{1,0:T(8,128)S(1)}, f32[8,1024]{1,0:T(8,128)S(1)}, u32[]{:S(2)}, u32[]{:S(2)}) collective-permute-start(f32[8,1024]{1,0:T(8,128)S(1)} %get-tuple-element.42.refs_4_.ef_ref), channel_id=1, source_target_pairs={{0,24},{8,16},{16,8},{24,0},{1,25},{9,17},{17,9},{25,1},{2,26},{10... | collective-permute-start | bytes 98312 | tf_op jit(solution)/shard_map/ppermute | solution.py:545
  48.1 1.1 %collective-permute-start.19 = (f32[8,1024]{1,0:T(8,128)S(1)}, f32[8,1024]{1,0:T(8,128)S(1)}, u32[]{:S(2)}, u32[]{:S(2)}) collective-permute-start(f32[8,1024]{1,0:T(8,128)S(1)} %get-tuple-element.42.refs_4_.ef_ref), channel_id=1, source_target_pairs={{0,8},{8,0},{16,24},{24,16},{1,9},{9,1},{17,25},{25,17},{2,10},{10... | collective-permute-start | bytes 98312 | tf_op jit(solution)/shard_map/ppermute | solution.py:546
  49.2 1.9 %own_plane.5.own_ref = f32[3,3584]{1,0:T(4,128)S(1)} custom-call(f32[48,1024]{1,0:T(8,128)S(1)} %get-tuple-element.37.refs_5_.u_ref, f32[16,3584]{1,0:T(8,128)S(1)} %get-tuple-element.26.slots_ref.refs_7_.refs_8_, f32[3,3584]{1,0:T(4,128)S(1)} %copy-done), custom_call_target="tpu_custom_call" | custom-call | tf_op jit(solution)/shard_map/own_plane/pallas_call | solution.py:578
  51.1 1.7 %ahead_plane.5.refs_11_ = f32[3,3584]{1,0:T(4,128)S(1)} custom-call(f32[48,1024]{1,0:T(8,128)S(1)} %collective-permute-done.17.one_ref.refs_2_.near_x_ref, f32[48,1024]{1,0:T(8,128)S(1)} %collective-permute-done.18.other_ref.refs_3_.far_x_ref, f32[16,3584]{1,0:T(8,128)S(1)} %get-tuple-element.26.slots_ref.refs_7_.refs_8_, f32[3,3584]{1,0:T(4,128)S(1)} %copy-done, ...), custom_call_target="tpu_custom_call" | custom-call | tf_op jit(solution)/shard_map/ahead_plane/pallas_call | solution.py:590
  52.8 2.1 %section.5 = (f32[48,1024]{1,0:T(8,128)S(1)}, f32[16,1024]{1,0:T(8,128)S(1)}, f32[3,3584]{1,0:T(4,128)S(1)}) custom-call(f32[48,1024]{1,0:T(8,128)S(1)} %get-tuple-element.40.refs_0_.u_ref, f32[3,1024]{1,0:T(4,128)S(1)} %get-tuple-element.41.refs_1_, f32[48,1024]{1,0:T(8,128)S(1)} %collective-permute-done.17.one_ref.refs_2_.near_x_ref, ...), custom_call_target="tpu_custom_call" | custom-call | tf_op jit(solution)/shard_map/section/pallas_call | solution.py:598
  56.3 1.1 %collective-permute-start.22 = (f32[2,8,1024]{2,1,0:T(8,128)S(1)}, f32[2,8,1024]{2,1,0:T(8,128)S(1)}, u32[]{:S(2)}, u32[]{:S(2)}) collective-permute-start(f32[2,8,1024]{2,1,0:T(8,128)S(1)} %pad_maximum_fusion.2), channel_id=1, source_target_pairs={{0,2},{1,5},{2,0},{3,7},{4,6},{5,1},{6,4},{7,3},{8,10},{9,13},{10,... | collective-permute-start | bytes 196616 | tf_op jit(solution)/shard_map/ppermute | solution.py:622
  57.4 1.5 %collective-permute-start.24 = (f32[2,8,1024]{2,1,0:T(8,128)S(1)}, f32[2,8,1024]{2,1,0:T(8,128)S(1)}, u32[]{:S(2)}, u32[]{:S(2)}) collective-permute-start(f32[2,8,1024]{2,1,0:T(8,128)S(1)} %pad_maximum_fusion.2), channel_id=1, source_target_pairs={{0,6},{1,7},{2,4},{3,5},{4,2},{5,3},{6,0},{7,1},{8,14},{9,15},{10,... | collective-permute-start | bytes 196616 | tf_op jit(solution)/shard_map/ppermute | solution.py:623
  58.9 2.2 %collective-permute-done.22.refs_2_ = f32[2,8,1024]{2,1,0:T(8,128)S(1)} collective-permute-done((f32[2,8,1024]{2,1,0:T(8,128)S(1)}, f32[2,8,1024]{2,1,0:T(8,128)S(1)}, u32[]{:S(2)}, u32[]{:S(2)}) %collective-permute-start.22) | collective-permute-done | bytes 65568 | tf_op jit(solution)/shard_map/ppermute | solution.py:622
  61.0 1.5 %collective-permute-done.24.refs_4_ = f32[2,8,1024]{2,1,0:T(8,128)S(1)} collective-permute-done((f32[2,8,1024]{2,1,0:T(8,128)S(1)}, f32[2,8,1024]{2,1,0:T(8,128)S(1)}, u32[]{:S(2)}, u32[]{:S(2)}) %collective-permute-start.24) | collective-permute-done | bytes 65568 | tf_op jit(solution)/shard_map/ppermute | solution.py:623
  (65 shorter events, 7.6 us)
Async XLA Ops:
  0.6 14.7 %collective-permute-start.2 = (f32[48,1024]{1,0:T(8,128)}, f32[48,1024]{1,0:T(8,128)S(1)}, u32[]{:S(2)}, u32[]{:S(2)}) collective-permute-start(f32[48,1024]{1,0:T(8,128)} %bitcast.18), channel_id=1, source_target_pairs={{0,8},{8,0},{16,24},{24,16},{1,9},{9,1},{17,25},{25,17},{2,10},{10... | collective-permute-start | bytes 589832 | tf_op jit(solution)/shard_map/ppermute | solution.py:546
  3.7 11.7 %collective-permute-start.1 = (f32[48,1024]{1,0:T(8,128)}, f32[48,1024]{1,0:T(8,128)S(1)}, u32[]{:S(2)}, u32[]{:S(2)}) collective-permute-start(f32[48,1024]{1,0:T(8,128)} %bitcast.19), channel_id=1, source_target_pairs={{0,24},{8,16},{16,8},{24,0},{1,25},{9,17},{17,9},{25,1},{2,26},{10... | collective-permute-start | bytes 589832 | tf_op jit(solution)/shard_map/ppermute | solution.py:545
  7.2 3.6 %copy-start.9 = (f32[3584]{0:T(1024)S(1)}, f32[3584]{0:T(1024)}, u32[]{:S(2)}) copy-start(f32[3584]{0:T(1024)} %param.18) | copy-start | bytes 43012
  7.2 3.7 %copy-start = (f32[3,3584]{1,0:T(4,128)S(1)}, f32[3,3584]{1,0:T(4,128)}, u32[]{:S(2)}) copy-start(f32[3,3584]{1,0:T(4,128)} %refs_8_.7) | copy-start | bytes 129028
  7.3 3.6 %copy-start.10 = (s32[3584]{0:T(1024)S(1)}, s32[3584]{0:T(1024)}, u32[]{:S(2)}) copy-start(s32[3584]{0:T(1024)} %param.16) | copy-start | bytes 43012
  7.3 9.9 %collective-permute-start.3 = (f32[6,1024]{1,0:T(8,128)S(1)}, f32[6,1024]{1,0:T(8,128)S(1)}, u32[]{:S(2)}, u32[]{:S(2)}) collective-permute-start(f32[6,1024]{1,0:T(8,128)S(1)} %pad_maximum_fusion.3), channel_id=1, source_target_pairs={{0,1},{1,0},{2,3},{3,2},{4,5},{5,4},{6,7},{7,6},{8,9},{9,8},{10,11... | collective-permute-start | bytes 73736 | tf_op jit(solution)/shard_map/ppermute | solution.py:560
  7.3 9.8 %collective-permute-start = (f32[6,1024]{1,0:T(8,128)S(1)}, f32[6,1024]{1,0:T(8,128)S(1)}, u32[]{:S(2)}, u32[]{:S(2)}) collective-permute-start(f32[6,1024]{1,0:T(8,128)S(1)} %pad_maximum_fusion.3), channel_id=1, source_target_pairs={{0,7},{1,2},{2,1},{3,4},{4,3},{5,6},{6,5},{7,0},{8,15},{9,10},{10,... | collective-permute-start | bytes 73736 | tf_op jit(solution)/shard_map/ppermute | solution.py:559
  9.9 7.2 %collective-permute-start.4 = (f32[3,1024]{1,0:T(4,128)S(1)}, f32[3,1024]{1,0:T(4,128)S(1)}, u32[]{:S(2)}, u32[]{:S(2)}) collective-permute-start(f32[3,1024]{1,0:T(4,128)S(1)} %bitcast.27), channel_id=1, source_target_pairs={{9,0},{10,1},{11,2},{12,3},{13,4},{14,5},{15,6},{8,7},{17,8},{18,9... | collective-permute-start | bytes 36872 | tf_op jit(solution)/shard_map/ppermute | solution.py:557
  10.9 0.7 %copy-start.6 = (f32[3,16]{1,0:T(4,128)S(1)}, f32[3,16]{1,0:T(4,128)}, u32[]{:S(2)}) copy-start(f32[3,16]{1,0:T(4,128)} %scale_ref.1) | copy-start | bytes 580
  12.7 0.9 %copy-start.1 = (f32[3,1,16,1024]{3,2,1,0:T(8,128)S(1)}, f32[3,1,16,1024]{3,2,1,0:T(8,128)}, u32[]{:S(2)}) copy-start(f32[3,1,16,1024]{3,2,1,0:T(8,128)} %param.10) | copy-start | bytes 589828
  15.3 1.9 %copy-start.2 = (f32[3,1,16,1024]{3,2,1,0:T(8,128)S(1)}, f32[3,1,16,1024]{3,2,1,0:T(8,128)}, u32[]{:S(2)}) copy-start(f32[3,1,16,1024]{3,2,1,0:T(8,128)} %param.10) | copy-start | bytes 589828
  15.3 1.9 %copy-start.3 = (f32[3,3584]{1,0:T(4,128)S(1)}, f32[3,3584]{1,0:T(4,128)}, u32[]{:S(2)}) copy-start(f32[3,3584]{1,0:T(4,128)} %refs_10_.1) | copy-start | bytes 129028
  19.3 2.7 %collective-permute-start.5 = (f32[8,1024]{1,0:T(8,128)S(1)}, f32[8,1024]{1,0:T(8,128)S(1)}, u32[]{:S(2)}, u32[]{:S(2)}) collective-permute-start(f32[8,1024]{1,0:T(8,128)S(1)} %get-tuple-element.30.refs_0_), channel_id=1, source_target_pairs={{0,1},{1,0},{2,3},{3,2},{4,5},{5,4},{6,7},{7,6},{8,9},{9,8},{10,11... | collective-permute-start | bytes 98312 | tf_op jit(solution)/shard_map/ppermute | solution.py:618
  19.8 13.5 %collective-permute-start.10 = (f32[48,1024]{1,0:T(8,128)S(1)}, f32[48,1024]{1,0:T(8,128)S(1)}, u32[]{:S(2)}, u32[]{:S(2)}) collective-permute-start(f32[48,1024]{1,0:T(8,128)S(1)} %get-tuple-element.31.refs_5_.u_ref), channel_id=1, source_target_pairs={{0,24},{8,16},{16,8},{24,0},{1,25},{9,17},{17,9},{25,1},{2,26},{10... | collective-permute-start | bytes 589832 | tf_op jit(solution)/shard_map/ppermute | solution.py:545
  21.2 12.1 %collective-permute-start.9 = (f32[48,1024]{1,0:T(8,128)S(1)}, f32[48,1024]{1,0:T(8,128)S(1)}, u32[]{:S(2)}, u32[]{:S(2)}) collective-permute-start(f32[48,1024]{1,0:T(8,128)S(1)} %get-tuple-element.31.refs_5_.u_ref), channel_id=1, source_target_pairs={{0,8},{8,0},{16,24},{24,16},{1,9},{9,1},{17,25},{25,17},{2,10},{10... | collective-permute-start | bytes 589832 | tf_op jit(solution)/shard_map/ppermute | solution.py:546
  22.1 4.9 %collective-permute-start.6 = (f32[2,8,1024]{2,1,0:T(8,128)S(1)}, f32[2,8,1024]{2,1,0:T(8,128)S(1)}, u32[]{:S(2)}, u32[]{:S(2)}) collective-permute-start(f32[2,8,1024]{2,1,0:T(8,128)S(1)} %pad_maximum_fusion), channel_id=1, source_target_pairs={{0,2},{1,5},{2,0},{3,7},{4,6},{5,1},{6,4},{7,3},{8,10},{9,13},{10,... | collective-permute-start | bytes 196616 | tf_op jit(solution)/shard_map/ppermute | solution.py:622
  23.6 5.2 %collective-permute-start.8 = (f32[2,8,1024]{2,1,0:T(8,128)S(1)}, f32[2,8,1024]{2,1,0:T(8,128)S(1)}, u32[]{:S(2)}, u32[]{:S(2)}) collective-permute-start(f32[2,8,1024]{2,1,0:T(8,128)S(1)} %pad_maximum_fusion), channel_id=1, source_target_pairs={{0,6},{1,7},{2,4},{3,5},{4,2},{5,3},{6,0},{7,1},{8,14},{9,15},{10,... | collective-permute-start | bytes 196616 | tf_op jit(solution)/shard_map/ppermute | solution.py:623
  27.0 1.8 %collective-permute-start.7 = (f32[2,8,1024]{2,1,0:T(8,128)S(1)}, f32[2,8,1024]{2,1,0:T(8,128)S(1)}, u32[]{:S(2)}, u32[]{:S(2)}) collective-permute-start(f32[2,8,1024]{2,1,0:T(8,128)S(1)} %collective-permute-done.6.refs_2_), channel_id=1, source_target_pairs={{0,1},{1,0},{2,3},{3,2},{4,5},{5,4},{6,7},{7,6},{8,9},{9,8},{10,11... | collective-permute-start | bytes 196616 | tf_op jit(solution)/shard_map/ppermute | solution.py:624
  29.1 5.9 %collective-permute-start.12 = (f32[8,1024]{1,0:T(8,128)S(1)}, f32[8,1024]{1,0:T(8,128)S(1)}, u32[]{:S(2)}, u32[]{:S(2)}) collective-permute-start(f32[8,1024]{1,0:T(8,128)S(1)} %get-tuple-element.35.refs_4_), channel_id=1, source_target_pairs={{0,24},{8,16},{16,8},{24,0},{1,25},{9,17},{17,9},{25,1},{2,26},{10... | collective-permute-start | bytes 98312 | tf_op jit(solution)/shard_map/ppermute | solution.py:545
  30.5 4.5 %collective-permute-start.11 = (f32[8,1024]{1,0:T(8,128)S(1)}, f32[8,1024]{1,0:T(8,128)S(1)}, u32[]{:S(2)}, u32[]{:S(2)}) collective-permute-start(f32[8,1024]{1,0:T(8,128)S(1)} %get-tuple-element.35.refs_4_), channel_id=1, source_target_pairs={{0,8},{8,0},{16,24},{24,16},{1,9},{9,1},{17,25},{25,17},{2,10},{10... | collective-permute-start | bytes 98312 | tf_op jit(solution)/shard_map/ppermute | solution.py:546
  37.1 2.6 %collective-permute-start.13 = (f32[8,1024]{1,0:T(8,128)S(1)}, f32[8,1024]{1,0:T(8,128)S(1)}, u32[]{:S(2)}, u32[]{:S(2)}) collective-permute-start(f32[8,1024]{1,0:T(8,128)S(1)} %get-tuple-element.36.refs_0_), channel_id=1, source_target_pairs={{0,1},{1,0},{2,3},{3,2},{4,5},{5,4},{6,7},{7,6},{8,9},{9,8},{10,11... | collective-permute-start | bytes 98312 | tf_op jit(solution)/shard_map/ppermute | solution.py:618
  37.2 13.9 %collective-permute-start.18 = (f32[48,1024]{1,0:T(8,128)S(1)}, f32[48,1024]{1,0:T(8,128)S(1)}, u32[]{:S(2)}, u32[]{:S(2)}) collective-permute-start(f32[48,1024]{1,0:T(8,128)S(1)} %get-tuple-element.37.refs_5_.u_ref), channel_id=1, source_target_pairs={{0,24},{8,16},{16,8},{24,0},{1,25},{9,17},{17,9},{25,1},{2,26},{10... | collective-permute-start | bytes 589832 | tf_op jit(solution)/shard_map/ppermute | solution.py:545
  39.1 12.0 %collective-permute-start.17 = (f32[48,1024]{1,0:T(8,128)S(1)}, f32[48,1024]{1,0:T(8,128)S(1)}, u32[]{:S(2)}, u32[]{:S(2)}) collective-permute-start(f32[48,1024]{1,0:T(8,128)S(1)} %get-tuple-element.37.refs_5_.u_ref), channel_id=1, source_target_pairs={{0,8},{8,0},{16,24},{24,16},{1,9},{9,1},{17,25},{25,17},{2,10},{10... | collective-permute-start | bytes 589832 | tf_op jit(solution)/shard_map/ppermute | solution.py:546
  39.8 4.9 %collective-permute-start.14 = (f32[2,8,1024]{2,1,0:T(8,128)S(1)}, f32[2,8,1024]{2,1,0:T(8,128)S(1)}, u32[]{:S(2)}, u32[]{:S(2)}) collective-permute-start(f32[2,8,1024]{2,1,0:T(8,128)S(1)} %pad_maximum_fusion.1), channel_id=1, source_target_pairs={{0,2},{1,5},{2,0},{3,7},{4,6},{5,1},{6,4},{7,3},{8,10},{9,13},{10,... | collective-permute-start | bytes 196616 | tf_op jit(solution)/shard_map/ppermute | solution.py:622
  41.3 5.2 %collective-permute-start.16 = (f32[2,8,1024]{2,1,0:T(8,128)S(1)}, f32[2,8,1024]{2,1,0:T(8,128)S(1)}, u32[]{:S(2)}, u32[]{:S(2)}) collective-permute-start(f32[2,8,1024]{2,1,0:T(8,128)S(1)} %pad_maximum_fusion.1), channel_id=1, source_target_pairs={{0,6},{1,7},{2,4},{3,5},{4,2},{5,3},{6,0},{7,1},{8,14},{9,15},{10,... | collective-permute-start | bytes 196616 | tf_op jit(solution)/shard_map/ppermute | solution.py:623
  44.7 1.8 %collective-permute-start.15 = (f32[2,8,1024]{2,1,0:T(8,128)S(1)}, f32[2,8,1024]{2,1,0:T(8,128)S(1)}, u32[]{:S(2)}, u32[]{:S(2)}) collective-permute-start(f32[2,8,1024]{2,1,0:T(8,128)S(1)} %collective-permute-done.14.refs_2_), channel_id=1, source_target_pairs={{0,1},{1,0},{2,3},{3,2},{4,5},{5,4},{6,7},{7,6},{8,9},{9,8},{10,11... | collective-permute-start | bytes 196616 | tf_op jit(solution)/shard_map/ppermute | solution.py:624
  46.7 6.1 %collective-permute-start.20 = (f32[8,1024]{1,0:T(8,128)S(1)}, f32[8,1024]{1,0:T(8,128)S(1)}, u32[]{:S(2)}, u32[]{:S(2)}) collective-permute-start(f32[8,1024]{1,0:T(8,128)S(1)} %get-tuple-element.42.refs_4_.ef_ref), channel_id=1, source_target_pairs={{0,24},{8,16},{16,8},{24,0},{1,25},{9,17},{17,9},{25,1},{2,26},{10... | collective-permute-start | bytes 98312 | tf_op jit(solution)/shard_map/ppermute | solution.py:545
  48.1 4.7 %collective-permute-start.19 = (f32[8,1024]{1,0:T(8,128)S(1)}, f32[8,1024]{1,0:T(8,128)S(1)}, u32[]{:S(2)}, u32[]{:S(2)}) collective-permute-start(f32[8,1024]{1,0:T(8,128)S(1)} %get-tuple-element.42.refs_4_.ef_ref), channel_id=1, source_target_pairs={{0,8},{8,0},{16,24},{24,16},{1,9},{9,1},{17,25},{25,17},{2,10},{10... | collective-permute-start | bytes 98312 | tf_op jit(solution)/shard_map/ppermute | solution.py:546
  55.0 1.3 %collective-permute-start.21 = (f32[16,1024]{1,0:T(8,128)S(1)}, f32[16,1024]{1,0:T(8,128)S(1)}, u32[]{:S(2)}, u32[]{:S(2)}) collective-permute-start(f32[16,1024]{1,0:T(8,128)S(1)} %get-tuple-element.43.refs_0_), channel_id=1, source_target_pairs={{0,1},{1,0},{2,3},{3,2},{4,5},{5,4},{6,7},{7,6},{8,9},{9,8},{10,11... | collective-permute-start | bytes 196616 | tf_op jit(solution)/shard_map/ppermute | solution.py:618
  56.3 4.7 %collective-permute-start.22 = (f32[2,8,1024]{2,1,0:T(8,128)S(1)}, f32[2,8,1024]{2,1,0:T(8,128)S(1)}, u32[]{:S(2)}, u32[]{:S(2)}) collective-permute-start(f32[2,8,1024]{2,1,0:T(8,128)S(1)} %pad_maximum_fusion.2), channel_id=1, source_target_pairs={{0,2},{1,5},{2,0},{3,7},{4,6},{5,1},{6,4},{7,3},{8,10},{9,13},{10,... | collective-permute-start | bytes 196616 | tf_op jit(solution)/shard_map/ppermute | solution.py:622
  57.4 5.2 %collective-permute-start.24 = (f32[2,8,1024]{2,1,0:T(8,128)S(1)}, f32[2,8,1024]{2,1,0:T(8,128)S(1)}, u32[]{:S(2)}, u32[]{:S(2)}) collective-permute-start(f32[2,8,1024]{2,1,0:T(8,128)S(1)} %pad_maximum_fusion.2), channel_id=1, source_target_pairs={{0,6},{1,7},{2,4},{3,5},{4,2},{5,3},{6,0},{7,1},{8,14},{9,15},{10,... | collective-permute-start | bytes 196616 | tf_op jit(solution)/shard_map/ppermute | solution.py:623
  61.0 1.5 %collective-permute-start.23 = (f32[2,8,1024]{2,1,0:T(8,128)S(1)}, f32[2,8,1024]{2,1,0:T(8,128)S(1)}, u32[]{:S(2)}, u32[]{:S(2)}) collective-permute-start(f32[2,8,1024]{2,1,0:T(8,128)S(1)} %collective-permute-done.22.refs_2_), channel_id=1, source_target_pairs={{0,1},{1,0},{2,3},{3,2},{4,5},{5,4},{6,7},{7,6},{8,9},{9,8},{10,11... | collective-permute-start | bytes 196616 | tf_op jit(solution)/shard_map/ppermute | solution.py:624
  (4 other events, 2.7 us)
